TPU v7x, 128 devices: a whole 4x4x4 slice. The times are simulated.
128 devices in a mesh: lon: 32 (over x, y, core), lat: 4 (over z).
Axes of the slice: x: 4, y: 4, z: 4, core: 2. Of those that a mesh axis runs over, the one named last changes fastest.
Arguments:
- departures: bfloat16 [524288, 128], P(('lon', 'lat')), may hold values from -8 to 8
- obs_owner: int32 [524288, 1], P(('lon', 'lat')), may hold values from 0 to 127; in each aligned block of 4096 rows (0 to 4095, 4096 to 8191, ...) at most 64 rows name the same one
- obs_cells: int32 [524288, 4], P(('lon', 'lat')), may hold values from 0 to 4095, as said below
- interp_weights: float32 [524288, 4], P(('lon', 'lat')), may hold values from 0 to 1
- inv_var: float32 [128], replicated, may hold values from 0.25 to 4
- jacobian: bfloat16 [128, 160], replicated, may hold values from -0.5 to 0.5
- face_rates: float32 [2, 128, 4096], P(None, 'lat', 'lon'), may hold values from 0.08 to 0.245
Outputs:
- gradient: float32 [160, 128, 4096], P(None, 'lat', 'lon')
Inputs may be any that keep to these rules, and one draw needn't show every extreme that they name: `obs_owner`: owners are numbered lon index times the number of lat devices plus lat index. In each aligned block of 4096 rows (the rows of one device) no owner is named by more than 64 rows, a bound that some block reaches. `obs_cells`: A cell c of a tile is latitude row c // 128 and longitude column c % 128 of the owner's block.
All inputs are finite; a program needn't handle non-finite values.
Results may differ from a plain program's by a relative error of at most 0.003.
Values may be sent and summed in bfloat16 or wider, within the bound.
No kernel may reach another device: no remote copies, remote signals or barrier semaphores. Data moves between devices by JAX's collectives and lax.ppermute only.
A program may use at most 64 MiB of HBM per device.

v0:
```python
import math

import jax
import jax.numpy as jnp
from jax import lax
from jax.sharding import PartitionSpec as P

STEPS = 4


def extended_2(shard, sides, width, wrap):
    for axis, dim in sides:
        devices, length = (lax.axis_size(axis), shard.shape[dim])
        up = [(i, (i + 1) % devices) for i in range(devices if wrap else devices - 1)]
        down = [(j, i) for i, j in up]
        last = lax.slice_in_dim(shard, length - width, length, axis=dim)
        leading = lax.slice_in_dim(shard, 0, width, axis=dim)
        before = lax.ppermute(last, axis, up)
        after = lax.ppermute(leading, axis, down)
        shard = jnp.concatenate([before, shard, after], axis=dim)
    return shard


def shrink(field, face_x, face_y):
    flux_x = face_x[1:-1, :] * (field[:, 1:-1, 1:] - field[:, 1:-1, :-1])
    flux_y = face_y[:, 1:-1] * (field[:, 1:, 1:-1] - field[:, :-1, 1:-1])
    inner = field[:, 1:-1, 1:-1]
    return inner + flux_x[:, :, 1:] - flux_x[:, :, :-1] + flux_y[:, 1:, :] - flux_y[:, :-1, :]


def local(departures, obs_owner, obs_cells, interp_weights, inv_var, jacobian, face_rates):
    devices = lax.axis_size(("lon", "lat"))
    ingest_rows = departures.shape[0]
    capacity = 2 * ingest_rows // devices
    owner = obs_owner[:, 0]
    owner_hits = (owner[:, None] == jnp.arange(devices, dtype=jnp.int32)[None, :]).astype(jnp.int32)
    slot_rank = jnp.sum((jnp.cumsum(owner_hits, axis=0) - 1) * owner_hits, axis=1)
    target_slot = owner * capacity + slot_rank
    slot_match = target_slot[None, :] == jnp.arange(devices * capacity, dtype=jnp.int32)[:, None]
    slot_filled = jnp.any(slot_match, axis=1)
    slot_source = jnp.sum(
        jnp.where(slot_match, jnp.arange(ingest_rows, dtype=jnp.int32)[None, :], 0), axis=1
    )

    def pack_rows(row_data):
        picked = jnp.take(row_data, slot_source, axis=0)
        mask_shape = (devices * capacity,) + (1,) * (row_data.ndim - 1)
        picked = jnp.where(slot_filled.reshape(mask_shape), picked, jnp.zeros_like(picked))
        return picked.reshape((devices, capacity) + row_data.shape[1:])

    scaled = (departures.astype(jnp.float32) * inv_var[None, :]).astype(jnp.bfloat16)
    cells_buffer = pack_rows(obs_cells)
    weight_buffer = pack_rows(interp_weights)
    radiance = lax.all_to_all(
        pack_rows(scaled), ("lon", "lat"), split_axis=0, concat_axis=0, tiled=True
    )
    cells = lax.all_to_all(cells_buffer, ("lon", "lat"), split_axis=0, concat_axis=0, tiled=True)
    weights = lax.all_to_all(
        weight_buffer.astype(jnp.bfloat16), ("lon", "lat"), split_axis=0, concat_axis=0, tiled=True
    ).astype(weight_buffer.dtype)
    profile_rows = jnp.einsum(
        "snc,cl->snl", radiance, jacobian, preferred_element_type=jnp.float32
    ).astype(jnp.bfloat16)
    level_count = jacobian.shape[1]
    band_rows = face_rates.shape[1]
    band_cols = face_rates.shape[2]
    corners = cells.shape[-1]
    slot_count = profile_rows.shape[0] * profile_rows.shape[1]
    profile_slots = profile_rows.reshape(slot_count, level_count).astype(jnp.float32)
    cell_slots = cells.reshape(slot_count, corners)
    weight_slots = weights.reshape(slot_count, corners)
    rows_block = math.gcd(band_rows, max(1, 512 // band_cols))
    block_cells = rows_block * band_cols
    block_count = band_rows // rows_block

    def cell_block(block_index):
        first = block_index * block_cells
        local_cells = cell_slots - first
        columns = jnp.arange(block_cells, dtype=jnp.int32)
        spread_map = jnp.zeros((slot_count, block_cells), jnp.float32)
        for corner in range(corners):
            spread_map = spread_map + jnp.where(
                local_cells[:, corner : corner + 1] == columns[None, :],
                weight_slots[:, corner : corner + 1],
                0.0,
            )
        return jnp.einsum(
            "sv,sc->vc",
            profile_slots,
            spread_map,
            precision=lax.Precision.HIGHEST,
            preferred_element_type=jnp.float32,
        )

    blocks = lax.map(cell_block, jnp.arange(block_count, dtype=jnp.int32))
    field = jnp.transpose(blocks, (1, 0, 2)).reshape(level_count, band_rows, band_cols)
    depth = STEPS
    rates = extended_2(face_rates.astype(jnp.bfloat16), (("lon", 2),), depth, True).astype(
        face_rates.dtype
    )
    rates = extended_2(rates.astype(jnp.bfloat16), (("lat", 1),), depth, False).astype(rates.dtype)
    total_rows = band_rows * lax.axis_size("lat")
    global_row = (
        lax.axis_index("lat") * band_rows
        + jnp.arange(band_rows + 2 * depth, dtype=jnp.int32)
        - depth
    )
    inside = ((global_row >= 0) & (global_row < total_rows - 1)).astype(jnp.float32)
    kappa_x = rates[0]
    kappa_y = rates[1]
    face_x = 0.5 * (kappa_x[:, 1:] + kappa_x[:, :-1])
    face_y = 0.5 * (kappa_y[1:, :] + kappa_y[:-1, :]) * inside[:-1, None]
    full_rows = kappa_x.shape[0]
    full_cols = kappa_x.shape[1]
    margin = depth - 1
    crop_x = face_x[margin : full_rows - margin, margin : full_cols - 1 - margin]
    crop_y = face_y[margin : full_rows - 1 - margin, margin : full_cols - margin]
    for sweep in range(depth):
        extended = extended_2(field, (("lon", 2),), 1, True)
        extended = extended_2(extended, (("lat", 1),), 1, False)
        field = shrink(extended, crop_x, crop_y)
    return field


def solution(mesh):
    in_specs = (
        P(("lon", "lat"), None),
        P(("lon", "lat"), None),
        P(("lon", "lat"), None),
        P(("lon", "lat"), None),
        P(),
        P(),
        P(None, "lat", "lon"),
    )
    out_specs = P(None, "lat", "lon")
    return jax.shard_map(local, mesh=mesh, in_specs=in_specs, out_specs=out_specs, check_vma=False)
```

profile of v0, /device:TPU:32, one launch (start us, length us, event | category | flops | bytes accessed | tf_op | source)
XLA Modules:
  0.0 721.9 jit_solution(13839811592752666484)
XLA Ops:
  4.5 37.2 %select_reduce_fusion = s32[8192]{0:T(1024)S(1)} fusion(s32[4096]{0:T(1024)S(1)} %multiply_add_fusion), kind=kLoop, calls=%fused_computation.28 | loop fusion | flops 100655104 | bytes 49152 | tf_op jit(solution)/shard_map/reduce_sum | solution.py:41
  41.7 37.2 %fusion.24 = pred[8192]{0:T(1024)(128)(4,1)S(1)} fusion(s32[4096]{0:T(1024)S(1)} %multiply_add_fusion), kind=kLoop, calls=%fused_computation.30 | loop fusion | flops 67100672 | bytes 24576 | tf_op jit(solution)/shard_map/reduce_or | solution.py:40
  79.7 24.0 %gather_fusion.1 = bf16[8192,4]{1,0:T(8,128)(2,1)S(1)} fusion(bf16[4096,4]{1,0:T(8,128)(2,1)S(1)} %copy.167, s32[8192]{0:T(1024)S(1)} %broadcast_clamp_fusion), kind=kCustom, calls=%fused_computation.1 | custom fusion | bytes 163840 | tf_op jit(solution)/shard_map/jit(_take)/gather | solution.py:46
  105.7 10.2 %all-to-all-start.1 = ((bf16[128,2,128]{2,1,0:T(2,128)(2,1)}), bf16[128,2,128]{2,1,0:T(2,128)(2,1)S(1)}, u32[]{:S(2)}, u32[]{:S(2)}) async-start(bf16[128,2,128]{2,1,0:T(2,128)(2,1)} %reshape.137), calls=%async_computation.1 | async-start | bytes 131072 | tf_op jit(solution)/shard_map/all_to_all | solution.py:58
  116.6 27.9 %gather_fusion = s32[8192,4]{1,0:T(8,128)} fusion(s32[4096,4]{1,0:T(8,128)S(1)} %copy.164, s32[8192]{0:T(1024)S(1)} %broadcast_clamp_fusion), kind=kCustom, calls=%fused_computation | custom fusion | bytes 294912 | tf_op jit(solution)/shard_map/jit(_take)/gather | solution.py:46
  148.8 24.0 %gather_fusion.2 = bf16[8192,128]{1,0:T(8,128)(2,1)S(1)} fusion(bf16[4096,128]{1,0:T(8,128)(2,1)S(1)} %multiply_convert_fusion, s32[8192]{0:T(1024)S(1)} %broadcast_clamp_fusion), kind=kCustom, calls=%fused_computation.2 | custom fusion | bytes 4227072 | tf_op jit(solution)/shard_map/jit(_take)/gather | solution.py:46
  172.8 9.8 %all-to-all-start = ((s32[128,1,256]{2,1,0:T(1,128)}), s32[128,1,256]{2,1,0:T(1,128)S(1)}, u32[]{:S(2)}, u32[]{:S(2)}) async-start(s32[128,1,256]{2,1,0:T(1,128)} %reshape.139), calls=%async_computation | async-start | bytes 262144 | tf_op jit(solution)/shard_map/all_to_all | solution.py:57
  182.6 4.5 select_select_fusion
  191.6 5.4 all-to-all-start.2
  197.0 4.8 collective-permute-start.1
  201.9 16.6 %collective-permute-done.1 = bf16[2,32,4]{2,1,0:T(8,128)(2,1)S(1)} collective-permute-done((bf16[2,32,4]{2,1,0:T(8,128)(2,1)S(1)}, bf16[2,32,4]{2,1,0:T(8,128)(2,1)S(1)}, u32[]{:S(2)}, u32[]{:S(2)}) %collective-permute-start.1) | collective-permute-done | bytes 544 | tf_op jit(solution)/shard_map/ppermute | solution.py:19
  218.5 6.2 collective-permute-done
  239.3 9.0 %copy.215 = f32[128,64,160]{2,1,0:T(8,128)} copy(f32[128,64,160]{0,2,1:T(8,128)} %convert_convert_fusion) | data formatting | bytes 10485760 | tf_op jit(solution)/shard_map/while | solution.py:95
  248.3 281.9 %while.10 = (s32[]{:T(128)}, f32[8,160,512]{2,1,0:T(8,128)}, s32[8]{0:T(128)S(1)}, s32[8192,4]{0,1:T(4,128)S(1)}, f32[8192,4]{0,1:T(4,128)S(1)}, /*index=5*/f32[8192,160]{1,0:T(8,128)}, s32[]{:T(128)}, s32[1]{0:T(128)}) while((s32[]{:T(128)}, f32[8,160,512]{2,1,0:T(8,128)}, s32[8]{0:T(128)S(1)}, s32[8192,4]{0,1:T(4,128)S(1)}, ...), condition=%wide.region_6.7_spmd, body=%wide.region_5.6_spmd.sunk | while | flops 8099233792 | bytes 9764989 | solution.py:95
  249.6 33.9 %fusion.71 = f32[8,160,512]{2,1,0:T(8,128)} fusion(f32[8,160,512]{2,1,0:T(8,128)} %get-tuple-element.172, s32[]{:T(128)S(6)} %copy.224, f32[8192,160]{1,0:T(8,128)} %get-tuple-element.184, f32[8192]{0:T(1024)S(1)} %bitcast.81, s32[8192]{0:T(1024)S(1)} %bitcast.85, f32[8192]{0:T(1024)S(1)} %bitcast.82, s32[8192]{0:T(1024)S(1)} %bitcast.86, ...), kind=kOutput, calls=%fused_computation.25.clone.2 | convolution fusion | flops 8099201024 | bytes 8978436 | tf_op jit(solution)/shard_map/while/body/eval_jaxpr/sv,sc->vc/dot_general | solution.py:87
  284.9 33.9 %fusion.71 = f32[8,160,512]{2,1,0:T(8,128)} fusion(f32[8,160,512]{2,1,0:T(8,128)} %get-tuple-element.172, s32[]{:T(128)S(6)} %copy.224, f32[8192,160]{1,0:T(8,128)} %get-tuple-element.184, f32[8192]{0:T(1024)S(1)} %bitcast.81, s32[8192]{0:T(1024)S(1)} %bitcast.85, f32[8192]{0:T(1024)S(1)} %bitcast.82, s32[8192]{0:T(1024)S(1)} %bitcast.86, ...), kind=kOutput, calls=%fused_computation.25.clone.2 | convolution fusion | flops 8099201024 | bytes 8978436 | tf_op jit(solution)/shard_map/while/body/eval_jaxpr/sv,sc->vc/dot_general | solution.py:87
  320.1 33.9 %fusion.71 = f32[8,160,512]{2,1,0:T(8,128)} fusion(f32[8,160,512]{2,1,0:T(8,128)} %get-tuple-element.172, s32[]{:T(128)S(6)} %copy.224, f32[8192,160]{1,0:T(8,128)} %get-tuple-element.184, f32[8192]{0:T(1024)S(1)} %bitcast.81, s32[8192]{0:T(1024)S(1)} %bitcast.85, f32[8192]{0:T(1024)S(1)} %bitcast.82, s32[8192]{0:T(1024)S(1)} %bitcast.86, ...), kind=kOutput, calls=%fused_computation.25.clone.2 | convolution fusion | flops 8099201024 | bytes 8978436 | tf_op jit(solution)/shard_map/while/body/eval_jaxpr/sv,sc->vc/dot_general | solution.py:87
  355.3 33.9 %fusion.71 = f32[8,160,512]{2,1,0:T(8,128)} fusion(f32[8,160,512]{2,1,0:T(8,128)} %get-tuple-element.172, s32[]{:T(128)S(6)} %copy.224, f32[8192,160]{1,0:T(8,128)} %get-tuple-element.184, f32[8192]{0:T(1024)S(1)} %bitcast.81, s32[8192]{0:T(1024)S(1)} %bitcast.85, f32[8192]{0:T(1024)S(1)} %bitcast.82, s32[8192]{0:T(1024)S(1)} %bitcast.86, ...), kind=kOutput, calls=%fused_computation.25.clone.2 | convolution fusion | flops 8099201024 | bytes 8978436 | tf_op jit(solution)/shard_map/while/body/eval_jaxpr/sv,sc->vc/dot_general | solution.py:87
  390.6 33.9 %fusion.71 = f32[8,160,512]{2,1,0:T(8,128)} fusion(f32[8,160,512]{2,1,0:T(8,128)} %get-tuple-element.172, s32[]{:T(128)S(6)} %copy.224, f32[8192,160]{1,0:T(8,128)} %get-tuple-element.184, f32[8192]{0:T(1024)S(1)} %bitcast.81, s32[8192]{0:T(1024)S(1)} %bitcast.85, f32[8192]{0:T(1024)S(1)} %bitcast.82, s32[8192]{0:T(1024)S(1)} %bitcast.86, ...), kind=kOutput, calls=%fused_computation.25.clone.2 | convolution fusion | flops 8099201024 | bytes 8978436 | tf_op jit(solution)/shard_map/while/body/eval_jaxpr/sv,sc->vc/dot_general | solution.py:87
  425.8 33.9 %fusion.71 = f32[8,160,512]{2,1,0:T(8,128)} fusion(f32[8,160,512]{2,1,0:T(8,128)} %get-tuple-element.172, s32[]{:T(128)S(6)} %copy.224, f32[8192,160]{1,0:T(8,128)} %get-tuple-element.184, f32[8192]{0:T(1024)S(1)} %bitcast.81, s32[8192]{0:T(1024)S(1)} %bitcast.85, f32[8192]{0:T(1024)S(1)} %bitcast.82, s32[8192]{0:T(1024)S(1)} %bitcast.86, ...), kind=kOutput, calls=%fused_computation.25.clone.2 | convolution fusion | flops 8099201024 | bytes 8978436 | tf_op jit(solution)/shard_map/while/body/eval_jaxpr/sv,sc->vc/dot_general | solution.py:87
  461.0 33.9 %fusion.71 = f32[8,160,512]{2,1,0:T(8,128)} fusion(f32[8,160,512]{2,1,0:T(8,128)} %get-tuple-element.172, s32[]{:T(128)S(6)} %copy.224, f32[8192,160]{1,0:T(8,128)} %get-tuple-element.184, f32[8192]{0:T(1024)S(1)} %bitcast.81, s32[8192]{0:T(1024)S(1)} %bitcast.85, f32[8192]{0:T(1024)S(1)} %bitcast.82, s32[8192]{0:T(1024)S(1)} %bitcast.86, ...), kind=kOutput, calls=%fused_computation.25.clone.2 | convolution fusion | flops 8099201024 | bytes 8978436 | tf_op jit(solution)/shard_map/while/body/eval_jaxpr/sv,sc->vc/dot_general | solution.py:87
  496.3 33.9 %fusion.71 = f32[8,160,512]{2,1,0:T(8,128)} fusion(f32[8,160,512]{2,1,0:T(8,128)} %get-tuple-element.172, s32[]{:T(128)S(6)} %copy.224, f32[8192,160]{1,0:T(8,128)} %get-tuple-element.184, f32[8192]{0:T(1024)S(1)} %bitcast.81, s32[8192]{0:T(1024)S(1)} %bitcast.85, f32[8192]{0:T(1024)S(1)} %bitcast.82, s32[8192]{0:T(1024)S(1)} %bitcast.86, ...), kind=kOutput, calls=%fused_computation.25.clone.2 | convolution fusion | flops 8099201024 | bytes 8978436 | tf_op jit(solution)/shard_map/while/body/eval_jaxpr/sv,sc->vc/dot_general | solution.py:87
  530.2 4.7 copy.174
  567.9 4.9 fusion.25
  574.0 5.0 fusion.36
  613.7 4.9 fusion.26
  619.7 5.0 fusion.34
  659.1 4.9 fusion.27
  665.7 5.2 fusion.32
  704.1 4.9 fusion.28
  710.6 5.0 fusion.30
  715.6 6.0 slice_subtract_fusion
  (191 shorter events, 177.7 us)
Async XLA Ops:
  0.0 235.1 %copy-start = (bf16[128,160]{0,1:T(8,128)(2,1)S(1)}, bf16[128,160]{0,1:T(8,128)(2,1)}, u32[]{:S(2)}) copy-start(bf16[128,160]{0,1:T(8,128)(2,1)} %param.14) | copy-start | bytes 122884
  1.8 77.4 %copy-start.10 = (f32[4096,4]{0,1:T(4,128)S(1)}, f32[4096,4]{0,1:T(4,128)}, u32[]{:S(2)}) copy-start(f32[4096,4]{0,1:T(4,128)} %param.12) | copy-start | bytes 196612
  79.7 36.3 %copy-start.11 = (s32[4096,4]{0,1:T(4,128)S(1)}, s32[4096,4]{0,1:T(4,128)}, u32[]{:S(2)}) copy-start(s32[4096,4]{0,1:T(4,128)} %param.11) | copy-start | bytes 196612
  105.7 67.1 %all-to-all-start.1 = ((bf16[128,2,128]{2,1,0:T(2,128)(2,1)}), bf16[128,2,128]{2,1,0:T(2,128)(2,1)S(1)}, u32[]{:S(2)}, u32[]{:S(2)}) async-start(bf16[128,2,128]{2,1,0:T(2,128)(2,1)} %reshape.137), calls=%async_computation.1 | async-start | bytes 131072 | tf_op jit(solution)/shard_map/all_to_all | solution.py:58
  172.8 18.7 %all-to-all-start = ((s32[128,1,256]{2,1,0:T(1,128)}), s32[128,1,256]{2,1,0:T(1,128)S(1)}, u32[]{:S(2)}, u32[]{:S(2)}) async-start(s32[128,1,256]{2,1,0:T(1,128)} %reshape.139), calls=%async_computation | async-start | bytes 262144 | tf_op jit(solution)/shard_map/all_to_all | solution.py:57
  182.6 14.3 %copy-start.12 = (f32[2,32,128]{2,1,0:T(8,128)S(1)}, f32[2,32,128]{2,1,0:T(8,128)}, u32[]{:S(2)}) copy-start(f32[2,32,128]{2,1,0:T(8,128)} %param.15) | copy-start | bytes 98308
  191.6 43.5 %all-to-all-start.2 = ((bf16[128,64,128]{2,1,0:T(8,128)(2,1)}), bf16[128,64,128]{2,1,0:T(8,128)(2,1)S(1)}, u32[]{:S(2)}, u32[]{:S(2)}) async-start(bf16[128,64,128]{2,1,0:T(8,128)(2,1)} %select_select_fusion), calls=%async_computation.2 | async-start | bytes 4194304 | tf_op jit(solution)/shard_map/all_to_all | solution.py:54
  197.0 21.4 %collective-permute-start.1 = (bf16[2,32,4]{2,1,0:T(8,128)(2,1)S(1)}, bf16[2,32,4]{2,1,0:T(8,128)(2,1)S(1)}, u32[]{:S(2)}, u32[]{:S(2)}) collective-permute-start(bf16[2,32,4]{2,1,0:T(8,128)(2,1)S(1)} %get-tuple-element.109), channel_id=1, source_target_pairs={{4,0},{8,4},{12,8},{16,12},{20,16},{24,20},{28,24},{32,28},{36,32}... | collective-permute-start | bytes 1544 | tf_op jit(solution)/shard_map/ppermute | solution.py:19
  201.8 22.8 %collective-permute-start = (bf16[2,32,4]{2,1,0:T(8,128)(2,1)S(1)}, bf16[2,32,4]{2,1,0:T(8,128)(2,1)S(1)}, u32[]{:S(2)}, u32[]{:S(2)}) collective-permute-start(bf16[2,32,4]{2,1,0:T(8,128)(2,1)S(1)} %get-tuple-element.108), channel_id=1, source_target_pairs={{0,4},{4,8},{8,12},{12,16},{16,20},{20,24},{24,28},{28,32},{32,36}... | collective-permute-start | bytes 1544 | tf_op jit(solution)/shard_map/ppermute | solution.py:18
  224.7 6.4 collective-permute-start.3
  226.9 5.5 collective-permute-start.2
  544.6 4.7 collective-permute-start.4
  548.5 6.9 collective-permute-start.5
  561.9 10.9 %collective-permute-start.7 = (f32[160,1,130]{0,2,1:T(8,128)S(1)}, f32[160,1,130]{0,2,1:T(8,128)S(1)}, u32[]{:S(2)}, u32[]{:S(2)}) collective-permute-start(f32[160,1,130]{0,2,1:T(8,128)S(1)} %copy.183), channel_id=1, source_target_pairs={{0,1},{1,2},{2,3},{4,5},{5,6},{6,7},{8,9},{9,10},{10,11},{12,13},{... | collective-permute-start | bytes 249608 | tf_op jit(solution)/shard_map/ppermute | solution.py:18
  565.7 7.3 %collective-permute-start.6 = (f32[160,1,130]{0,2,1:T(8,128)S(1)}, f32[160,1,130]{0,2,1:T(8,128)}, u32[]{:S(2)}, u32[]{:S(2)}) collective-permute-start(f32[160,1,130]{0,2,1:T(8,128)S(1)} %copy.181), channel_id=1, source_target_pairs={{1,0},{2,1},{3,2},{5,4},{6,5},{7,6},{9,8},{10,9},{11,10},{13,12},{... | collective-permute-start | bytes 249608 | tf_op jit(solution)/shard_map/ppermute | solution.py:19
  589.9 4.2 collective-permute-start.8
  594.0 10.3 %copy-start.3 = (f32[160,32,128]{2,1,0:T(8,128)S(1)}, f32[160,32,128]{2,1,0:T(8,128)}, u32[]{:S(2)}) copy-start(f32[160,32,128]{2,1,0:T(8,128)} %copy-done.2) | copy-start | bytes 7864324
  594.0 6.7 collective-permute-start.9
  607.3 11.3 %collective-permute-start.11 = (f32[160,1,130]{0,2,1:T(8,128)S(1)}, f32[160,1,130]{0,2,1:T(8,128)S(1)}, u32[]{:S(2)}, u32[]{:S(2)}) collective-permute-start(f32[160,1,130]{0,2,1:T(8,128)S(1)} %copy.193), channel_id=1, source_target_pairs={{0,1},{1,2},{2,3},{4,5},{5,6},{6,7},{8,9},{9,10},{10,11},{12,13},{... | collective-permute-start | bytes 249608 | tf_op jit(solution)/shard_map/ppermute | solution.py:18
  611.0 7.7 %collective-permute-start.10 = (f32[160,1,130]{0,2,1:T(8,128)S(1)}, f32[160,1,130]{0,2,1:T(8,128)}, u32[]{:S(2)}, u32[]{:S(2)}) collective-permute-start(f32[160,1,130]{0,2,1:T(8,128)S(1)} %copy.191), channel_id=1, source_target_pairs={{1,0},{2,1},{3,2},{5,4},{6,5},{7,6},{9,8},{10,9},{11,10},{13,12},{... | collective-permute-start | bytes 249608 | tf_op jit(solution)/shard_map/ppermute | solution.py:19
  635.6 4.1 collective-permute-start.12
  639.5 10.5 %copy-start.5 = (f32[160,32,128]{2,1,0:T(8,128)S(1)}, f32[160,32,128]{2,1,0:T(8,128)}, u32[]{:S(2)}) copy-start(f32[160,32,128]{2,1,0:T(8,128)} %copy-done.4) | copy-start | bytes 7864324
  639.5 6.9 collective-permute-start.13
  653.0 11.1 %collective-permute-start.15 = (f32[160,1,130]{0,2,1:T(8,128)S(1)}, f32[160,1,130]{0,2,1:T(8,128)S(1)}, u32[]{:S(2)}, u32[]{:S(2)}) collective-permute-start(f32[160,1,130]{0,2,1:T(8,128)S(1)} %copy.203), channel_id=1, source_target_pairs={{0,1},{1,2},{2,3},{4,5},{5,6},{6,7},{8,9},{9,10},{10,11},{12,13},{... | collective-permute-start | bytes 249608 | tf_op jit(solution)/shard_map/ppermute | solution.py:18
  657.2 7.4 %collective-permute-start.14 = (f32[160,1,130]{0,2,1:T(8,128)S(1)}, f32[160,1,130]{0,2,1:T(8,128)}, u32[]{:S(2)}, u32[]{:S(2)}) collective-permute-start(f32[160,1,130]{0,2,1:T(8,128)S(1)} %copy.201), channel_id=1, source_target_pairs={{1,0},{2,1},{3,2},{5,4},{6,5},{7,6},{9,8},{10,9},{11,10},{13,12},{... | collective-permute-start | bytes 249608 | tf_op jit(solution)/shard_map/ppermute | solution.py:19
  665.6 5.3 copy-start.6
  665.6 5.3 copy-start.7
  679.1 5.5 collective-permute-start.16
  684.5 6.7 collective-permute-start.17
  697.8 11.2 %collective-permute-start.19 = (f32[160,1,130]{0,2,1:T(8,128)S(1)}, f32[160,1,130]{0,2,1:T(8,128)S(1)}, u32[]{:S(2)}, u32[]{:S(2)}) collective-permute-start(f32[160,1,130]{0,2,1:T(8,128)S(1)} %copy.213), channel_id=1, source_target_pairs={{0,1},{1,2},{2,3},{4,5},{5,6},{6,7},{8,9},{9,10},{10,11},{12,13},{... | collective-permute-start | bytes 249608 | tf_op jit(solution)/shard_map/ppermute | solution.py:18
  702.1 7.4 %collective-permute-start.18 = (f32[160,1,130]{0,2,1:T(8,128)S(1)}, f32[160,1,130]{0,2,1:T(8,128)}, u32[]{:S(2)}, u32[]{:S(2)}) collective-permute-start(f32[160,1,130]{0,2,1:T(8,128)S(1)} %copy.211), channel_id=1, source_target_pairs={{1,0},{2,1},{3,2},{5,4},{6,5},{7,6},{9,8},{10,9},{11,10},{13,12},{... | collective-permute-start | bytes 249608 | tf_op jit(solution)/shard_map/ppermute | solution.py:19
  715.6 6.0 copy-start.1
  (5 other events, 12.5 us)
where the time goes:
time: 732 us; the launch traced here: 722 us
  matrix products  275 us (38%)
  local copies, waits for them, and re-layouts  183 us (25%)
  other arithmetic  151 us (21%)
  starting transfers between devices  66.5 us (9%)
  waiting for transfers between devices  41.1 us (6%)
    dot_general x8, matrix products, cell_block(): jnp.einsum('sv,sc->vc', profile_slots, spread_map, precision=lax.Precisio...  271 us
    gather x5, local copies, waits for them, and re-layouts, pack_rows(): picked = jnp.take(row_data, slot_source, axis=0)  80 us
    reduce_or x1, other arithmetic, local(): slot_filled = jnp.any(slot_match, axis=1)  37.2 us
    reduce_sum x1, other arithmetic, local(): jnp.sum(jnp.where(slot_match, jnp.arange(ingest_rows, dtype=jnp.int32)[No...  37.2 us
    slice x13, local copies, waits for them, and re-layouts, extended_2(): last = lax.slice_in_dim(shard, length - width, length, axis=dim)  24.6 us
    ppermute x10, starting transfers between devices, extended_2(): before = lax.ppermute(last, axis, up)  20.7 us
    ppermute x10, starting transfers between devices, extended_2(): after = lax.ppermute(leading, axis, down)  20.4 us
    mul x4, other arithmetic, shrink(): flux_y = face_y[:, 1:-1] * (field[:, 1:, 1:-1] - field[:, :-1, 1:-1])  20.3 us
  transfers between devices with their start and end apart: 23, of which 10 were waited for; matrix products, arithmetic and copies ran while one was open for 16% of the time, Pallas kernels for 0%

commit v1 on v0

v1 whole, which is shorter than its diff:
```python
import functools

import jax
import jax.numpy as jnp
from jax import lax
from jax.experimental import pallas as pl
from jax.experimental.pallas import tpu as pltpu
from jax.sharding import PartitionSpec as P

STEPS = 4
LANES = 128
META = 8
PAD = 8
F32 = jnp.float32
BF16 = jnp.bfloat16
VMEM_LIMIT = 56 * 1024 * 1024


def iota(shape, dim):
    return lax.broadcasted_iota(jnp.int32, shape, dim)


def pack_kernel(cap, owner_ref, cells_ref, weights_ref, rows_ref, out_ref, xd, xm, yd, ym, slots_v, slots_s, sem):
    groups = owner_ref.shape[0]
    slots = yd.shape[0]
    owner_id = iota((LANES, LANES), 0)
    before = (iota((LANES, 2 * LANES), 0) < iota((LANES, 2 * LANES), 1)).astype(F32).astype(BF16)

    def rank_group(g, base):
        own = owner_ref[pl.ds(g, 1), :]
        hit = (own == owner_id).astype(F32)
        seen = jnp.dot(hit.astype(BF16), before, preferred_element_type=F32)
        rank = jnp.sum(hit * (seen[:, :LANES] + base), axis=0, keepdims=True)
        slots_v[pl.ds(g, 1), :] = own * cap + rank.astype(jnp.int32)
        return base + seen[:, LANES:]

    lax.fori_loop(0, groups, rank_group, jnp.zeros((LANES, LANES), F32), unroll=4)
    copy = pltpu.make_async_copy(slots_v, slots_s, sem)
    copy.start()

    def stage(g, _):
        at = pl.ds(pl.multiple_of(g * LANES, LANES), LANES)
        xd[at, :] = rows_ref[at, :].astype(F32)
        cells = cells_ref[:, at]
        weights = weights_ref[:, at]
        c = [cells[k : k + 1] for k in range(4)]
        w = [weights[k : k + 1] for k in range(4)]
        merged = []
        for k in range(4):
            total = w[k]
            for m in range(k + 1, 4):
                total = total + jnp.where(c[m] == c[k], w[m], 0.0)
            for m in range(k):
                total = jnp.where(c[m] == c[k], 0.0, total)
            merged.append(total)
        row = (cells >> 7).astype(F32)
        col = (cells & 127).astype(F32)
        block = jnp.concatenate([row, col] + merged + [jnp.zeros((LANES - 12, LANES), F32)], axis=0)
        xm[at, :] = block.T
        return 0

    lax.fori_loop(0, groups, stage, 0, unroll=2)

    def clear(g, _):
        at = pl.ds(pl.multiple_of(g * LANES, LANES), LANES)
        yd[at, :] = jnp.zeros((LANES, LANES), F32)
        ym[at, :] = jnp.zeros((LANES, LANES), F32)
        return 0

    lax.fori_loop(0, slots // LANES, clear, 0, unroll=2)
    copy.wait()

    def move(g, _):
        first = pl.multiple_of(g * LANES, LANES)
        for u in range(LANES):
            s = slots_s[g, u]
            yd[pl.ds(s, 1), :] = xd[pl.ds(first + u, 1), :]
            ym[pl.ds(s, 1), :] = xm[pl.ds(first + u, 1), :]
        return 0

    lax.fori_loop(0, groups, move, 0)

    pick = (iota((16, LANES), 0) == iota((16, LANES), 1)).astype(F32).astype(BF16)
    left = iota((META, LANES), 1) < cap
    step = 2 * (cap + META)

    def emit(a, _):
        at = pl.ds(pl.multiple_of(a * LANES, LANES), LANES)
        data = yd[at, :]
        meta = lax.dot_general(
            pick, ym[at, :].astype(BF16), (((1,), (1,)), ((), ())), preferred_element_type=F32
        )
        low, high = meta[:META], meta[META:]
        first = jnp.where(left, low, pltpu.roll(high, cap, 1))
        second = jnp.where(left, pltpu.roll(low, cap, 1), high)
        block = jnp.concatenate([data[:cap], first, data[cap:], second], axis=0)
        out_ref[pl.ds(pl.multiple_of(a * step, 16), step), :] = block.astype(BF16)
        return 0

    lax.fori_loop(0, slots // LANES, emit, 0, unroll=2)


def pack(owner, cells, weights, rows, devices, cap):
    count = rows.shape[0]
    slots = devices * cap
    full = pl.BlockSpec(memory_space=pltpu.VMEM)
    return pl.pallas_call(
        functools.partial(pack_kernel, cap),
        out_shape=jax.ShapeDtypeStruct((devices * (cap + META), LANES), BF16),
        in_specs=[full] * 4,
        out_specs=full,
        scratch_shapes=[
            pltpu.VMEM((count, LANES), F32),
            pltpu.VMEM((count, LANES), F32),
            pltpu.VMEM((slots, LANES), F32),
            pltpu.VMEM((slots, LANES), F32),
            pltpu.VMEM((count // LANES, LANES), jnp.int32),
            pltpu.SMEM((count // LANES, LANES), jnp.int32),
            pltpu.SemaphoreType.DMA,
        ],
        compiler_params=pltpu.CompilerParams(vmem_limit_bytes=VMEM_LIMIT),
        cost_estimate=pl.CostEstimate(flops=4_000_000_000, bytes_accessed=40_000_000, transcendentals=0),
        name="pack",
    )(owner.reshape(count // LANES, LANES), cells.T, weights.T, rows)


def scatter_kernel(
    cap, lat_rows, recv_ref, field_ref, south_ref, north_ref, west_ref, east_ref, corner_ref, rows, meta, side
):
    slots = rows.shape[0]
    left = iota((META, LANES), 1) < cap
    step = 2 * (cap + META)
    lon_cols = field_ref.shape[0] // lat_rows

    def unpack(b, _):
        block = recv_ref[pl.ds(pl.multiple_of(b * step, 16), step), :].astype(F32)
        data = jnp.concatenate([block[:cap], block[cap + META : 2 * cap + META]], axis=0)
        rows[pl.ds(pl.multiple_of(b * LANES, LANES), LANES), :] = data.astype(BF16)
        first, second = block[cap : cap + META], block[2 * cap + META :]
        meta[b] = jnp.concatenate(
            [
                jnp.where(left, first, pltpu.roll(second, cap, 1)),
                jnp.where(left, pltpu.roll(first, cap, 1), second),
            ],
            axis=0,
        )
        return 0

    lax.fori_loop(0, slots // LANES, unpack, 0, unroll=2)
    field_ref[...] = jnp.zeros_like(field_ref)
    depth = 2 * LANES
    per = 8
    col_id = iota((lon_cols, depth), 0).astype(F32)
    row_id = iota((lat_rows, depth), 0).astype(F32)

    def accumulate(t, _):
        both = jnp.concatenate([meta[2 * t], meta[2 * t + 1]], axis=1)
        data = rows[pl.ds(pl.multiple_of(t * depth, depth), depth), :]
        col, row = [], []
        for k in range(4):
            col.append((both[4 + k : 5 + k] == col_id).astype(F32).astype(BF16))
            row.append(jnp.where(both[k : k + 1] == row_id, both[8 + k : 9 + k], 0.0))
        for block in range(lat_rows // per):
            parts = []
            for i in range(block * per, block * per + per):
                total = None
                for k in range(4):
                    term = jnp.broadcast_to(row[k][i : i + 1], (lon_cols, depth)).astype(BF16) * col[k]
                    total = term if total is None else total + term
                parts.append(total)
            spread = jnp.concatenate(parts, axis=0)
            at = pl.ds(block * per * lon_cols, per * lon_cols)
            field_ref[at, :] += jnp.dot(spread, data, preferred_element_type=F32)
        return 0

    lax.fori_loop(0, slots // depth, accumulate, 0)

    wide = STEPS * lon_cols
    total = lat_rows * lon_cols
    south_ref[...] = field_ref[:wide, :].astype(BF16)
    north_ref[...] = field_ref[total - wide :, :].astype(BF16)
    for i in range(lat_rows):
        side[0, pl.ds(STEPS * i, STEPS), :] = field_ref[pl.ds(i * lon_cols, STEPS), :]
        side[1, pl.ds(STEPS * i, STEPS), :] = field_ref[pl.ds((i + 1) * lon_cols - STEPS, STEPS), :]
    west = side[0]
    east = side[1]
    west_ref[...] = west.astype(BF16)
    east_ref[...] = east.astype(BF16)
    edge = STEPS * STEPS
    corner_ref[0] = west[:edge].astype(BF16)
    corner_ref[1] = east[:edge].astype(BF16)
    corner_ref[2] = west[-edge:].astype(BF16)
    corner_ref[3] = east[-edge:].astype(BF16)


def scatter(recv, devices, cap, lat_rows, lon_cols):
    slots = devices * cap
    full = pl.BlockSpec(memory_space=pltpu.VMEM)
    wide = STEPS * lon_cols
    tall = STEPS * lat_rows
    shapes = [
        jax.ShapeDtypeStruct((lat_rows * lon_cols, LANES), F32),
        jax.ShapeDtypeStruct((wide, LANES), BF16),
        jax.ShapeDtypeStruct((wide, LANES), BF16),
        jax.ShapeDtypeStruct((tall, LANES), BF16),
        jax.ShapeDtypeStruct((tall, LANES), BF16),
        jax.ShapeDtypeStruct((4, STEPS * STEPS, LANES), BF16),
    ]
    return pl.pallas_call(
        functools.partial(scatter_kernel, cap, lat_rows),
        out_shape=shapes,
        in_specs=[full],
        out_specs=[full] * len(shapes),
        scratch_shapes=[
            pltpu.VMEM((slots, LANES), BF16),
            pltpu.VMEM((slots // LANES, 16, LANES), F32),
            pltpu.VMEM((2, tall, LANES), F32),
        ],
        compiler_params=pltpu.CompilerParams(vmem_limit_bytes=VMEM_LIMIT),
        cost_estimate=pl.CostEstimate(flops=17_000_000_000, bytes_accessed=20_000_000, transcendentals=0),
        name="scatter",
    )(recv)


def diffuse_kernel(
    lat_rows,
    field_ref,
    south_ref,
    north_ref,
    west_ref,
    east_ref,
    corner_ref,
    face_x,
    face_y,
    gain_ref,
    jac_ref,
    out_ref,
    ping,
    pong,
):
    lon_cols = field_ref.shape[0] // lat_rows
    width = lon_cols + 2 * PAD
    tall = lat_rows + 2 * STEPS
    lead = PAD - STEPS
    trail = PAD + lon_cols
    west = west_ref[...].astype(F32)
    east = east_ref[...].astype(F32)
    corner = corner_ref[...].astype(F32)
    for i in range(tall):
        if i < STEPS:
            middle = south_ref[pl.ds(i * lon_cols, lon_cols), :].astype(F32)
            before = corner[0][STEPS * i : STEPS * i + STEPS]
            after = corner[1][STEPS * i : STEPS * i + STEPS]
        elif i < STEPS + lat_rows:
            n = i - STEPS
            middle = field_ref[pl.ds(n * lon_cols, lon_cols), :]
            before = west[STEPS * n : STEPS * n + STEPS]
            after = east[STEPS * n : STEPS * n + STEPS]
        else:
            n = i - STEPS - lat_rows
            middle = north_ref[pl.ds(n * lon_cols, lon_cols), :].astype(F32)
            before = corner[2][STEPS * n : STEPS * n + STEPS]
            after = corner[3][STEPS * n : STEPS * n + STEPS]
        ping[pl.ds(i * width, PAD), :] = jnp.zeros((PAD, LANES), F32)
        ping[pl.ds(i * width + trail, PAD), :] = jnp.zeros((PAD, LANES), F32)
        ping[pl.ds(i * width + PAD, lon_cols), :] = middle
        ping[pl.ds(i * width + lead, STEPS), :] = before
        ping[pl.ds(i * width + trail, STEPS), :] = after

    def row_at(i):
        return pl.ds(pl.multiple_of(i * width, 8), width)

    for sweep in range(STEPS):
        old, new = (ping, pong) if sweep % 2 == 0 else (pong, ping)
        low, high = sweep + 1, tall - sweep - 1

        def one_row(i, carry, old=old, new=new):
            here, flux_below = carry
            above = old[row_at(i + 1), :]
            flux_y = face_y[row_at(i), :] * (above - here)
            flux_x = face_x[row_at(i), :] * (pltpu.roll(here, width - 1, 0) - here)
            new[row_at(i), :] = here + flux_x - pltpu.roll(flux_x, 1, 0) + flux_y - flux_below
            return above, flux_y

        here = old[row_at(low), :]
        start = face_y[row_at(low - 1), :] * (here - old[row_at(low - 1), :])
        lax.fori_loop(low, high, one_row, (here, start))

    last = ping if STEPS % 2 == 0 else pong
    gain = gain_ref[...]
    jac = jnp.concatenate([jac_ref[...], jac_ref[...]], axis=1)
    levels = jac_ref.shape[0]

    def project(h, _):
        pair = []
        for u in range(2):
            at = pl.multiple_of((2 * h + u + STEPS) * width + PAD, 8)
            value = last[pl.ds(at, lon_cols), :] * gain
            head = value.astype(BF16)
            rest = (value - head.astype(F32)).astype(BF16)
            pair.append(jnp.concatenate([head, rest], axis=1))
        both = jnp.concatenate(pair, axis=0)
        result = lax.dot_general(jac, both, (((1,), (1,)), ((), ())), preferred_element_type=F32)
        out_ref[pl.ds(2 * h, levels, stride=lat_rows), :] = result[:, :lon_cols]
        out_ref[pl.ds(2 * h + 1, levels, stride=lat_rows), :] = result[:, lon_cols:]
        return 0

    lax.fori_loop(0, lat_rows // 2, project, 0)


def diffuse(field, south, north, west, east, corner, face_x, face_y, inv_var, jacobian, lat_rows, lon_cols):
    full = pl.BlockSpec(memory_space=pltpu.VMEM)
    levels = jacobian.shape[1]
    tall, width = lat_rows + 2 * STEPS, lon_cols + 2 * PAD
    out = pl.pallas_call(
        functools.partial(diffuse_kernel, lat_rows),
        out_shape=jax.ShapeDtypeStruct((levels * lat_rows, lon_cols), F32),
        in_specs=[full] * 10,
        out_specs=full,
        scratch_shapes=[pltpu.VMEM((tall * width, LANES), F32)] * 2,
        compiler_params=pltpu.CompilerParams(vmem_limit_bytes=VMEM_LIMIT),
        cost_estimate=pl.CostEstimate(flops=1_000_000_000, bytes_accessed=20_000_000, transcendentals=0),
        name="diffuse",
    )(field, south, north, west, east, corner, face_x, face_y, inv_var.reshape(1, -1), jacobian.T)
    return out.reshape(levels, lat_rows, lon_cols)


def moved(value, lon_step, lat_step):
    lons, lats = lax.axis_size("lon"), lax.axis_size("lat")
    pairs = []
    for i in range(lons):
        for j in range(lats):
            if 0 <= j + lat_step < lats:
                source = ((i + lon_step) % lons) * lats + j + lat_step
                pairs.append((source, i * lats + j))
    return lax.ppermute(value, ("lon", "lat"), pairs)


def faces(face_rates):
    lat_rows, lon_cols = face_rates.shape[1:]
    width = lon_cols + 2 * PAD
    before = moved(face_rates[:, :, -STEPS:], -1, 0)
    after = moved(face_rates[:, :, :STEPS], 1, 0)
    rates = jnp.concatenate([before, face_rates, after], axis=2)
    below = moved(rates[:, -STEPS:], 0, -1)
    above = moved(rates[:, :STEPS], 0, 1)
    rates = jnp.concatenate([below, rates, above], axis=1)
    gap = PAD - STEPS
    rates = jnp.pad(rates, ((0, 0), (0, 0), (gap, gap)))
    row = lax.axis_index("lat") * lat_rows + jnp.arange(lat_rows + 2 * STEPS) - STEPS
    inside = (row >= 0) & (row < lat_rows * lax.axis_size("lat") - 1)
    face_x = 0.5 * (rates[0] + jnp.roll(rates[0], -1, 1))
    face_y = jnp.where(inside[:, None], 0.5 * (rates[1] + jnp.roll(rates[1], -1, 0)), 0.0)
    shape = ((lat_rows + 2 * STEPS) * width, LANES)
    return (
        jnp.broadcast_to(face_x.reshape(-1, 1), shape),
        jnp.broadcast_to(face_y.reshape(-1, 1), shape),
    )


def local(departures, obs_owner, obs_cells, interp_weights, inv_var, jacobian, face_rates):
    devices = lax.axis_size(("lon", "lat"))
    cap = 2 * departures.shape[0] // devices
    lat_rows, lon_cols = face_rates.shape[1:]
    face_x, face_y = faces(face_rates)
    send = pack(obs_owner, obs_cells, interp_weights, departures, devices, cap)
    recv = lax.all_to_all(
        send.reshape(devices, cap + META, LANES), ("lon", "lat"), split_axis=0, concat_axis=0, tiled=True
    ).reshape(devices * (cap + META), LANES)
    field, south, north, west, east, corner = scatter(recv, devices, cap, lat_rows, lon_cols)
    below = moved(north, 0, -1)
    above = moved(south, 0, 1)
    before = moved(east, -1, 0)
    after = moved(west, 1, 0)
    corners = jnp.stack(
        [
            moved(corner[3], -1, -1),
            moved(corner[2], 1, -1),
            moved(corner[1], -1, 1),
            moved(corner[0], 1, 1),
        ]
    )
    return diffuse(
        field, below, above, before, after, corners, face_x, face_y, inv_var, jacobian, lat_rows, lon_cols
    )


def solution(mesh):
    in_specs = (
        P(("lon", "lat"), None),
        P(("lon", "lat"), None),
        P(("lon", "lat"), None),
        P(("lon", "lat"), None),
        P(),
        P(),
        P(None, "lat", "lon"),
    )
    out_specs = P(None, "lat", "lon")
    return jax.shard_map(local, mesh=mesh, in_specs=in_specs, out_specs=out_specs, check_vma=False)
```

time: 732 us -> 160 us (0.22); the launches traced: 722 us -> 159 us
  matrix products: 275 us -> 0 us
  local copies, waits for them, and re-layouts: 183 us -> 9.89 us
  other arithmetic: 151 us -> 0.93 us
  Pallas kernels: 0 us -> 66.4 us
  starting transfers between devices: 66.5 us -> 51.7 us
  waiting for transfers between devices: 41.1 us -> 30.1 us
    dot_general x9 -> x0, matrix products: 275 us -> none  [the longest x8 271 us: cell_block(): jnp.einsum('sv,sc->vc', profile_slots, spread_map, precision=lax.Precisio...]
    gather x5 -> x0, local copies, waits for them, and re-layouts: 80 us -> none  [pack_rows(): picked = jnp.take(row_data, slot_source, axis=0)]
    pallas_call x0 -> x3, Pallas kernels: none -> 66.4 us  [the longest x1 32.2 us: scatter(): pl.pallas_call(functools.partial(scatter_kernel, cap, lat_rows), out_shap...]
    slice x39 -> x6, local copies, waits for them, and re-layouts: 42.3 us -> 0.17 us  [the longest x2 0.08 us: faces(): face_x = 0.5 * (rates[0] + jnp.roll(rates[0], -1, 1))]
    mul x11 -> x1, other arithmetic: 40.1 us -> 0.01 us  [faces(): face_x = 0.5 * (rates[0] + jnp.roll(rates[0], -1, 1))]
    reduce_sum x2 -> x0, other arithmetic: 38.6 us -> none  [the longest x1 37.2 us: local(): jnp.sum(jnp.where(slot_match, jnp.arange(ingest_rows, dtype=jnp.int32)[No...]
    reduce_or x1 -> x0, other arithmetic: 37.2 us -> none  [local(): slot_filled = jnp.any(slot_match, axis=1)]
    ppermute x16 -> x0, local copies, waits for them, and re-layouts: 33.2 us -> none  [the longest x8 18.4 us: extended_2(): after = lax.ppermute(leading, axis, down)]
  transfers between devices with their start and end apart: 23 -> 13, of which waited for: 10 -> 4; matrix products, arithmetic and copies ran while one was open for 16% -> 1% of each run, Pallas kernels for 0% -> 0%
where the time goes in v1:
time: 160 us; the launch traced here: 159 us
  Pallas kernels  66.4 us (42%)
  starting transfers between devices  51.7 us (32%)
  waiting for transfers between devices  30.1 us (19%)
  local copies, waits for them, and re-layouts  9.89 us (6%)
    ppermute x12, starting transfers between devices, moved(): return lax.ppermute(value, ('lon', 'lat'), pairs)  41.4 us
    pallas_call x1, Pallas kernels, scatter(): pl.pallas_call(functools.partial(scatter_kernel, cap, lat_rows), out_shap...  32.2 us
    ppermute x12, waiting for transfers between devices, moved(): return lax.ppermute(value, ('lon', 'lat'), pairs)  30.1 us
    pallas_call x1, Pallas kernels, pack(): pl.pallas_call(functools.partial(pack_kernel, cap), out_shape=jax.ShapeDt...  18.7 us
    pallas_call x1, Pallas kernels, diffuse(): pl.pallas_call(functools.partial(diffuse_kernel, lat_rows), out_shape=jax...  15.5 us
    all_to_all x1, starting transfers between devices, local(): lax.all_to_all(send.reshape(devices, cap + META, LANES), ('lon', 'lat'),...  10.2 us
    broadcast_in_dim x1, local copies, waits for them, and re-layouts, faces(): jnp.broadcast_to(face_x.reshape(-1, 1), shape)  3.54 us
    broadcast_in_dim x1, local copies, waits for them, and re-layouts, faces(): jnp.broadcast_to(face_y.reshape(-1, 1), shape)  3.52 us
  transfers between devices with their start and end apart: 13, of which 4 were waited for; matrix products, arithmetic and copies ran while one was open for 1% of the time, Pallas kernels for 0%

profile of v1, /device:TPU:32, one launch (start us, length us, event | category | flops | bytes accessed | tf_op | source)
XLA Modules:
  0.0 159.3 jit_solution(1825736969699593978)
XLA Ops:
  0.0 18.7 %pack.1 = bf16[9216,128]{1,0:T(8,128)(2,1)} custom-call(s32[32,128]{1,0:T(8,128)} %bitcast.36, s32[4,4096]{1,0:T(4,128)} %bitcast.34, f32[4,4096]{1,0:T(4,128)} %bitcast.35, bf16[4096,128]{1,0:T(8,128)(2,1)} %rows_ref.1), custom_call_target="tpu_custom_call" | custom-call | flops 4000000000 | bytes 40000000 | tf_op jit(solution)/shard_map/pack/pallas_call | solution.py:107
  18.7 10.2 %all-to-all-start = ((bf16[128,72,128]{2,1,0:T(8,128)(2,1)}), bf16[128,72,128]{2,1,0:T(8,128)(2,1)S(1)}, u32[]{:S(2)}, u32[]{:S(2)}) async-start(bf16[128,72,128]{2,1,0:T(8,128)(2,1)} %bitcast.27), calls=%async_computation | async-start | bytes 4718592 | tf_op jit(solution)/shard_map/all_to_all | solution.py:367
  29.0 0.2 collective-permute-start.8
  29.2 4.9 %collective-permute-start.9 = (f32[2,32,4]{2,1,0:T(8,128)S(1)}, f32[2,32,4]{2,1,0:T(8,128)S(1)}, u32[]{:S(2)}, u32[]{:S(2)}) collective-permute-start(f32[2,32,4]{2,1,0:T(8,128)S(1)} %get-tuple-element.23), channel_id=1, source_target_pairs={{4,0},{5,1},{6,2},{7,3},{8,4},{9,5},{10,6},{11,7},{12,8},{13,9},{1... | collective-permute-start | bytes 3080 | tf_op jit(solution)/shard_map/ppermute | solution.py:336
  34.1 25.6 %collective-permute-done.8 = f32[2,32,4]{2,1,0:T(8,128)S(1)} collective-permute-done((f32[2,32,4]{2,1,0:T(8,128)S(1)}, f32[2,32,4]{2,1,0:T(8,128)S(1)}, u32[]{:S(2)}, u32[]{:S(2)}) %collective-permute-start.8) | collective-permute-done | bytes 1056 | tf_op jit(solution)/shard_map/ppermute | solution.py:336
  59.8 0.1 pad_maximum_fusion.5
  59.9 3.6 %collective-permute-start.10 = (f32[2,4,136]{2,1,0:T(4,128)S(1)}, f32[2,4,136]{2,1,0:T(4,128)S(1)}, u32[]{:S(2)}, u32[]{:S(2)}) collective-permute-start(f32[2,4,136]{2,1,0:T(4,128)S(1)} %get-tuple-element.17), channel_id=1, source_target_pairs={{0,1},{1,2},{2,3},{4,5},{5,6},{6,7},{8,9},{9,10},{10,11},{12,13},{... | collective-permute-start | bytes 13064 | tf_op jit(solution)/shard_map/ppermute | solution.py:336
  63.5 2.2 %collective-permute-start.11 = (f32[2,4,136]{2,1,0:T(4,128)S(1)}, f32[2,4,136]{2,1,0:T(4,128)S(1)}, u32[]{:S(2)}, u32[]{:S(2)}) collective-permute-start(f32[2,4,136]{2,1,0:T(4,128)S(1)} %get-tuple-element.18), channel_id=1, source_target_pairs={{1,0},{2,1},{3,2},{5,4},{6,5},{7,6},{9,8},{10,9},{11,10},{13,12},{... | collective-permute-start | bytes 13064 | tf_op jit(solution)/shard_map/ppermute | solution.py:336
  65.8 0.1 broadcast_in_dim.27
  65.9 3.1 %collective-permute-done.11 = f32[2,4,136]{2,1,0:T(4,128)S(1)} collective-permute-done((f32[2,4,136]{2,1,0:T(4,128)S(1)}, f32[2,4,136]{2,1,0:T(4,128)S(1)}, u32[]{:S(2)}, u32[]{:S(2)}) %collective-permute-start.11) | collective-permute-done | bytes 4384 | tf_op jit(solution)/shard_map/ppermute | solution.py:336
  69.0 0.1 select_maximum_fusion
  69.3 0.1 concatenate.23
  69.4 0.1 squeeze.28
  69.6 1.4 copy-done
  71.0 32.2 %scatter.1 = (f32[4096,128]{1,0:T(8,128)}, bf16[512,128]{1,0:T(8,128)(2,1)}, bf16[512,128]{1,0:T(8,128)(2,1)}, bf16[128,128]{1,0:T(8,128)(2,1)}, bf16[128,128]{1,0:T(8,128)(2,1)}, /*index=5*/bf16[4,16,128]{2,1,0:T(8,128)(2,1)}) custom-call(bf16[9216,128]{1,0:T(8,128)(2,1)} %bitcast.26), custom_call_target="tpu_custom_call" | custom-call | flops 16999999488 | bytes 20000000 | tf_op jit(solution)/shard_map/scatter/pallas_call | solution.py:209
  103.1 0.7 slice_bitcast_fusion.4
  103.8 1.9 %collective-permute-start.4 = (bf16[16,128]{1,0:T(8,128)(2,1)S(1)}, bf16[16,128]{1,0:T(8,128)(2,1)S(1)}, u32[]{:S(2)}, u32[]{:S(2)}) collective-permute-start(bf16[16,128]{1,0:T(8,128)(2,1)S(1)} %get-tuple-element.24), channel_id=1, source_target_pairs={{124,1},{125,2},{126,3},{0,5},{1,6},{2,7},{4,9},{5,10},{6,11},{8,1... | collective-permute-start | bytes 12296 | tf_op jit(solution)/shard_map/ppermute | solution.py:336
  105.8 0.1 pad_maximum_fusion
  105.8 0.1 concatenate.21
  105.9 0.1 squeeze.26
  106.0 7.9 %collective-permute-start.7 = (bf16[16,128]{1,0:T(8,128)(2,1)S(1)}, bf16[16,128]{1,0:T(8,128)(2,1)S(1)}, u32[]{:S(2)}, u32[]{:S(2)}) collective-permute-start(bf16[16,128]{1,0:T(8,128)(2,1)S(1)} %get-tuple-element.25), channel_id=1, source_target_pairs={{5,0},{6,1},{7,2},{9,4},{10,5},{11,6},{13,8},{14,9},{15,10},{17,12... | collective-permute-start | bytes 12296 | tf_op jit(solution)/shard_map/ppermute | solution.py:336
  113.9 1.9 %collective-permute-start.6 = (bf16[16,128]{1,0:T(8,128)(2,1)S(1)}, bf16[16,128]{1,0:T(8,128)(2,1)S(1)}, u32[]{:S(2)}, u32[]{:S(2)}) collective-permute-start(bf16[16,128]{1,0:T(8,128)(2,1)S(1)} %get-tuple-element.26), channel_id=1, source_target_pairs={{125,0},{126,1},{127,2},{1,4},{2,5},{3,6},{5,8},{6,9},{7,10},{9,12... | collective-permute-start | bytes 12296 | tf_op jit(solution)/shard_map/ppermute | solution.py:336
  115.8 7.9 %collective-permute-start.5 = (bf16[16,128]{1,0:T(8,128)(2,1)S(1)}, bf16[16,128]{1,0:T(8,128)(2,1)S(1)}, u32[]{:S(2)}, u32[]{:S(2)}) collective-permute-start(bf16[16,128]{1,0:T(8,128)(2,1)S(1)} %get-tuple-element.27), channel_id=1, source_target_pairs={{4,1},{5,2},{6,3},{8,5},{9,6},{10,7},{12,9},{13,10},{14,11},{16,13... | collective-permute-start | bytes 12296 | tf_op jit(solution)/shard_map/ppermute | solution.py:336
  123.7 3.4 %collective-permute-start = (bf16[512,128]{1,0:T(8,128)(2,1)}, bf16[512,128]{1,0:T(8,128)(2,1)S(1)}, u32[]{:S(2)}, u32[]{:S(2)}) collective-permute-start(bf16[512,128]{1,0:T(8,128)(2,1)} %get-tuple-element.12), channel_id=1, source_target_pairs={{0,1},{1,2},{2,3},{4,5},{5,6},{6,7},{8,9},{9,10},{10,11},{12,13},{... | collective-permute-start | bytes 393224 | tf_op jit(solution)/shard_map/ppermute | solution.py:336
  127.1 2.5 %collective-permute-start.1 = (bf16[512,128]{1,0:T(8,128)(2,1)}, bf16[512,128]{1,0:T(8,128)(2,1)S(1)}, u32[]{:S(2)}, u32[]{:S(2)}) collective-permute-start(bf16[512,128]{1,0:T(8,128)(2,1)} %get-tuple-element.13), channel_id=1, source_target_pairs={{1,0},{2,1},{3,2},{5,4},{6,5},{7,6},{9,8},{10,9},{11,10},{13,12},{... | collective-permute-start | bytes 393224 | tf_op jit(solution)/shard_map/ppermute | solution.py:336
  129.7 5.0 %collective-permute-start.3 = (bf16[128,128]{1,0:T(8,128)(2,1)}, bf16[128,128]{1,0:T(8,128)(2,1)S(1)}, u32[]{:S(2)}, u32[]{:S(2)}) collective-permute-start(bf16[128,128]{1,0:T(8,128)(2,1)} %get-tuple-element.15), channel_id=1, source_target_pairs={{4,0},{5,1},{6,2},{7,3},{8,4},{9,5},{10,6},{11,7},{12,8},{13,9},{1... | collective-permute-start | bytes 98312 | tf_op jit(solution)/shard_map/ppermute | solution.py:336
  134.7 0.6 pad_maximum_fusion.2.corner_ref
  135.3 1.2 collective-permute-done.2.west_ref
  136.5 0.1 collective-permute-done.3.east_ref
  136.7 3.5 %broadcast_in_dim.25.face_x = f32[5760,128]{1,0:T(8,128)} broadcast(f32[5760]{0:T(1024)S(1)} %add_multiply_fusion), dimensions={0} | broadcast | bytes 2972160 | tf_op jit(solution)/shard_map/broadcast_in_dim | solution.py:356
  140.2 3.5 %broadcast_in_dim.29.face_y = f32[5760,128]{1,0:T(8,128)} broadcast(f32[5760]{0:T(1024)S(1)} %multiply_select_fusion), dimensions={0} | broadcast | bytes 2972160 | tf_op jit(solution)/shard_map/broadcast_in_dim | solution.py:357
  143.8 15.5 %diffuse.1 = f32[5120,128]{1,0:T(8,128)} custom-call(f32[4096,128]{1,0:T(8,128)} %get-tuple-element.11.field_ref, bf16[512,128]{1,0:T(8,128)(2,1)} %copy-done.2, bf16[512,128]{1,0:T(8,128)(2,1)} %copy-done.3, bf16[128,128]{1,0:T(8,128)(2,1)} %copy-done.4, bf16[128,128]{1,0:T(8,128)(2,1)} %copy-done.5, bf16[4,16,128]{2,1,0:T(8,128)(2,1)} %pad_maximum_fusion.2.corner_ref, ...), custom_call_target="tpu_custom_call" | custom-call | flops 1000000000 | bytes 20000000 | tf_op jit(solution)/shard_map/diffuse/pallas_call | solution.py:315
  (32 shorter events, 0.4 us)
Async XLA Ops:
  18.7 10.3 %copy-start.1 = (f32[2,32,128]{2,1,0:T(8,128)S(1)}, f32[2,32,128]{2,1,0:T(8,128)}, u32[]{:S(2)}) copy-start(f32[2,32,128]{2,1,0:T(8,128)} %param.13) | copy-start | bytes 98308
  18.7 50.8 %all-to-all-start = ((bf16[128,72,128]{2,1,0:T(8,128)(2,1)}), bf16[128,72,128]{2,1,0:T(8,128)(2,1)S(1)}, u32[]{:S(2)}, u32[]{:S(2)}) async-start(bf16[128,72,128]{2,1,0:T(8,128)(2,1)} %bitcast.27), calls=%async_computation | async-start | bytes 4718592 | tf_op jit(solution)/shard_map/all_to_all | solution.py:367
  29.0 30.7 %collective-permute-start.8 = (f32[2,32,4]{2,1,0:T(8,128)S(1)}, f32[2,32,4]{2,1,0:T(8,128)S(1)}, u32[]{:S(2)}, u32[]{:S(2)}) collective-permute-start(f32[2,32,4]{2,1,0:T(8,128)S(1)} %get-tuple-element.22), channel_id=1, source_target_pairs={{124,0},{125,1},{126,2},{127,3},{0,4},{1,5},{2,6},{3,7},{4,8},{5,9... | collective-permute-start | bytes 3080 | tf_op jit(solution)/shard_map/ppermute | solution.py:336
  29.2 30.6 %collective-permute-start.9 = (f32[2,32,4]{2,1,0:T(8,128)S(1)}, f32[2,32,4]{2,1,0:T(8,128)S(1)}, u32[]{:S(2)}, u32[]{:S(2)}) collective-permute-start(f32[2,32,4]{2,1,0:T(8,128)S(1)} %get-tuple-element.23), channel_id=1, source_target_pairs={{4,0},{5,1},{6,2},{7,3},{8,4},{9,5},{10,6},{11,7},{12,8},{13,9},{1... | collective-permute-start | bytes 3080 | tf_op jit(solution)/shard_map/ppermute | solution.py:336
  59.9 6.1 %collective-permute-start.10 = (f32[2,4,136]{2,1,0:T(4,128)S(1)}, f32[2,4,136]{2,1,0:T(4,128)S(1)}, u32[]{:S(2)}, u32[]{:S(2)}) collective-permute-start(f32[2,4,136]{2,1,0:T(4,128)S(1)} %get-tuple-element.17), channel_id=1, source_target_pairs={{0,1},{1,2},{2,3},{4,5},{5,6},{6,7},{8,9},{9,10},{10,11},{12,13},{... | collective-permute-start | bytes 13064 | tf_op jit(solution)/shard_map/ppermute | solution.py:336
  63.5 5.5 %collective-permute-start.11 = (f32[2,4,136]{2,1,0:T(4,128)S(1)}, f32[2,4,136]{2,1,0:T(4,128)S(1)}, u32[]{:S(2)}, u32[]{:S(2)}) collective-permute-start(f32[2,4,136]{2,1,0:T(4,128)S(1)} %get-tuple-element.18), channel_id=1, source_target_pairs={{1,0},{2,1},{3,2},{5,4},{6,5},{7,6},{9,8},{10,9},{11,10},{13,12},{... | collective-permute-start | bytes 13064 | tf_op jit(solution)/shard_map/ppermute | solution.py:336
  69.5 1.4 copy-start
  103.8 23.2 %collective-permute-start.4 = (bf16[16,128]{1,0:T(8,128)(2,1)S(1)}, bf16[16,128]{1,0:T(8,128)(2,1)S(1)}, u32[]{:S(2)}, u32[]{:S(2)}) collective-permute-start(bf16[16,128]{1,0:T(8,128)(2,1)S(1)} %get-tuple-element.24), channel_id=1, source_target_pairs={{124,1},{125,2},{126,3},{0,5},{1,6},{2,7},{4,9},{5,10},{6,11},{8,1... | collective-permute-start | bytes 12296 | tf_op jit(solution)/shard_map/ppermute | solution.py:336
  106.0 23.6 %collective-permute-start.7 = (bf16[16,128]{1,0:T(8,128)(2,1)S(1)}, bf16[16,128]{1,0:T(8,128)(2,1)S(1)}, u32[]{:S(2)}, u32[]{:S(2)}) collective-permute-start(bf16[16,128]{1,0:T(8,128)(2,1)S(1)} %get-tuple-element.25), channel_id=1, source_target_pairs={{5,0},{6,1},{7,2},{9,4},{10,5},{11,6},{13,8},{14,9},{15,10},{17,12... | collective-permute-start | bytes 12296 | tf_op jit(solution)/shard_map/ppermute | solution.py:336
  113.9 15.8 %collective-permute-start.6 = (bf16[16,128]{1,0:T(8,128)(2,1)S(1)}, bf16[16,128]{1,0:T(8,128)(2,1)S(1)}, u32[]{:S(2)}, u32[]{:S(2)}) collective-permute-start(bf16[16,128]{1,0:T(8,128)(2,1)S(1)} %get-tuple-element.26), channel_id=1, source_target_pairs={{125,0},{126,1},{127,2},{1,4},{2,5},{3,6},{5,8},{6,9},{7,10},{9,12... | collective-permute-start | bytes 12296 | tf_op jit(solution)/shard_map/ppermute | solution.py:336
  115.8 18.9 %collective-permute-start.5 = (bf16[16,128]{1,0:T(8,128)(2,1)S(1)}, bf16[16,128]{1,0:T(8,128)(2,1)S(1)}, u32[]{:S(2)}, u32[]{:S(2)}) collective-permute-start(bf16[16,128]{1,0:T(8,128)(2,1)S(1)} %get-tuple-element.27), channel_id=1, source_target_pairs={{4,1},{5,2},{6,3},{8,5},{9,6},{10,7},{12,9},{13,10},{14,11},{16,13... | collective-permute-start | bytes 12296 | tf_op jit(solution)/shard_map/ppermute | solution.py:336
  123.7 13.0 %collective-permute-start = (bf16[512,128]{1,0:T(8,128)(2,1)}, bf16[512,128]{1,0:T(8,128)(2,1)S(1)}, u32[]{:S(2)}, u32[]{:S(2)}) collective-permute-start(bf16[512,128]{1,0:T(8,128)(2,1)} %get-tuple-element.12), channel_id=1, source_target_pairs={{0,1},{1,2},{2,3},{4,5},{5,6},{6,7},{8,9},{9,10},{10,11},{12,13},{... | collective-permute-start | bytes 393224 | tf_op jit(solution)/shard_map/ppermute | solution.py:336
  127.1 9.6 %collective-permute-start.1 = (bf16[512,128]{1,0:T(8,128)(2,1)}, bf16[512,128]{1,0:T(8,128)(2,1)S(1)}, u32[]{:S(2)}, u32[]{:S(2)}) collective-permute-start(bf16[512,128]{1,0:T(8,128)(2,1)} %get-tuple-element.13), channel_id=1, source_target_pairs={{1,0},{2,1},{3,2},{5,4},{6,5},{7,6},{9,8},{10,9},{11,10},{13,12},{... | collective-permute-start | bytes 393224 | tf_op jit(solution)/shard_map/ppermute | solution.py:336
  129.6 6.9 %collective-permute-start.2 = (bf16[128,128]{1,0:T(8,128)(2,1)}, bf16[128,128]{1,0:T(8,128)(2,1)S(1)}, u32[]{:S(2)}, u32[]{:S(2)}) collective-permute-start(bf16[128,128]{1,0:T(8,128)(2,1)} %get-tuple-element.14), channel_id=1, source_target_pairs={{124,0},{125,1},{126,2},{127,3},{0,4},{1,5},{2,6},{3,7},{4,8},{5,9... | collective-permute-start | bytes 98312 | tf_op jit(solution)/shard_map/ppermute | solution.py:336
  129.7 7.0 %collective-permute-start.3 = (bf16[128,128]{1,0:T(8,128)(2,1)}, bf16[128,128]{1,0:T(8,128)(2,1)S(1)}, u32[]{:S(2)}, u32[]{:S(2)}) collective-permute-start(bf16[128,128]{1,0:T(8,128)(2,1)} %get-tuple-element.15), channel_id=1, source_target_pairs={{4,0},{5,1},{6,2},{7,3},{8,4},{9,5},{10,6},{11,7},{12,8},{13,9},{1... | collective-permute-start | bytes 98312 | tf_op jit(solution)/shard_map/ppermute | solution.py:336
  136.5 7.2 %copy-start.4 = (bf16[128,128]{1,0:T(8,128)(2,1)}, bf16[128,128]{1,0:T(8,128)(2,1)S(1)}, u32[]{:S(2)}) copy-start(bf16[128,128]{1,0:T(8,128)(2,1)S(1)} %collective-permute-done.2.west_ref) | copy-start | bytes 98308
  136.6 7.1 %copy-start.5 = (bf16[128,128]{1,0:T(8,128)(2,1)}, bf16[128,128]{1,0:T(8,128)(2,1)S(1)}, u32[]{:S(2)}) copy-start(bf16[128,128]{1,0:T(8,128)(2,1)S(1)} %collective-permute-done.3.east_ref) | copy-start | bytes 98308
  136.6 7.1 %copy-start.2 = (bf16[512,128]{1,0:T(8,128)(2,1)}, bf16[512,128]{1,0:T(8,128)(2,1)S(1)}, u32[]{:S(2)}) copy-start(bf16[512,128]{1,0:T(8,128)(2,1)S(1)} %collective-permute-done.south_ref) | copy-start | bytes 393220
  136.7 7.1 %copy-start.3 = (bf16[512,128]{1,0:T(8,128)(2,1)}, bf16[512,128]{1,0:T(8,128)(2,1)S(1)}, u32[]{:S(2)}) copy-start(bf16[512,128]{1,0:T(8,128)(2,1)S(1)} %collective-permute-done.1.north_ref) | copy-start | bytes 393220

commit v2 on v1

v2 whole, which is shorter than its diff:
```python
import functools

import jax
import jax.numpy as jnp
from jax import lax
from jax.experimental import pallas as pl
from jax.experimental.pallas import tpu as pltpu
from jax.sharding import PartitionSpec as P

STEPS = 4
LANES = 128
META = 8
PAD = 8
F32 = jnp.float32
BF16 = jnp.bfloat16
VMEM_LIMIT = 56 * 1024 * 1024


def iota(shape, dim):
    return lax.broadcasted_iota(jnp.int32, shape, dim)


def pack_kernel(cap, owner_ref, cells_ref, weights_ref, rows_ref, out_ref, xd, xm, yd, ym, slots_v, slots_s, sem):
    groups = owner_ref.shape[0]
    slots = yd.shape[0]
    owner_id = iota((LANES, LANES), 0)
    before = (iota((LANES, 2 * LANES), 0) < iota((LANES, 2 * LANES), 1)).astype(F32).astype(BF16)

    def rank_group(g, base):
        own = owner_ref[pl.ds(g, 1), :]
        hit = (own == owner_id).astype(F32)
        seen = jnp.dot(hit.astype(BF16), before, preferred_element_type=F32)
        rank = jnp.sum(hit * (seen[:, :LANES] + base), axis=0, keepdims=True)
        slots_v[pl.ds(g, 1), :] = own * cap + rank.astype(jnp.int32)
        return base + seen[:, LANES:]

    lax.fori_loop(0, groups, rank_group, jnp.zeros((LANES, LANES), F32), unroll=4)
    copy = pltpu.make_async_copy(slots_v, slots_s, sem)
    copy.start()

    def stage(g, _):
        at = pl.ds(pl.multiple_of(g * LANES, LANES), LANES)
        xd[at, :] = rows_ref[at, :].astype(F32)
        cells = cells_ref[:, at]
        weights = weights_ref[:, at]
        c = [cells[k : k + 1] for k in range(4)]
        w = [weights[k : k + 1] for k in range(4)]
        merged = []
        for k in range(4):
            total = w[k]
            for m in range(k + 1, 4):
                total = total + jnp.where(c[m] == c[k], w[m], 0.0)
            for m in range(k):
                total = jnp.where(c[m] == c[k], 0.0, total)
            merged.append(total)
        row = (cells >> 7).astype(F32)
        col = (cells & 127).astype(F32)
        block = jnp.concatenate([row, col] + merged + [jnp.zeros((LANES - 12, LANES), F32)], axis=0)
        xm[at, :] = block.T
        return 0

    lax.fori_loop(0, groups, stage, 0, unroll=2)

    def clear(g, _):
        at = pl.ds(pl.multiple_of(g * LANES, LANES), LANES)
        yd[at, :] = jnp.zeros((LANES, LANES), F32)
        ym[at, :] = jnp.zeros((LANES, LANES), F32)
        return 0

    lax.fori_loop(0, slots // LANES, clear, 0, unroll=2)
    copy.wait()

    def move(g, _):
        first = pl.multiple_of(g * LANES, LANES)
        for u in range(LANES):
            s = slots_s[g, u]
            yd[pl.ds(s, 1), :] = xd[pl.ds(first + u, 1), :]
            ym[pl.ds(s, 1), :] = xm[pl.ds(first + u, 1), :]
        return 0

    lax.fori_loop(0, groups, move, 0)

    pick = (iota((16, LANES), 0) == iota((16, LANES), 1)).astype(F32).astype(BF16)
    left = iota((META, LANES), 1) < cap
    step = 2 * (cap + META)

    batch = 8

    def emit(c, _):
        first_slot = pl.multiple_of(c * batch * LANES, LANES)
        wide = ym[pl.ds(first_slot, batch * LANES), :].astype(BF16)
        metas = lax.dot_general(pick, wide, (((1,), (1,)), ((), ())), preferred_element_type=F32)
        for u in range(batch):
            data = yd[pl.ds(first_slot + u * LANES, LANES), :]
            low = metas[:META, u * LANES : (u + 1) * LANES]
            high = metas[META:, u * LANES : (u + 1) * LANES]
            first = jnp.where(left, low, pltpu.roll(high, cap, 1))
            second = jnp.where(left, pltpu.roll(low, cap, 1), high)
            block = jnp.concatenate([data[:cap], first, data[cap:], second], axis=0)
            out_ref[pl.ds(pl.multiple_of((c * batch + u) * step, 16), step), :] = block.astype(BF16)
        return 0

    lax.fori_loop(0, slots // LANES // batch, emit, 0)


def pack(owner, cells, weights, rows, devices, cap):
    count = rows.shape[0]
    slots = devices * cap
    full = pl.BlockSpec(memory_space=pltpu.VMEM)
    return pl.pallas_call(
        functools.partial(pack_kernel, cap),
        out_shape=jax.ShapeDtypeStruct((devices * (cap + META), LANES), BF16),
        in_specs=[full] * 4,
        out_specs=full,
        scratch_shapes=[
            pltpu.VMEM((count, LANES), F32),
            pltpu.VMEM((count, LANES), F32),
            pltpu.VMEM((slots, LANES), F32),
            pltpu.VMEM((slots, LANES), F32),
            pltpu.VMEM((count // LANES, LANES), jnp.int32),
            pltpu.SMEM((count // LANES, LANES), jnp.int32),
            pltpu.SemaphoreType.DMA,
        ],
        compiler_params=pltpu.CompilerParams(vmem_limit_bytes=VMEM_LIMIT),
        cost_estimate=pl.CostEstimate(flops=4_000_000_000, bytes_accessed=40_000_000, transcendentals=0),
        name="pack",
    )(owner.reshape(count // LANES, LANES), cells.T, weights.T, rows)


def one_hots(metas, lat_rows, lon_cols):
    both = jnp.concatenate(metas, axis=1)
    depth = both.shape[1]
    col_id = iota((lon_cols, depth), 0).astype(F32)
    row_id = iota((lat_rows, depth), 0).astype(F32)
    col = [(both[4 + k : 5 + k] == col_id).astype(F32) for k in range(4)]
    row = [jnp.where(both[k : k + 1] == row_id, both[8 + k : 9 + k], 0.0) for k in range(4)]
    return col, row


def spread_rows(col, row, which, lon_cols):
    parts = []
    for i in which:
        total = None
        for k in range(4):
            term = jnp.broadcast_to(row[k][i : i + 1], (lon_cols, row[k].shape[1])).astype(BF16) * col[k]
            total = term if total is None else total + term
        parts.append(total)
    return jnp.concatenate(parts, axis=0)


def edge_kernel(
    cap, lat_rows, lon_cols, recv_ref, rates_ref, rows, meta, field_ref, south_ref, north_ref, strip_ref, acc, tmp
):
    slots = rows.shape[0]
    left = iota((META, LANES), 1) < cap
    step = 2 * (cap + META)

    def unpack(b, _):
        block = recv_ref[pl.ds(pl.multiple_of(b * step, 16), step), :].astype(F32)
        data = jnp.concatenate([block[:cap], block[cap + META : 2 * cap + META]], axis=0)
        rows[pl.ds(pl.multiple_of(b * LANES, LANES), LANES), :] = data.astype(BF16)
        first, second = block[cap : cap + META], block[2 * cap + META :]
        meta[b] = jnp.concatenate(
            [
                jnp.where(left, first, pltpu.roll(second, cap, 1)),
                jnp.where(left, pltpu.roll(first, cap, 1), second),
            ],
            axis=0,
        )
        return 0

    lax.fori_loop(0, slots // LANES, unpack, 0, unroll=4)
    field_ref[...] = jnp.zeros_like(field_ref)
    acc[...] = jnp.zeros_like(acc)
    depth = 2 * LANES
    outer = list(range(STEPS)) + list(range(lat_rows - STEPS, lat_rows))
    sides = list(range(STEPS)) + list(range(lon_cols - STEPS, lon_cols))

    def accumulate(t, _):
        data = rows[pl.ds(pl.multiple_of(t * depth, depth), depth), :]
        col, row = one_hots([meta[2 * t], meta[2 * t + 1]], lat_rows, lon_cols)
        colb = [c.astype(BF16) for c in col]
        rowb = [r.astype(BF16) for r in row]
        field_ref[...] += jnp.dot(spread_rows(colb, row, outer, lon_cols), data, preferred_element_type=F32)
        parts = []
        for j in sides:
            total = None
            for k in range(4):
                term = jnp.broadcast_to(col[k][j : j + 1], (lat_rows, depth)).astype(BF16) * rowb[k]
                total = term if total is None else total + term
            parts.append(total)
        acc[...] += jnp.dot(jnp.concatenate(parts, axis=0), data, preferred_element_type=F32)
        return 0

    lax.fori_loop(0, slots // depth, accumulate, 0)
    wide = STEPS * lon_cols
    strip_ref[...] = acc[...].astype(BF16)
    tmp[...] = jnp.zeros_like(tmp)
    for ref, first, at in ((south_ref, 0, 0), (north_ref, wide, lat_rows - STEPS)):
        tmp[0:STEPS, :] = rates_ref[at : at + STEPS, :]
        tmp[STEPS : 2 * STEPS, :] = rates_ref[lat_rows + at : lat_rows + at + STEPS, :]
        ref[:wide, :] = field_ref[first : first + wide, :].astype(BF16)
        ref[wide:, :] = tmp[...].astype(BF16)


def scatter_edges(recv, rates, devices, cap, lat_rows, lon_cols):
    slots = devices * cap
    full = pl.BlockSpec(memory_space=pltpu.VMEM)
    wide = STEPS * lon_cols
    shapes = [
        jax.ShapeDtypeStruct((slots, LANES), BF16),
        jax.ShapeDtypeStruct((slots // LANES, 16, LANES), F32),
        jax.ShapeDtypeStruct((2 * wide, LANES), F32),
        jax.ShapeDtypeStruct((wide + 16, LANES), BF16),
        jax.ShapeDtypeStruct((wide + 16, LANES), BF16),
        jax.ShapeDtypeStruct((2 * STEPS * lat_rows, LANES), BF16),
    ]
    return pl.pallas_call(
        functools.partial(edge_kernel, cap, lat_rows, lon_cols),
        out_shape=shapes,
        in_specs=[full] * 2,
        out_specs=[full] * len(shapes),
        scratch_shapes=[pltpu.VMEM((2 * STEPS * lat_rows, LANES), F32), pltpu.VMEM((16, LANES), F32)],
        compiler_params=pltpu.CompilerParams(vmem_limit_bytes=VMEM_LIMIT),
        cost_estimate=pl.CostEstimate(flops=5_000_000_000, bytes_accessed=20_000_000, transcendentals=0),
        name="scatter_edges",
    )(recv, rates)


def middle_kernel(first, last, lat_rows, lon_cols, rows_ref, meta_ref, field_ref):
    field_ref[...] = jnp.zeros_like(field_ref)
    depth = 2 * LANES
    per = 6

    def accumulate(t, _):
        data = rows_ref[pl.ds(pl.multiple_of(t * depth, depth), depth), :]
        col, row = one_hots([meta_ref[2 * t], meta_ref[2 * t + 1]], lat_rows, lon_cols)
        colb = [c.astype(BF16) for c in col]
        for i in range(first, last, per):
            spread = spread_rows(colb, row, range(i, i + per), lon_cols)
            at = pl.ds((i - first) * lon_cols, per * lon_cols)
            field_ref[at, :] += jnp.dot(spread, data, preferred_element_type=F32)
        return 0

    lax.fori_loop(0, rows_ref.shape[0] // depth, accumulate, 0)


def scatter_middle(rows, meta, first, last, lat_rows, lon_cols):
    full = pl.BlockSpec(memory_space=pltpu.VMEM)
    return pl.pallas_call(
        functools.partial(middle_kernel, first, last, lat_rows, lon_cols),
        out_shape=jax.ShapeDtypeStruct(((last - first) * lon_cols, LANES), F32),
        in_specs=[full] * 2,
        out_specs=full,
        compiler_params=pltpu.CompilerParams(vmem_limit_bytes=VMEM_LIMIT),
        cost_estimate=pl.CostEstimate(flops=7_000_000_000, bytes_accessed=20_000_000, transcendentals=0),
        name="scatter_middle",
    )(rows, meta)


def turn_kernel(lat_rows, lon_cols, below_ref, above_ref, strip_ref, rates_ref, west_ref, east_ref, tall_ref, cols):
    tall = lat_rows + 2 * STEPS
    wide = STEPS * lon_cols
    below = below_ref[...].astype(F32)
    above = above_ref[...].astype(F32)
    strip = strip_ref[...].astype(F32)
    for c in range(2):
        at = c * tall
        tall_ref[at : at + STEPS, :] = below[wide + c * STEPS : wide + (c + 1) * STEPS]
        tall_ref[at + STEPS : at + STEPS + lat_rows, :] = rates_ref[c * lat_rows : (c + 1) * lat_rows, :]
        tall_ref[at + STEPS + lat_rows : at + tall, :] = above[wide + c * STEPS : wide + (c + 1) * STEPS]
    for side, ref in ((0, west_ref), (1, east_ref)):
        base = side * (lon_cols - STEPS)
        for j in range(STEPS):
            n = (side * STEPS + j) * lat_rows
            cols[pl.ds(STEPS * STEPS + j, lat_rows, stride=STEPS), :] = strip[n : n + lat_rows]
        for i in range(STEPS):
            cols[pl.ds(STEPS * i, STEPS), :] = below[i * lon_cols + base : i * lon_cols + base + STEPS]
            n = STEPS * (STEPS + lat_rows + i)
            cols[pl.ds(n, STEPS), :] = above[i * lon_cols + base : i * lon_cols + base + STEPS]
        ref[: STEPS * tall, :] = cols[...].astype(BF16)
        ref[STEPS * tall :, :] = tall_ref[...].astype(BF16)


def turn(below, above, strip, rates, lat_rows, lon_cols):
    full = pl.BlockSpec(memory_space=pltpu.VMEM)
    tall = lat_rows + 2 * STEPS
    side = jax.ShapeDtypeStruct(((STEPS + 2) * tall, LANES), BF16)
    return pl.pallas_call(
        functools.partial(turn_kernel, lat_rows, lon_cols),
        out_shape=[side, side, jax.ShapeDtypeStruct((2 * tall, LANES), F32)],
        in_specs=[full] * 4,
        out_specs=[full] * 3,
        scratch_shapes=[pltpu.VMEM((STEPS * tall, LANES), F32)],
        compiler_params=pltpu.CompilerParams(vmem_limit_bytes=VMEM_LIMIT),
        cost_estimate=pl.CostEstimate(flops=1_000_000, bytes_accessed=1_000_000, transcendentals=0),
        name="turn",
    )(below, above, strip, rates)


def diffuse_kernel(
    lat_rows,
    lon_cols,
    lat_devices,
    place_ref,
    outer_ref,
    mid1_ref,
    mid2_ref,
    below_ref,
    above_ref,
    west_ref,
    east_ref,
    rates_ref,
    gain_ref,
    jac_ref,
    out_ref,
    ping,
    pong,
    face_x,
    face_y,
    kappa,
):
    width = lon_cols + 2 * PAD
    tall = lat_rows + 2 * STEPS
    lead = PAD - STEPS
    trail = PAD + lon_cols
    half = (lat_rows - 2 * STEPS) // 2
    west = west_ref[...].astype(F32)
    east = east_ref[...].astype(F32)

    rest = jnp.zeros((LANES - tall, LANES), F32)
    for c in range(2):
        at = STEPS * tall + c * tall
        kappa[c, 0:lead, :] = jnp.zeros((lead, LANES), F32)
        kappa[c, lead:PAD, :] = jnp.concatenate([west[at : at + tall], rest], axis=0).T[LANES - STEPS :]
        kappa[c, PAD:trail, :] = jnp.concatenate([rates_ref[c * tall : (c + 1) * tall, :], rest], axis=0).T
        kappa[c, trail : trail + STEPS, :] = jnp.concatenate([east[at : at + tall], rest], axis=0).T[:STEPS]
        kappa[c, trail + STEPS :, :] = jnp.zeros((lead, LANES), F32)
    kx, ky = kappa[0], kappa[1]
    ex = 0.5 * (kx + pltpu.roll(kx, width - 1, 0))
    row = place_ref[0] * lat_rows - STEPS + iota((width, LANES), 1)
    inside = (row >= 0) & (row < lat_rows * lat_devices - 1)
    ny = jnp.where(inside, 0.5 * (ky + pltpu.roll(ky, LANES - 1, 1)), 0.0)
    for i in range(tall):
        at = pl.ds(i * width, width)
        face_x[at, :] = jnp.broadcast_to(ex[:, i : i + 1], (width, LANES))
        face_y[at, :] = jnp.broadcast_to(ny[:, i : i + 1], (width, LANES))

    for i in range(tall):
        n = i - STEPS
        if n < 0:
            middle = below_ref[pl.ds(i * lon_cols, lon_cols), :].astype(F32)
        elif n < STEPS:
            middle = outer_ref[pl.ds(n * lon_cols, lon_cols), :]
        elif n < STEPS + half:
            middle = mid1_ref[pl.ds((n - STEPS) * lon_cols, lon_cols), :]
        elif n < STEPS + 2 * half:
            middle = mid2_ref[pl.ds((n - STEPS - half) * lon_cols, lon_cols), :]
        elif n < lat_rows:
            middle = outer_ref[pl.ds((n - 2 * half) * lon_cols, lon_cols), :]
        else:
            middle = above_ref[pl.ds((n - lat_rows) * lon_cols, lon_cols), :].astype(F32)
        ping[pl.ds(i * width, PAD), :] = jnp.zeros((PAD, LANES), F32)
        ping[pl.ds(i * width + trail, PAD), :] = jnp.zeros((PAD, LANES), F32)
        ping[pl.ds(i * width + PAD, lon_cols), :] = middle
        ping[pl.ds(i * width + lead, STEPS), :] = west[STEPS * i : STEPS * i + STEPS]
        ping[pl.ds(i * width + trail, STEPS), :] = east[STEPS * i : STEPS * i + STEPS]

    def row_at(i):
        return pl.ds(pl.multiple_of(i * width, 8), width)

    for sweep in range(STEPS):
        old, new = (ping, pong) if sweep % 2 == 0 else (pong, ping)
        low, high = sweep + 1, tall - sweep - 1

        def one_row(i, carry, old=old, new=new):
            here, flux_below = carry
            above = old[row_at(i + 1), :]
            flux_y = face_y[row_at(i), :] * (above - here)
            flux_x = face_x[row_at(i), :] * (pltpu.roll(here, width - 1, 0) - here)
            new[row_at(i), :] = here + flux_x - pltpu.roll(flux_x, 1, 0) + flux_y - flux_below
            return above, flux_y

        here = old[row_at(low), :]
        start = face_y[row_at(low - 1), :] * (here - old[row_at(low - 1), :])
        lax.fori_loop(low, high, one_row, (here, start))

    last = ping if STEPS % 2 == 0 else pong
    gain = gain_ref[...]
    jac = jnp.concatenate([jac_ref[...], jac_ref[...]], axis=1)
    levels = jac_ref.shape[0]

    def project(h, _):
        pair = []
        for u in range(2):
            at = pl.multiple_of((2 * h + u + STEPS) * width + PAD, 8)
            value = last[pl.ds(at, lon_cols), :] * gain
            head = value.astype(BF16)
            low = (value - head.astype(F32)).astype(BF16)
            pair.append(jnp.concatenate([head, low], axis=1))
        both = jnp.concatenate(pair, axis=0)
        result = lax.dot_general(jac, both, (((1,), (1,)), ((), ())), preferred_element_type=F32)
        out_ref[pl.ds(2 * h, levels, stride=lat_rows), :] = result[:, :lon_cols]
        out_ref[pl.ds(2 * h + 1, levels, stride=lat_rows), :] = result[:, lon_cols:]
        return 0

    lax.fori_loop(0, lat_rows // 2, project, 0)


def diffuse(place, outer, mid1, mid2, below, above, west, east, rates, inv_var, jacobian, lat_rows, lon_cols, lats):
    full = pl.BlockSpec(memory_space=pltpu.VMEM)
    levels = jacobian.shape[1]
    tall, width = lat_rows + 2 * STEPS, lon_cols + 2 * PAD
    out = pl.pallas_call(
        functools.partial(diffuse_kernel, lat_rows, lon_cols, lats),
        out_shape=jax.ShapeDtypeStruct((levels * lat_rows, lon_cols), F32),
        in_specs=[pl.BlockSpec(memory_space=pltpu.SMEM)] + [full] * 10,
        out_specs=full,
        scratch_shapes=[pltpu.VMEM((tall * width, LANES), F32)] * 4 + [pltpu.VMEM((2, width, LANES), F32)],
        compiler_params=pltpu.CompilerParams(vmem_limit_bytes=VMEM_LIMIT),
        cost_estimate=pl.CostEstimate(flops=1_000_000_000, bytes_accessed=20_000_000, transcendentals=0),
        name="diffuse",
    )(place, outer, mid1, mid2, below, above, west, east, rates, inv_var.reshape(1, -1), jacobian.T)
    return out.reshape(levels, lat_rows, lon_cols)


def moved(value, axis, step, wrap):
    size = lax.axis_size(axis)
    pairs = [((i + step) % size, i) for i in range(size) if wrap or 0 <= i + step < size]
    return lax.ppermute(value, axis, pairs)


def local(departures, obs_owner, obs_cells, interp_weights, inv_var, jacobian, face_rates):
    devices = lax.axis_size(("lon", "lat"))
    cap = 2 * departures.shape[0] // devices
    lat_rows, lon_cols = face_rates.shape[1:]
    rates = face_rates.reshape(2 * lat_rows, lon_cols)
    send = pack(obs_owner, obs_cells, interp_weights, departures, devices, cap)
    recv = lax.all_to_all(
        send.reshape(devices, cap + META, LANES), ("lon", "lat"), split_axis=0, concat_axis=0, tiled=True
    ).reshape(devices * (cap + META), LANES)
    rows, meta, outer, south, north, strip = scatter_edges(recv, rates, devices, cap, lat_rows, lon_cols)
    below = moved(north, "lat", -1, False)
    above = moved(south, "lat", 1, False)
    middle = lat_rows // 2
    mid1 = scatter_middle(rows, meta, STEPS, middle, lat_rows, lon_cols)
    meta, below, above = lax.optimization_barrier((meta, below, above))
    to_west, to_east, tall_rates = turn(below, above, strip, rates, lat_rows, lon_cols)
    west = moved(to_east, "lon", -1, True)
    east = moved(to_west, "lon", 1, True)
    mid2 = scatter_middle(rows, meta, middle, lat_rows - STEPS, lat_rows, lon_cols)
    place = lax.axis_index("lat").astype(jnp.int32).reshape(1)
    return diffuse(
        place,
        outer,
        mid1,
        mid2,
        below,
        above,
        west,
        east,
        tall_rates,
        inv_var,
        jacobian,
        lat_rows,
        lon_cols,
        lax.axis_size("lat"),
    )


def solution(mesh):
    in_specs = (
        P(("lon", "lat"), None),
        P(("lon", "lat"), None),
        P(("lon", "lat"), None),
        P(("lon", "lat"), None),
        P(),
        P(),
        P(None, "lat", "lon"),
    )
    out_specs = P(None, "lat", "lon")
    return jax.shard_map(local, mesh=mesh, in_specs=in_specs, out_specs=out_specs, check_vma=False)
```

time: 160 us -> 136 us (0.85)
  starting transfers between devices: 51.7 us -> 21.1 us
  Pallas kernels: 66.4 us -> 79.3 us
  local copies, waits for them, and re-layouts: 9.89 us -> 2.75 us
  waiting for transfers between devices: 30.1 us -> 32.7 us
    all_to_all x1, waiting for transfers between devices: 0.01 us -> 32.7 us  [local(): lax.all_to_all(send.reshape(devices, cap + META, LANES), ('lon', 'lat'),...]
    ppermute x12 -> x4, starting transfers between devices: 41.4 us -> 10.9 us  [moved(): return lax.ppermute(value, axis, pairs)]
    ppermute x12 -> x4, waiting for transfers between devices: 30.1 us -> 0.01 us  [moved(): return lax.ppermute(value, axis, pairs)]
    pallas_call x2 -> x5, Pallas kernels: 47.7 us -> 65.7 us  [the longest x2 31.6 us: scatter_middle(): pl.pallas_call(functools.partial(middle_kernel, first, last, lat_rows, lo...]
    broadcast_in_dim x4 -> x0, local copies, waits for them, and re-layouts: 7.25 us -> none  [the longest x1 3.54 us: faces(): jnp.broadcast_to(face_x.reshape(-1, 1), shape)]
    pallas_call x1, Pallas kernels: 18.7 us -> 13.6 us  [pack(): pl.pallas_call(functools.partial(pack_kernel, cap), out_shape=jax.ShapeDt...]
  transfers between devices with their start and end apart: 13 -> 5, of which waited for: 4 -> 1; matrix products, arithmetic and copies ran while one was open for 1% -> 0% of each run, Pallas kernels for 0% -> 23%
where the time goes in v2:
time: 136 us
  Pallas kernels  79.3 us (58%)
  waiting for transfers between devices  32.7 us (24%)
  starting transfers between devices  21.1 us (16%)
  local copies, waits for them, and re-layouts  2.75 us (2%)
    all_to_all x1, waiting for transfers between devices, local(): lax.all_to_all(send.reshape(devices, cap + META, LANES), ('lon', 'lat'),...  32.7 us
    pallas_call x2, Pallas kernels, scatter_middle(): pl.pallas_call(functools.partial(middle_kernel, first, last, lat_rows, lo...  31.6 us
    pallas_call x1, Pallas kernels, scatter_edges(): pl.pallas_call(functools.partial(edge_kernel, cap, lat_rows, lon_cols), o...  17 us
    pallas_call x1, Pallas kernels, diffuse(): pl.pallas_call(functools.partial(diffuse_kernel, lat_rows, lon_cols, lats...  15.4 us
    pallas_call x1, Pallas kernels, pack(): pl.pallas_call(functools.partial(pack_kernel, cap), out_shape=jax.ShapeDt...  13.6 us
    ppermute x4, starting transfers between devices, moved(): return lax.ppermute(value, axis, pairs)  10.9 us
    all_to_all x1, starting transfers between devices, local(): lax.all_to_all(send.reshape(devices, cap + META, LANES), ('lon', 'lat'),...  10.2 us
    unnamed x10, local copies, waits for them, and re-layouts  2.75 us
  transfers between devices with their start and end apart: 5, of which 1 were waited for; matrix products, arithmetic and copies ran while one was open for 0% of the time, Pallas kernels for 23%

profile of v2, /device:TPU:32, one launch (start us, length us, event | category | flops | bytes accessed | tf_op | source)
XLA Modules:
  0.0 136.0 jit_solution(2426856238653388009)
XLA Ops:
  0.0 13.6 %pack.1 = bf16[9216,128]{1,0:T(8,128)(2,1)} custom-call(s32[32,128]{1,0:T(8,128)} %bitcast.18, s32[4,4096]{1,0:T(4,128)} %bitcast.16, f32[4,4096]{1,0:T(4,128)} %bitcast.17, bf16[4096,128]{1,0:T(8,128)(2,1)} %rows_ref.1), custom_call_target="tpu_custom_call" | custom-call | flops 4000000000 | bytes 40000000 | tf_op jit(solution)/shard_map/pack/pallas_call | solution.py:110
  13.6 10.2 %all-to-all-start = ((bf16[128,72,128]{2,1,0:T(8,128)(2,1)}), bf16[128,72,128]{2,1,0:T(8,128)(2,1)S(1)}, u32[]{:S(2)}, u32[]{:S(2)}) async-start(bf16[128,72,128]{2,1,0:T(8,128)(2,1)} %bitcast.11), calls=%async_computation | async-start | bytes 4718592 | tf_op jit(solution)/shard_map/all_to_all | solution.py:439
  23.9 32.7 %all-to-all-done = bf16[128,72,128]{2,1,0:T(8,128)(2,1)S(1)} async-done(((bf16[128,72,128]{2,1,0:T(8,128)(2,1)}), bf16[128,72,128]{2,1,0:T(8,128)(2,1)S(1)}, u32[]{:S(2)}, u32[]{:S(2)}) %all-to-all-start) | async-done | bytes 2359328 | tf_op jit(solution)/shard_map/all_to_all | solution.py:439
  56.6 0.0 copy-start
  56.6 1.4 %copy-done = bf16[128,72,128]{2,1,0:T(8,128)(2,1)} copy-done((bf16[128,72,128]{2,1,0:T(8,128)(2,1)}, bf16[128,72,128]{2,1,0:T(8,128)(2,1)S(1)}, u32[]{:S(2)}) %copy-start) | copy-done | bytes 2359320
  58.0 17.0 %scatter_edges.1 = (bf16[8192,128]{1,0:T(8,128)(2,1)}, f32[64,16,128]{2,1,0:T(8,128)}, f32[1024,128]{1,0:T(8,128)}, bf16[528,128]{1,0:T(8,128)(2,1)}, bf16[528,1...) custom-call(bf16[9216,128]{1,0:T(8,128)(2,1)} %bitcast.10, f32[64,128]{1,0:T(8,128)} %bitcast.13), custom_call_target="tpu_custom_call" | custom-call | flops 5000000000 | bytes 20000000 | tf_op jit(solution)/shard_map/scatter_edges/pallas_call | solution.py:218
  75.0 1.9 %collective-permute-start = (bf16[528,128]{1,0:T(8,128)(2,1)}, bf16[528,128]{1,0:T(8,128)(2,1)S(1)}, u32[]{:S(2)}, u32[]{:S(2)}) collective-permute-start(bf16[528,128]{1,0:T(8,128)(2,1)} %get-tuple-element.20), channel_id=1, source_target_pairs={{0,1},{1,2},{2,3},{4,5},{5,6},{6,7},{8,9},{9,10},{10,11},{12,13},{... | collective-permute-start | bytes 405512 | tf_op jit(solution)/shard_map/ppermute | solution.py:430
  76.9 3.9 %collective-permute-start.1 = (bf16[528,128]{1,0:T(8,128)(2,1)}, bf16[528,128]{1,0:T(8,128)(2,1)S(1)}, u32[]{:S(2)}, u32[]{:S(2)}) collective-permute-start(bf16[528,128]{1,0:T(8,128)(2,1)} %get-tuple-element.21), channel_id=1, source_target_pairs={{1,0},{2,1},{3,2},{5,4},{6,5},{7,6},{9,8},{10,9},{11,10},{13,12},{... | collective-permute-start | bytes 405512 | tf_op jit(solution)/shard_map/ppermute | solution.py:430
  80.9 15.8 %scatter_middle.2.mid1_ref = f32[1536,128]{1,0:T(8,128)} custom-call(bf16[8192,128]{1,0:T(8,128)(2,1)} %get-tuple-element.18.rows_ref, f32[64,16,128]{2,1,0:T(8,128)} %get-tuple-element.22.meta_ref), custom_call_target="tpu_custom_call" | custom-call | flops 7000000000 | bytes 20000000 | tf_op jit(solution)/shard_map/scatter_middle/pallas_call | solution.py:250
  96.7 0.0 collective-permute-done.below_ref
  96.7 0.0 copy-start.1
  96.7 0.0 collective-permute-done.1.above_ref
  96.7 0.0 copy-start.2
  96.7 0.6 copy-done.1
  97.4 0.1 copy-done.2
  97.4 1.7 %turn.1 = (bf16[240,128]{1,0:T(8,128)(2,1)}, bf16[240,128]{1,0:T(8,128)(2,1)}, f32[80,128]{1,0:T(8,128)}) custom-call(bf16[528,128]{1,0:T(8,128)(2,1)} %copy-done.1, bf16[528,128]{1,0:T(8,128)(2,1)} %copy-done.2, bf16[256,128]{1,0:T(8,128)(2,1)} %get-tuple-element.25.strip_ref, f32[64,128]{1,0:T(8,128)} %bitcast.14), custom_call_target="tpu_custom_call" | custom-call | flops 1000000 | bytes 1000000 | tf_op jit(solution)/shard_map/turn/pallas_call | solution.py:289
  99.1 0.0 collective-permute-start.2
  99.1 5.1 %collective-permute-start.3 = (bf16[240,128]{1,0:T(8,128)(2,1)}, bf16[240,128]{1,0:T(8,128)(2,1)S(1)}, u32[]{:S(2)}, u32[]{:S(2)}) collective-permute-start(bf16[240,128]{1,0:T(8,128)(2,1)} %get-tuple-element.27), channel_id=1, source_target_pairs={{4,0},{8,4},{12,8},{16,12},{20,16},{24,20},{28,24},{32,28},{36,32}... | collective-permute-start | bytes 184328 | tf_op jit(solution)/shard_map/ppermute | solution.py:430
  104.2 15.8 %scatter_middle.3.mid2_ref = f32[1536,128]{1,0:T(8,128)} custom-call(bf16[8192,128]{1,0:T(8,128)(2,1)} %get-tuple-element.18.rows_ref, f32[64,16,128]{2,1,0:T(8,128)} %get-tuple-element.22.meta_ref), custom_call_target="tpu_custom_call" | custom-call | flops 7000000000 | bytes 20000000 | tf_op jit(solution)/shard_map/scatter_middle/pallas_call | solution.py:250
  119.9 0.0 collective-permute-done.2.west_ref
  119.9 0.0 copy-start.3
  119.9 0.0 collective-permute-done.3.east_ref
  119.9 0.0 copy-start.4
  120.0 0.6 copy-done.3
  120.6 0.0 copy-done.4
  120.6 15.4 %diffuse.1 = f32[5120,128]{1,0:T(8,128)} custom-call(s32[1]{0:T(128)} %bitcast.place_ref, f32[1024,128]{1,0:T(8,128)} %get-tuple-element.17.outer_ref, f32[1536,128]{1,0:T(8,128)} %scatter_middle.2.mid1_ref, f32[1536,128]{1,0:T(8,128)} %scatter_middle.3.mid2_ref, bf16[528,128]{1,0:T(8,128)(2,1)} %copy-done.1, bf16[528,128]{1,0:T(8,128)(2,1)} %copy-done.2, ...), custom_call_target="tpu_custom_call" | custom-call | flops 1000000000 | bytes 20000000 | tf_op jit(solution)/shard_map/diffuse/pallas_call | solution.py:414
Async XLA Ops:
  13.6 43.0 %all-to-all-start = ((bf16[128,72,128]{2,1,0:T(8,128)(2,1)}), bf16[128,72,128]{2,1,0:T(8,128)(2,1)S(1)}, u32[]{:S(2)}, u32[]{:S(2)}) async-start(bf16[128,72,128]{2,1,0:T(8,128)(2,1)} %bitcast.11), calls=%async_computation | async-start | bytes 4718592 | tf_op jit(solution)/shard_map/all_to_all | solution.py:439
  56.6 1.4 %copy-start = (bf16[128,72,128]{2,1,0:T(8,128)(2,1)}, bf16[128,72,128]{2,1,0:T(8,128)(2,1)S(1)}, u32[]{:S(2)}) copy-start(bf16[128,72,128]{2,1,0:T(8,128)(2,1)S(1)} %all-to-all-done) | copy-start | bytes 7077892
  75.0 21.7 %collective-permute-start = (bf16[528,128]{1,0:T(8,128)(2,1)}, bf16[528,128]{1,0:T(8,128)(2,1)S(1)}, u32[]{:S(2)}, u32[]{:S(2)}) collective-permute-start(bf16[528,128]{1,0:T(8,128)(2,1)} %get-tuple-element.20), channel_id=1, source_target_pairs={{0,1},{1,2},{2,3},{4,5},{5,6},{6,7},{8,9},{9,10},{10,11},{12,13},{... | collective-permute-start | bytes 405512 | tf_op jit(solution)/shard_map/ppermute | solution.py:430
  76.9 19.8 %collective-permute-start.1 = (bf16[528,128]{1,0:T(8,128)(2,1)}, bf16[528,128]{1,0:T(8,128)(2,1)S(1)}, u32[]{:S(2)}, u32[]{:S(2)}) collective-permute-start(bf16[528,128]{1,0:T(8,128)(2,1)} %get-tuple-element.21), channel_id=1, source_target_pairs={{1,0},{2,1},{3,2},{5,4},{6,5},{7,6},{9,8},{10,9},{11,10},{13,12},{... | collective-permute-start | bytes 405512 | tf_op jit(solution)/shard_map/ppermute | solution.py:430
  96.7 0.7 copy-start.1
  96.7 0.7 copy-start.2
  99.1 20.8 %collective-permute-start.2 = (bf16[240,128]{1,0:T(8,128)(2,1)}, bf16[240,128]{1,0:T(8,128)(2,1)S(1)}, u32[]{:S(2)}, u32[]{:S(2)}) collective-permute-start(bf16[240,128]{1,0:T(8,128)(2,1)} %get-tuple-element.26), channel_id=1, source_target_pairs={{124,0},{0,4},{4,8},{8,12},{12,16},{16,20},{20,24},{24,28},{28,32}... | collective-permute-start | bytes 184328 | tf_op jit(solution)/shard_map/ppermute | solution.py:430
  99.1 20.8 %collective-permute-start.3 = (bf16[240,128]{1,0:T(8,128)(2,1)}, bf16[240,128]{1,0:T(8,128)(2,1)S(1)}, u32[]{:S(2)}, u32[]{:S(2)}) collective-permute-start(bf16[240,128]{1,0:T(8,128)(2,1)} %get-tuple-element.27), channel_id=1, source_target_pairs={{4,0},{8,4},{12,8},{16,12},{20,16},{24,20},{28,24},{32,28},{36,32}... | collective-permute-start | bytes 184328 | tf_op jit(solution)/shard_map/ppermute | solution.py:430
  119.9 0.6 copy-start.3
  119.9 0.6 copy-start.4

commit v3 on v2

--- a/solution.py
+++ b/solution.py
@@ -11,9 +11,13 @@
 LANES = 128
 META = 8
 PAD = 8
+GROUPS = 8
+TILES = 4
+UNROLL_SWEEP = 1
+UNROLL_PROJECT = 2
 F32 = jnp.float32
 BF16 = jnp.bfloat16
-VMEM_LIMIT = 56 * 1024 * 1024
+MIB = 1024 * 1024
 
 
 def iota(shape, dim):
@@ -121,20 +125,29 @@
             pltpu.SMEM((count // LANES, LANES), jnp.int32),
             pltpu.SemaphoreType.DMA,
         ],
-        compiler_params=pltpu.CompilerParams(vmem_limit_bytes=VMEM_LIMIT),
+        compiler_params=pltpu.CompilerParams(vmem_limit_bytes=20 * MIB),
         cost_estimate=pl.CostEstimate(flops=4_000_000_000, bytes_accessed=40_000_000, transcendentals=0),
         name="pack",
     )(owner.reshape(count // LANES, LANES), cells.T, weights.T, rows)
 
 
+def column_of(lon_cols, dim_rows):
+    p = iota(dim_rows, 0)
+    return (p % GROUPS) * (lon_cols // GROUPS) + p // GROUPS
+
+
 def one_hots(metas, lat_rows, lon_cols):
     both = jnp.concatenate(metas, axis=1)
     depth = both.shape[1]
-    col_id = iota((lon_cols, depth), 0).astype(F32)
+    col_id = column_of(lon_cols, (lon_cols, depth)).astype(F32).astype(BF16)
     row_id = iota((lat_rows, depth), 0).astype(F32)
-    col = [(both[4 + k : 5 + k] == col_id).astype(F32) for k in range(4)]
-    row = [jnp.where(both[k : k + 1] == row_id, both[8 + k : 9 + k], 0.0) for k in range(4)]
-    return col, row
+    col, row = [], []
+    for k in range(4):
+        apart = jnp.broadcast_to(both[4 + k : 5 + k], (16, depth)).astype(BF16)
+        apart = jnp.concatenate([apart] * (lon_cols // 16), axis=0) - col_id
+        col.append(jnp.maximum(1.0 - apart * apart, 0.0).astype(BF16))
+        row.append(jnp.where(both[k : k + 1] == row_id, both[8 + k : 9 + k], 0.0))
+    return both, col, row
 
 
 def spread_rows(col, row, which, lon_cols):
@@ -172,21 +185,21 @@
     lax.fori_loop(0, slots // LANES, unpack, 0, unroll=4)
     field_ref[...] = jnp.zeros_like(field_ref)
     acc[...] = jnp.zeros_like(acc)
-    depth = 2 * LANES
+    depth = TILES * LANES
     outer = list(range(STEPS)) + list(range(lat_rows - STEPS, lat_rows))
     sides = list(range(STEPS)) + list(range(lon_cols - STEPS, lon_cols))
 
     def accumulate(t, _):
         data = rows[pl.ds(pl.multiple_of(t * depth, depth), depth), :]
-        col, row = one_hots([meta[2 * t], meta[2 * t + 1]], lat_rows, lon_cols)
-        colb = [c.astype(BF16) for c in col]
+        both, col, row = one_hots([meta[TILES * t + h] for h in range(TILES)], lat_rows, lon_cols)
         rowb = [r.astype(BF16) for r in row]
-        field_ref[...] += jnp.dot(spread_rows(colb, row, outer, lon_cols), data, preferred_element_type=F32)
+        field_ref[...] += jnp.dot(spread_rows(col, row, outer, lon_cols), data, preferred_element_type=F32)
         parts = []
         for j in sides:
             total = None
             for k in range(4):
-                term = jnp.broadcast_to(col[k][j : j + 1], (lat_rows, depth)).astype(BF16) * rowb[k]
+                same = jnp.where(both[4 + k : 5 + k] == float(j), 1.0, 0.0)
+                term = jnp.broadcast_to(same, (lat_rows, depth)).astype(BF16) * rowb[k]
                 total = term if total is None else total + term
             parts.append(total)
         acc[...] += jnp.dot(jnp.concatenate(parts, axis=0), data, preferred_element_type=F32)
@@ -221,7 +234,7 @@
         in_specs=[full] * 2,
         out_specs=[full] * len(shapes),
         scratch_shapes=[pltpu.VMEM((2 * STEPS * lat_rows, LANES), F32), pltpu.VMEM((16, LANES), F32)],
-        compiler_params=pltpu.CompilerParams(vmem_limit_bytes=VMEM_LIMIT),
+        compiler_params=pltpu.CompilerParams(vmem_limit_bytes=14 * MIB),
         cost_estimate=pl.CostEstimate(flops=5_000_000_000, bytes_accessed=20_000_000, transcendentals=0),
         name="scatter_edges",
     )(recv, rates)
@@ -229,15 +242,14 @@
 
 def middle_kernel(first, last, lat_rows, lon_cols, rows_ref, meta_ref, field_ref):
     field_ref[...] = jnp.zeros_like(field_ref)
-    depth = 2 * LANES
-    per = 6
+    depth = TILES * LANES
+    per = 4
 
     def accumulate(t, _):
         data = rows_ref[pl.ds(pl.multiple_of(t * depth, depth), depth), :]
-        col, row = one_hots([meta_ref[2 * t], meta_ref[2 * t + 1]], lat_rows, lon_cols)
-        colb = [c.astype(BF16) for c in col]
+        _, col, row = one_hots([meta_ref[TILES * t + h] for h in range(TILES)], lat_rows, lon_cols)
         for i in range(first, last, per):
-            spread = spread_rows(colb, row, range(i, i + per), lon_cols)
+            spread = spread_rows(col, row, range(i, i + per), lon_cols)
             at = pl.ds((i - first) * lon_cols, per * lon_cols)
             field_ref[at, :] += jnp.dot(spread, data, preferred_element_type=F32)
         return 0
@@ -252,32 +264,34 @@
         out_shape=jax.ShapeDtypeStruct(((last - first) * lon_cols, LANES), F32),
         in_specs=[full] * 2,
         out_specs=full,
-        compiler_params=pltpu.CompilerParams(vmem_limit_bytes=VMEM_LIMIT),
+        compiler_params=pltpu.CompilerParams(vmem_limit_bytes=10 * MIB),
         cost_estimate=pl.CostEstimate(flops=7_000_000_000, bytes_accessed=20_000_000, transcendentals=0),
         name="scatter_middle",
     )(rows, meta)
 
 
-def turn_kernel(lat_rows, lon_cols, below_ref, above_ref, strip_ref, rates_ref, west_ref, east_ref, tall_ref, cols):
+def turn_kernel(lat_rows, lon_cols, below_ref, above_ref, strip_ref, rates_ref, west_ref, east_ref, tall_ref, cols, wide_rows):
     tall = lat_rows + 2 * STEPS
     wide = STEPS * lon_cols
     below = below_ref[...].astype(F32)
     above = above_ref[...].astype(F32)
     strip = strip_ref[...].astype(F32)
+    wide_rows[0] = below
+    wide_rows[1] = above
     for c in range(2):
         at = c * tall
         tall_ref[at : at + STEPS, :] = below[wide + c * STEPS : wide + (c + 1) * STEPS]
         tall_ref[at + STEPS : at + STEPS + lat_rows, :] = rates_ref[c * lat_rows : (c + 1) * lat_rows, :]
         tall_ref[at + STEPS + lat_rows : at + tall, :] = above[wide + c * STEPS : wide + (c + 1) * STEPS]
     for side, ref in ((0, west_ref), (1, east_ref)):
-        base = side * (lon_cols - STEPS)
+        first = side * (lon_cols // GROUPS - STEPS) * GROUPS + side * (GROUPS - 1)
         for j in range(STEPS):
             n = (side * STEPS + j) * lat_rows
             cols[pl.ds(STEPS * STEPS + j, lat_rows, stride=STEPS), :] = strip[n : n + lat_rows]
         for i in range(STEPS):
-            cols[pl.ds(STEPS * i, STEPS), :] = below[i * lon_cols + base : i * lon_cols + base + STEPS]
-            n = STEPS * (STEPS + lat_rows + i)
-            cols[pl.ds(n, STEPS), :] = above[i * lon_cols + base : i * lon_cols + base + STEPS]
+            picked = pl.ds(i * lon_cols + first, STEPS, stride=GROUPS)
+            cols[pl.ds(STEPS * i, STEPS), :] = wide_rows[0, picked, :]
+            cols[pl.ds(STEPS * (STEPS + lat_rows + i), STEPS), :] = wide_rows[1, picked, :]
         ref[: STEPS * tall, :] = cols[...].astype(BF16)
         ref[STEPS * tall :, :] = tall_ref[...].astype(BF16)
 
@@ -291,8 +305,8 @@
         out_shape=[side, side, jax.ShapeDtypeStruct((2 * tall, LANES), F32)],
         in_specs=[full] * 4,
         out_specs=[full] * 3,
-        scratch_shapes=[pltpu.VMEM((STEPS * tall, LANES), F32)],
-        compiler_params=pltpu.CompilerParams(vmem_limit_bytes=VMEM_LIMIT),
+        scratch_shapes=[pltpu.VMEM((STEPS * tall, LANES), F32), pltpu.VMEM((2, STEPS * lon_cols + 16, LANES), F32)],
+        compiler_params=pltpu.CompilerParams(vmem_limit_bytes=3 * MIB),
         cost_estimate=pl.CostEstimate(flops=1_000_000, bytes_accessed=1_000_000, transcendentals=0),
         name="turn",
     )(below, above, strip, rates)
@@ -325,6 +339,8 @@
     lead = PAD - STEPS
     trail = PAD + lon_cols
     half = (lat_rows - 2 * STEPS) // 2
+    part = lon_cols // GROUPS
+    span = (part + 2 * STEPS) * GROUPS
     west = west_ref[...].astype(F32)
     east = east_ref[...].astype(F32)
 
@@ -336,16 +352,24 @@
         kappa[c, PAD:trail, :] = jnp.concatenate([rates_ref[c * tall : (c + 1) * tall, :], rest], axis=0).T
         kappa[c, trail : trail + STEPS, :] = jnp.concatenate([east[at : at + tall], rest], axis=0).T[:STEPS]
         kappa[c, trail + STEPS :, :] = jnp.zeros((lead, LANES), F32)
-    kx, ky = kappa[0], kappa[1]
-    ex = 0.5 * (kx + pltpu.roll(kx, width - 1, 0))
-    row = place_ref[0] * lat_rows - STEPS + iota((width, LANES), 1)
+
+    def strips(c):
+        return jnp.concatenate(
+            [kappa[c, pl.ds(lead + m, GROUPS, stride=part), :] for m in range(part + 2 * STEPS)], axis=0
+        )
+
+    kx, ky = strips(0), strips(1)
+    ex = 0.5 * (kx + jnp.concatenate([kx[GROUPS:], kx[:GROUPS]], axis=0))
+    row = place_ref[0] * lat_rows - STEPS + iota((span, LANES), 1)
     inside = (row >= 0) & (row < lat_rows * lat_devices - 1)
     ny = jnp.where(inside, 0.5 * (ky + pltpu.roll(ky, LANES - 1, 1)), 0.0)
     for i in range(tall):
-        at = pl.ds(i * width, width)
-        face_x[at, :] = jnp.broadcast_to(ex[:, i : i + 1], (width, LANES))
-        face_y[at, :] = jnp.broadcast_to(ny[:, i : i + 1], (width, LANES))
-
+        at = pl.ds(i * span, span)
+        face_x[at, :] = jnp.broadcast_to(ex[:, i : i + 1], (span, LANES))
+        face_y[at, :] = jnp.broadcast_to(ny[:, i : i + 1], (span, LANES))
+
+    strip_id = iota((GROUPS, LANES), 0)
+    inner = STEPS * GROUPS
     for i in range(tall):
         n = i - STEPS
         if n < 0:
@@ -360,30 +384,39 @@
             middle = outer_ref[pl.ds((n - 2 * half) * lon_cols, lon_cols), :]
         else:
             middle = above_ref[pl.ds((n - lat_rows) * lon_cols, lon_cols), :].astype(F32)
-        ping[pl.ds(i * width, PAD), :] = jnp.zeros((PAD, LANES), F32)
-        ping[pl.ds(i * width + trail, PAD), :] = jnp.zeros((PAD, LANES), F32)
-        ping[pl.ds(i * width + PAD, lon_cols), :] = middle
-        ping[pl.ds(i * width + lead, STEPS), :] = west[STEPS * i : STEPS * i + STEPS]
-        ping[pl.ds(i * width + trail, STEPS), :] = east[STEPS * i : STEPS * i + STEPS]
-
-    def row_at(i):
-        return pl.ds(pl.multiple_of(i * width, 8), width)
+        ping[pl.ds(i * span + inner, lon_cols), :] = middle
+        for q in range(STEPS):
+            tail = middle[(part - STEPS + q) * GROUPS : (part - STEPS + q + 1) * GROUPS]
+            side = jnp.broadcast_to(west[STEPS * i + q : STEPS * i + q + 1], (GROUPS, LANES))
+            before = jnp.where(strip_id == 0, side, pltpu.roll(tail, 1, 0))
+            ping[pl.ds(i * span + q * GROUPS, GROUPS), :] = before
+            head = middle[q * GROUPS : (q + 1) * GROUPS]
+            side = jnp.broadcast_to(east[STEPS * i + q : STEPS * i + q + 1], (GROUPS, LANES))
+            after = jnp.where(strip_id == GROUPS - 1, side, pltpu.roll(head, GROUPS - 1, 0))
+            ping[pl.ds(i * span + inner + lon_cols + q * GROUPS, GROUPS), :] = after
 
     for sweep in range(STEPS):
         old, new = (ping, pong) if sweep % 2 == 0 else (pong, ping)
         low, high = sweep + 1, tall - sweep - 1
-
-        def one_row(i, carry, old=old, new=new):
+        edge = sweep * GROUPS
+        count = span - 2 * edge
+
+        def load(ref, i, edge=edge, count=count):
+            return ref[pl.ds(pl.multiple_of(i * span + edge, 8), count), :]
+
+        def one_row(i, carry, old=old, new=new, load=load, edge=edge, count=count):
             here, flux_below = carry
-            above = old[row_at(i + 1), :]
-            flux_y = face_y[row_at(i), :] * (above - here)
-            flux_x = face_x[row_at(i), :] * (pltpu.roll(here, width - 1, 0) - here)
-            new[row_at(i), :] = here + flux_x - pltpu.roll(flux_x, 1, 0) + flux_y - flux_below
+            above = load(old, i + 1)
+            flux_y = load(face_y, i) * (above - here)
+            flux_x = load(face_x, i)[: count - GROUPS] * (here[GROUPS:] - here[: count - GROUPS])
+            change = flux_x[GROUPS:] - flux_x[: count - 2 * GROUPS] + (flux_y - flux_below)[GROUPS : count - GROUPS]
+            at = pl.ds(pl.multiple_of(i * span + edge + GROUPS, 8), count - 2 * GROUPS)
+            new[at, :] = here[GROUPS : count - GROUPS] + change
             return above, flux_y
 
-        here = old[row_at(low), :]
-        start = face_y[row_at(low - 1), :] * (here - old[row_at(low - 1), :])
-        lax.fori_loop(low, high, one_row, (here, start))
+        here = load(old, low)
+        start = load(face_y, low - 1) * (here - load(old, low - 1))
+        lax.fori_loop(low, high, one_row, (here, start), unroll=UNROLL_SWEEP)
 
     last = ping if STEPS % 2 == 0 else pong
     gain = gain_ref[...]
@@ -393,8 +426,9 @@
     def project(h, _):
         pair = []
         for u in range(2):
-            at = pl.multiple_of((2 * h + u + STEPS) * width + PAD, 8)
-            value = last[pl.ds(at, lon_cols), :] * gain
+            at = (2 * h + u + STEPS) * span + inner
+            value = jnp.concatenate([last[pl.ds(at + t, part, stride=GROUPS), :] for t in range(GROUPS)], axis=0)
+            value = value * gain
             head = value.astype(BF16)
             low = (value - head.astype(F32)).astype(BF16)
             pair.append(jnp.concatenate([head, low], axis=1))
@@ -404,20 +438,21 @@
         out_ref[pl.ds(2 * h + 1, levels, stride=lat_rows), :] = result[:, lon_cols:]
         return 0
 
-    lax.fori_loop(0, lat_rows // 2, project, 0)
+    lax.fori_loop(0, lat_rows // 2, project, 0, unroll=UNROLL_PROJECT)
 
 
 def diffuse(place, outer, mid1, mid2, below, above, west, east, rates, inv_var, jacobian, lat_rows, lon_cols, lats):
     full = pl.BlockSpec(memory_space=pltpu.VMEM)
     levels = jacobian.shape[1]
     tall, width = lat_rows + 2 * STEPS, lon_cols + 2 * PAD
+    span = lon_cols + 2 * STEPS * GROUPS
     out = pl.pallas_call(
         functools.partial(diffuse_kernel, lat_rows, lon_cols, lats),
         out_shape=jax.ShapeDtypeStruct((levels * lat_rows, lon_cols), F32),
         in_specs=[pl.BlockSpec(memory_space=pltpu.SMEM)] + [full] * 10,
         out_specs=full,
-        scratch_shapes=[pltpu.VMEM((tall * width, LANES), F32)] * 4 + [pltpu.VMEM((2, width, LANES), F32)],
-        compiler_params=pltpu.CompilerParams(vmem_limit_bytes=VMEM_LIMIT),
+        scratch_shapes=[pltpu.VMEM((tall * span, LANES), F32)] * 4 + [pltpu.VMEM((2, width, LANES), F32)],
+        compiler_params=pltpu.CompilerParams(vmem_limit_bytes=28 * MIB),
         cost_estimate=pl.CostEstimate(flops=1_000_000_000, bytes_accessed=20_000_000, transcendentals=0),
         name="diffuse",
     )(place, outer, mid1, mid2, below, above, west, east, rates, inv_var.reshape(1, -1), jacobian.T)

time: 136 us -> 116 us (0.85)
  Pallas kernels: 79.3 us -> 56.4 us
  local copies, waits for them, and re-layouts: 2.75 us -> 5.04 us
    pallas_call x2, Pallas kernels: 31.6 us -> 22.3 us  [scatter_middle(): pl.pallas_call(functools.partial(middle_kernel, first, last, lat_rows, lo...]
    pallas_call x1, Pallas kernels: 17 us -> 12 us  [scatter_edges(): pl.pallas_call(functools.partial(edge_kernel, cap, lat_rows, lon_cols), o...]
    pallas_call x1, Pallas kernels: 15.4 us -> 11.1 us  [diffuse(): pl.pallas_call(functools.partial(diffuse_kernel, lat_rows, lon_cols, lats...]
    pallas_call x1, Pallas kernels: 13.6 us -> 10.9 us  [pack(): pl.pallas_call(functools.partial(pack_kernel, cap), out_shape=jax.ShapeDt...]
    unnamed x10 -> x16, local copies, waits for them, and re-layouts: 2.75 us -> 5.04 us
    pallas_call x1, Pallas kernels: 1.67 us -> 0.06 us  [turn(): pl.pallas_call(functools.partial(turn_kernel, lat_rows, lon_cols), out_sh...]
  transfers between devices with their start and end apart: 5 -> 5, of which waited for: 1 -> 1; matrix products, arithmetic and copies ran while one was open for 0% -> 0% of each run, Pallas kernels for 23% -> 19%
where the time goes in v3:
time: 116 us
  Pallas kernels  56.4 us (49%)
  waiting for transfers between devices  32.7 us (28%)
  starting transfers between devices  21.2 us (18%)
  local copies, waits for them, and re-layouts  5.04 us (4%)
    all_to_all x1, waiting for transfers between devices, local(): lax.all_to_all(send.reshape(devices, cap + META, LANES), ('lon', 'lat'),...  32.7 us
    pallas_call x2, Pallas kernels, scatter_middle(): pl.pallas_call(functools.partial(middle_kernel, first, last, lat_rows, lo...  22.3 us
    pallas_call x1, Pallas kernels, scatter_edges(): pl.pallas_call(functools.partial(edge_kernel, cap, lat_rows, lon_cols), o...  12 us
    pallas_call x1, Pallas kernels, diffuse(): pl.pallas_call(functools.partial(diffuse_kernel, lat_rows, lon_cols, lats...  11.1 us
    ppermute x4, starting transfers between devices, moved(): return lax.ppermute(value, axis, pairs)  11 us
    pallas_call x1, Pallas kernels, pack(): pl.pallas_call(functools.partial(pack_kernel, cap), out_shape=jax.ShapeDt...  10.9 us
    all_to_all x1, starting transfers between devices, local(): lax.all_to_all(send.reshape(devices, cap + META, LANES), ('lon', 'lat'),...  10.3 us
    unnamed x16, local copies, waits for them, and re-layouts  5.04 us
  transfers between devices with their start and end apart: 5, of which 1 were waited for; matrix products, arithmetic and copies ran while one was open for 0% of the time, Pallas kernels for 19%

profile of v3, /device:TPU:32, one launch (start us, length us, event | category | flops | bytes accessed | tf_op | source)
XLA Modules:
  0.0 115.6 jit_solution(5775222329909816248)
XLA Ops:
  0.0 0.0 copy-start.4
  0.0 1.2 %copy-done.4 = bf16[4096,128]{1,0:T(8,128)(2,1)S(1)} copy-done((bf16[4096,128]{1,0:T(8,128)(2,1)S(1)}, bf16[4096,128]{1,0:T(8,128)(2,1)}, u32[]{:S(2)}) %copy-start.4) | copy-done | bytes 1048600
  1.2 0.0 copy-start.5
  1.2 0.8 copy-done.5
  2.1 0.0 copy-start.6
  2.1 0.8 copy-done.6
  2.9 0.0 copy-start.7
  2.9 0.7 copy-done.7
  3.6 10.9 %pack.1 = bf16[9216,128]{1,0:T(8,128)(2,1)S(1)} custom-call(s32[32,128]{1,0:T(8,128)S(1)} %bitcast.18, s32[4,4096]{1,0:T(4,128)S(1)} %bitcast.16, f32[4,4096]{1,0:T(4,128)S(1)} %bitcast.17, bf16[4096,128]{1,0:T(8,128)(2,1)S(1)} %copy-done.4), custom_call_target="tpu_custom_call" | custom-call | flops 4000000000 | bytes 40000000 | tf_op jit(solution)/shard_map/pack/pallas_call | solution.py:114
  14.5 0.0 copy-start
  14.5 1.4 %copy-done = bf16[9216,128]{1,0:T(8,128)(2,1)} copy-done((bf16[9216,128]{1,0:T(8,128)(2,1)}, bf16[9216,128]{1,0:T(8,128)(2,1)S(1)}, u32[]{:S(2)}) %copy-start) | copy-done | bytes 2359320
  15.9 0.0 copy-start.2
  15.9 10.3 %all-to-all-start = ((bf16[128,72,128]{2,1,0:T(8,128)(2,1)}), bf16[128,72,128]{2,1,0:T(8,128)(2,1)S(1)}, u32[]{:S(2)}, u32[]{:S(2)}) async-start(bf16[128,72,128]{2,1,0:T(8,128)(2,1)} %bitcast.11), calls=%async_computation | async-start | bytes 4718592 | tf_op jit(solution)/shard_map/all_to_all | solution.py:474
  26.2 32.7 %all-to-all-done = bf16[128,72,128]{2,1,0:T(8,128)(2,1)S(1)} async-done(((bf16[128,72,128]{2,1,0:T(8,128)(2,1)}), bf16[128,72,128]{2,1,0:T(8,128)(2,1)S(1)}, u32[]{:S(2)}, u32[]{:S(2)}) %all-to-all-start) | async-done | bytes 2359328 | tf_op jit(solution)/shard_map/all_to_all | solution.py:474
  59.0 0.0 copy-done.2
  59.0 12.0 %scatter_edges.1 = (bf16[8192,128]{1,0:T(8,128)(2,1)S(1)}, f32[64,16,128]{2,1,0:T(8,128)S(1)}, f32[1024,128]{1,0:T(8,128)S(1)}, bf16[528,128]{1,0:T(8,128)(2,1)S...) custom-call(bf16[9216,128]{1,0:T(8,128)(2,1)S(1)} %bitcast.10, f32[64,128]{1,0:T(8,128)S(1)} %bitcast.13), custom_call_target="tpu_custom_call" | custom-call | flops 5000000000 | bytes 20000000 | tf_op jit(solution)/shard_map/scatter_edges/pallas_call | solution.py:231
  71.0 1.9 %collective-permute-start = (bf16[528,128]{1,0:T(8,128)(2,1)S(1)}, bf16[528,128]{1,0:T(8,128)(2,1)S(1)}, u32[]{:S(2)}, u32[]{:S(2)}) collective-permute-start(bf16[528,128]{1,0:T(8,128)(2,1)S(1)} %get-tuple-element.20), channel_id=1, source_target_pairs={{0,1},{1,2},{2,3},{4,5},{5,6},{6,7},{8,9},{9,10},{10,11},{12,13},{... | collective-permute-start | bytes 405512 | tf_op jit(solution)/shard_map/ppermute | solution.py:465
  72.9 3.9 %collective-permute-start.1 = (bf16[528,128]{1,0:T(8,128)(2,1)S(1)}, bf16[528,128]{1,0:T(8,128)(2,1)S(1)}, u32[]{:S(2)}, u32[]{:S(2)}) collective-permute-start(bf16[528,128]{1,0:T(8,128)(2,1)S(1)} %get-tuple-element.21), channel_id=1, source_target_pairs={{1,0},{2,1},{3,2},{5,4},{6,5},{7,6},{9,8},{10,9},{11,10},{13,12},{... | collective-permute-start | bytes 405512 | tf_op jit(solution)/shard_map/ppermute | solution.py:465
  76.9 11.2 %scatter_middle.2.mid1_ref = f32[1536,128]{1,0:T(8,128)S(1)} custom-call(bf16[8192,128]{1,0:T(8,128)(2,1)S(1)} %get-tuple-element.18.rows_ref, f32[64,16,128]{2,1,0:T(8,128)S(1)} %get-tuple-element.22.meta_ref), custom_call_target="tpu_custom_call" | custom-call | flops 7000000000 | bytes 20000000 | tf_op jit(solution)/shard_map/scatter_middle/pallas_call | solution.py:262
  88.0 0.0 collective-permute-done.below_ref
  88.0 0.0 collective-permute-done.1.above_ref
  88.0 0.1 turn.1
  88.1 0.1 collective-permute-start.2
  88.2 0.0 copy-start.1
  88.2 0.0 copy-start.3
  88.2 5.0 %collective-permute-start.3 = (bf16[240,128]{1,0:T(8,128)(2,1)S(1)}, bf16[240,128]{1,0:T(8,128)(2,1)S(1)}, u32[]{:S(2)}, u32[]{:S(2)}) collective-permute-start(bf16[240,128]{1,0:T(8,128)(2,1)S(1)} %get-tuple-element.27), channel_id=1, source_target_pairs={{4,0},{8,4},{12,8},{16,12},{20,16},{24,20},{28,24},{32,28},{36,32}... | collective-permute-start | bytes 184328 | tf_op jit(solution)/shard_map/ppermute | solution.py:465
  93.2 11.2 %scatter_middle.3.mid2_ref = f32[1536,128]{1,0:T(8,128)S(1)} custom-call(bf16[8192,128]{1,0:T(8,128)(2,1)S(1)} %get-tuple-element.18.rows_ref, f32[64,16,128]{2,1,0:T(8,128)S(1)} %get-tuple-element.22.meta_ref), custom_call_target="tpu_custom_call" | custom-call | flops 7000000000 | bytes 20000000 | tf_op jit(solution)/shard_map/scatter_middle/pallas_call | solution.py:262
  104.4 0.0 collective-permute-done.2.west_ref
  104.4 0.0 collective-permute-done.3.east_ref
  104.4 0.0 copy-done.1
  104.4 0.0 copy-done.3
  104.4 11.1 %diffuse.1 = f32[5120,128]{1,0:T(8,128)} custom-call(s32[1]{0:T(128)} %bitcast.place_ref, f32[1024,128]{1,0:T(8,128)S(1)} %get-tuple-element.17.outer_ref, f32[1536,128]{1,0:T(8,128)S(1)} %scatter_middle.2.mid1_ref, f32[1536,128]{1,0:T(8,128)S(1)} %scatter_middle.3.mid2_ref, bf16[528,128]{1,0:T(8,128)(2,1)S(1)} %collective-permute-done.below_ref, ...), custom_call_target="tpu_custom_call" | custom-call | flops 1000000000 | bytes 20000000 | tf_op jit(solution)/shard_map/diffuse/pallas_call | solution.py:449
Async XLA Ops:
  0.0 1.2 %copy-start.4 = (bf16[4096,128]{1,0:T(8,128)(2,1)S(1)}, bf16[4096,128]{1,0:T(8,128)(2,1)}, u32[]{:S(2)}) copy-start(bf16[4096,128]{1,0:T(8,128)(2,1)} %rows_ref.1) | copy-start | bytes 3145732
  1.2 0.8 copy-start.5
  2.1 0.8 copy-start.6
  2.9 0.7 copy-start.7
  14.5 1.4 %copy-start = (bf16[9216,128]{1,0:T(8,128)(2,1)}, bf16[9216,128]{1,0:T(8,128)(2,1)S(1)}, u32[]{:S(2)}) copy-start(bf16[9216,128]{1,0:T(8,128)(2,1)S(1)} %pack.1) | copy-start | bytes 7077892
  15.9 43.0 %copy-start.2 = (f32[2,32,128]{2,1,0:T(8,128)S(1)}, f32[2,32,128]{2,1,0:T(8,128)}, u32[]{:S(2)}) copy-start(f32[2,32,128]{2,1,0:T(8,128)} %param.13) | copy-start | bytes 98308
  15.9 43.0 %all-to-all-start = ((bf16[128,72,128]{2,1,0:T(8,128)(2,1)}), bf16[128,72,128]{2,1,0:T(8,128)(2,1)S(1)}, u32[]{:S(2)}, u32[]{:S(2)}) async-start(bf16[128,72,128]{2,1,0:T(8,128)(2,1)} %bitcast.11), calls=%async_computation | async-start | bytes 4718592 | tf_op jit(solution)/shard_map/all_to_all | solution.py:474
  71.0 17.0 %collective-permute-start = (bf16[528,128]{1,0:T(8,128)(2,1)S(1)}, bf16[528,128]{1,0:T(8,128)(2,1)S(1)}, u32[]{:S(2)}, u32[]{:S(2)}) collective-permute-start(bf16[528,128]{1,0:T(8,128)(2,1)S(1)} %get-tuple-element.20), channel_id=1, source_target_pairs={{0,1},{1,2},{2,3},{4,5},{5,6},{6,7},{8,9},{9,10},{10,11},{12,13},{... | collective-permute-start | bytes 405512 | tf_op jit(solution)/shard_map/ppermute | solution.py:465
  72.9 15.1 %collective-permute-start.1 = (bf16[528,128]{1,0:T(8,128)(2,1)S(1)}, bf16[528,128]{1,0:T(8,128)(2,1)S(1)}, u32[]{:S(2)}, u32[]{:S(2)}) collective-permute-start(bf16[528,128]{1,0:T(8,128)(2,1)S(1)} %get-tuple-element.21), channel_id=1, source_target_pairs={{1,0},{2,1},{3,2},{5,4},{6,5},{7,6},{9,8},{10,9},{11,10},{13,12},{... | collective-permute-start | bytes 405512 | tf_op jit(solution)/shard_map/ppermute | solution.py:465
  88.1 16.3 %collective-permute-start.2 = (bf16[240,128]{1,0:T(8,128)(2,1)S(1)}, bf16[240,128]{1,0:T(8,128)(2,1)S(1)}, u32[]{:S(2)}, u32[]{:S(2)}) collective-permute-start(bf16[240,128]{1,0:T(8,128)(2,1)S(1)} %get-tuple-element.26), channel_id=1, source_target_pairs={{124,0},{0,4},{4,8},{8,12},{12,16},{16,20},{20,24},{24,28},{28,32}... | collective-permute-start | bytes 184328 | tf_op jit(solution)/shard_map/ppermute | solution.py:465
  88.2 16.2 %copy-start.1 = (bf16[128,160]{0,1:T(8,128)(2,1)S(1)}, bf16[128,160]{0,1:T(8,128)(2,1)}, u32[]{:S(2)}) copy-start(bf16[128,160]{0,1:T(8,128)(2,1)} %param.12) | copy-start | bytes 122884
  88.2 16.2 %copy-start.3 = (f32[128]{0:T(128)S(1)}, f32[128]{0:T(128)}, u32[]{:S(2)}) copy-start(f32[128]{0:T(128)} %param.11) | copy-start | bytes 1540
  88.2 16.2 %collective-permute-start.3 = (bf16[240,128]{1,0:T(8,128)(2,1)S(1)}, bf16[240,128]{1,0:T(8,128)(2,1)S(1)}, u32[]{:S(2)}, u32[]{:S(2)}) collective-permute-start(bf16[240,128]{1,0:T(8,128)(2,1)S(1)} %get-tuple-element.27), channel_id=1, source_target_pairs={{4,0},{8,4},{12,8},{16,12},{20,16},{24,20},{28,24},{32,28},{36,32}... | collective-permute-start | bytes 184328 | tf_op jit(solution)/shard_map/ppermute | solution.py:465

commit v4 on v3

--- a/solution.py
+++ b/solution.py
@@ -12,9 +12,12 @@
 META = 8
 PAD = 8
 GROUPS = 8
-TILES = 4
-UNROLL_SWEEP = 1
-UNROLL_PROJECT = 2
+TILES = 16
+CHUNKS = 8
+UNROLL_RANK = 8
+UNROLL_SWEEP = 6
+SWEEP_PARTS = 2
+UNROLL_PROJECT = 16
 F32 = jnp.float32
 BF16 = jnp.bfloat16
 MIB = 1024 * 1024
@@ -24,25 +27,58 @@
     return lax.broadcasted_iota(jnp.int32, shape, dim)
 
 
-def pack_kernel(cap, owner_ref, cells_ref, weights_ref, rows_ref, out_ref, xd, xm, yd, ym, slots_v, slots_s, sem):
+def pack_kernel(
+    cap,
+    owner_hbm,
+    cells_hbm,
+    weights_hbm,
+    rows_hbm,
+    out_hbm,
+    owner_ref,
+    cells_ref,
+    weights_ref,
+    rows_ref,
+    out_ref,
+    xd,
+    xm,
+    yd,
+    ym,
+    slots_v,
+    slots_s,
+    in_sems,
+    slot_sems,
+    out_sems,
+):
     groups = owner_ref.shape[0]
     slots = yd.shape[0]
+    loads = [
+        pltpu.make_async_copy(src, dst, in_sems.at[n])
+        for n, (src, dst) in enumerate(
+            ((owner_hbm, owner_ref), (cells_hbm, cells_ref), (weights_hbm, weights_ref), (rows_hbm, rows_ref))
+        )
+    ]
+    for load in loads:
+        load.start()
+
+    def clear(g, _):
+        at = pl.ds(pl.multiple_of(g * LANES, LANES), LANES)
+        yd[at, :] = jnp.zeros((LANES, LANES), F32)
+        ym[at, :] = jnp.zeros((LANES, LANES), F32)
+        return 0
+
+    lax.fori_loop(0, slots // LANES, clear, 0, unroll=2)
     owner_id = iota((LANES, LANES), 0)
     before = (iota((LANES, 2 * LANES), 0) < iota((LANES, 2 * LANES), 1)).astype(F32).astype(BF16)
-
-    def rank_group(g, base):
+    for load in loads:
+        load.wait()
+
+    def rank_and_stage(g, base):
         own = owner_ref[pl.ds(g, 1), :]
         hit = (own == owner_id).astype(F32)
         seen = jnp.dot(hit.astype(BF16), before, preferred_element_type=F32)
         rank = jnp.sum(hit * (seen[:, :LANES] + base), axis=0, keepdims=True)
         slots_v[pl.ds(g, 1), :] = own * cap + rank.astype(jnp.int32)
-        return base + seen[:, LANES:]
-
-    lax.fori_loop(0, groups, rank_group, jnp.zeros((LANES, LANES), F32), unroll=4)
-    copy = pltpu.make_async_copy(slots_v, slots_s, sem)
-    copy.start()
-
-    def stage(g, _):
+
         at = pl.ds(pl.multiple_of(g * LANES, LANES), LANES)
         xd[at, :] = rows_ref[at, :].astype(F32)
         cells = cells_ref[:, at]
@@ -61,18 +97,7 @@
         col = (cells & 127).astype(F32)
         block = jnp.concatenate([row, col] + merged + [jnp.zeros((LANES - 12, LANES), F32)], axis=0)
         xm[at, :] = block.T
-        return 0
-
-    lax.fori_loop(0, groups, stage, 0, unroll=2)
-
-    def clear(g, _):
-        at = pl.ds(pl.multiple_of(g * LANES, LANES), LANES)
-        yd[at, :] = jnp.zeros((LANES, LANES), F32)
-        ym[at, :] = jnp.zeros((LANES, LANES), F32)
-        return 0
-
-    lax.fori_loop(0, slots // LANES, clear, 0, unroll=2)
-    copy.wait()
+        return base + seen[:, LANES:]
 
     def move(g, _):
         first = pl.multiple_of(g * LANES, LANES)
@@ -82,16 +107,25 @@
             ym[pl.ds(s, 1), :] = xm[pl.ds(first + u, 1), :]
         return 0
 
-    lax.fori_loop(0, groups, move, 0)
+    half = groups // 2
+    base = jnp.zeros((LANES, LANES), F32)
+    copies = []
+    for h in range(2):
+        base = lax.fori_loop(h * half, (h + 1) * half, rank_and_stage, base, unroll=UNROLL_RANK)
+        part = pl.ds(h * half, half)
+        copies.append(pltpu.make_async_copy(slots_v.at[part], slots_s.at[part], slot_sems.at[h]))
+        copies[h].start()
+    for h in range(2):
+        copies[h].wait()
+        lax.fori_loop(h * half, (h + 1) * half, move, 0)
 
     pick = (iota((16, LANES), 0) == iota((16, LANES), 1)).astype(F32).astype(BF16)
     left = iota((META, LANES), 1) < cap
     step = 2 * (cap + META)
-
-    batch = 8
-
-    def emit(c, _):
-        first_slot = pl.multiple_of(c * batch * LANES, LANES)
+    batch = slots // LANES // CHUNKS
+    stores = []
+    for c in range(CHUNKS):
+        first_slot = c * batch * LANES
         wide = ym[pl.ds(first_slot, batch * LANES), :].astype(BF16)
         metas = lax.dot_general(pick, wide, (((1,), (1,)), ((), ())), preferred_element_type=F32)
         for u in range(batch):
@@ -101,34 +135,45 @@
             first = jnp.where(left, low, pltpu.roll(high, cap, 1))
             second = jnp.where(left, pltpu.roll(low, cap, 1), high)
             block = jnp.concatenate([data[:cap], first, data[cap:], second], axis=0)
-            out_ref[pl.ds(pl.multiple_of((c * batch + u) * step, 16), step), :] = block.astype(BF16)
-        return 0
-
-    lax.fori_loop(0, slots // LANES // batch, emit, 0)
+            out_ref[pl.ds((c * batch + u) * step, step), :] = block.astype(BF16)
+        part = pl.ds(c * batch * step, batch * step)
+        stores.append(pltpu.make_async_copy(out_ref.at[part], out_hbm.at[part], out_sems.at[c]))
+        stores[c].start()
+    for store in stores:
+        store.wait()
 
 
 def pack(owner, cells, weights, rows, devices, cap):
     count = rows.shape[0]
     slots = devices * cap
-    full = pl.BlockSpec(memory_space=pltpu.VMEM)
+    groups = count // LANES
+    sent = devices * (cap + META)
+    hbm = pl.BlockSpec(memory_space=pltpu.HBM)
     return pl.pallas_call(
         functools.partial(pack_kernel, cap),
-        out_shape=jax.ShapeDtypeStruct((devices * (cap + META), LANES), BF16),
-        in_specs=[full] * 4,
-        out_specs=full,
+        out_shape=jax.ShapeDtypeStruct((sent, LANES), BF16),
+        in_specs=[hbm] * 4,
+        out_specs=hbm,
         scratch_shapes=[
+            pltpu.VMEM((groups, LANES), jnp.int32),
+            pltpu.VMEM((4, count), jnp.int32),
+            pltpu.VMEM((4, count), F32),
+            pltpu.VMEM((count, LANES), BF16),
+            pltpu.VMEM((sent, LANES), BF16),
             pltpu.VMEM((count, LANES), F32),
             pltpu.VMEM((count, LANES), F32),
             pltpu.VMEM((slots, LANES), F32),
             pltpu.VMEM((slots, LANES), F32),
-            pltpu.VMEM((count // LANES, LANES), jnp.int32),
-            pltpu.SMEM((count // LANES, LANES), jnp.int32),
-            pltpu.SemaphoreType.DMA,
+            pltpu.VMEM((groups, LANES), jnp.int32),
+            pltpu.SMEM((groups, LANES), jnp.int32),
+            pltpu.SemaphoreType.DMA((4,)),
+            pltpu.SemaphoreType.DMA((2,)),
+            pltpu.SemaphoreType.DMA((CHUNKS,)),
         ],
-        compiler_params=pltpu.CompilerParams(vmem_limit_bytes=20 * MIB),
+        compiler_params=pltpu.CompilerParams(vmem_limit_bytes=60 * MIB),
         cost_estimate=pl.CostEstimate(flops=4_000_000_000, bytes_accessed=40_000_000, transcendentals=0),
         name="pack",
-    )(owner.reshape(count // LANES, LANES), cells.T, weights.T, rows)
+    )(owner.reshape(groups, LANES), cells.T, weights.T, rows)
 
 
 def column_of(lon_cols, dim_rows):
@@ -398,25 +443,27 @@
     for sweep in range(STEPS):
         old, new = (ping, pong) if sweep % 2 == 0 else (pong, ping)
         low, high = sweep + 1, tall - sweep - 1
-        edge = sweep * GROUPS
-        count = span - 2 * edge
-
-        def load(ref, i, edge=edge, count=count):
-            return ref[pl.ds(pl.multiple_of(i * span + edge, 8), count), :]
-
-        def one_row(i, carry, old=old, new=new, load=load, edge=edge, count=count):
-            here, flux_below = carry
-            above = load(old, i + 1)
-            flux_y = load(face_y, i) * (above - here)
-            flux_x = load(face_x, i)[: count - GROUPS] * (here[GROUPS:] - here[: count - GROUPS])
-            change = flux_x[GROUPS:] - flux_x[: count - 2 * GROUPS] + (flux_y - flux_below)[GROUPS : count - GROUPS]
-            at = pl.ds(pl.multiple_of(i * span + edge + GROUPS, 8), count - 2 * GROUPS)
-            new[at, :] = here[GROUPS : count - GROUPS] + change
-            return above, flux_y
-
-        here = load(old, low)
-        start = load(face_y, low - 1) * (here - load(old, low - 1))
-        lax.fori_loop(low, high, one_row, (here, start), unroll=UNROLL_SWEEP)
+        first, stop = sweep + 1, span // GROUPS - 1 - sweep
+        cuts = [first + (stop - first) * n // SWEEP_PARTS for n in range(SWEEP_PARTS + 1)]
+        for at, end in zip(cuts[:-1], cuts[1:]):
+            inside_rows = (end - at) * GROUPS
+
+            def load(ref, i, start, count):
+                return ref[pl.ds(pl.multiple_of(i * span + start * GROUPS, 8), count), :]
+
+            def one_row(i, carry, old=old, new=new, at=at, count=inside_rows):
+                here, flux_below = carry
+                above = load(old, i + 1, at - 1, count + 2 * GROUPS)
+                flux_y = load(face_y, i, at, count) * (above - here)[GROUPS : count + GROUPS]
+                flux_x = load(face_x, i, at - 1, count + GROUPS) * (here[GROUPS:] - here[: count + GROUPS])
+                change = flux_x[GROUPS:] - flux_x[:count] + (flux_y - flux_below)
+                new[pl.ds(pl.multiple_of(i * span + at * GROUPS, 8), count), :] = here[GROUPS : count + GROUPS] + change
+                return above, flux_y
+
+            here = load(old, low, at - 1, inside_rows + 2 * GROUPS)
+            start = load(old, low - 1, at, inside_rows)
+            start = load(face_y, low - 1, at, inside_rows) * (here[GROUPS : inside_rows + GROUPS] - start)
+            lax.fori_loop(low, high, one_row, (here, start), unroll=UNROLL_SWEEP)
 
     last = ping if STEPS % 2 == 0 else pong
     gain = gain_ref[...]

time: 116 us -> 103 us (0.89)
  Pallas kernels: 56.4 us -> 48.4 us
  local copies, waits for them, and re-layouts: 5.04 us -> 0.02 us
    unnamed x16 -> x6, local copies, waits for them, and re-layouts: 5.04 us -> 0.02 us
    pallas_call x2, Pallas kernels: 22.3 us -> 19.5 us  [scatter_middle(): pl.pallas_call(functools.partial(middle_kernel, first, last, lat_rows, lo...]
    pallas_call x1, Pallas kernels: 10.9 us -> 8.85 us  [pack(): pl.pallas_call(functools.partial(pack_kernel, cap), out_shape=jax.ShapeDt...]
    pallas_call x1, Pallas kernels: 11.1 us -> 9.44 us  [diffuse(): pl.pallas_call(functools.partial(diffuse_kernel, lat_rows, lon_cols, lats...]
    pallas_call x1, Pallas kernels: 12 us -> 10.6 us  [scatter_edges(): pl.pallas_call(functools.partial(edge_kernel, cap, lat_rows, lon_cols), o...]
where the time goes in v4:
time: 103 us
  Pallas kernels  48.4 us (47%)
  waiting for transfers between devices  32.7 us (32%)
  starting transfers between devices  21.2 us (21%)
    all_to_all x1, waiting for transfers between devices, local(): lax.all_to_all(send.reshape(devices, cap + META, LANES), ('lon', 'lat'),...  32.7 us
    pallas_call x2, Pallas kernels, scatter_middle(): pl.pallas_call(functools.partial(middle_kernel, first, last, lat_rows, lo...  19.5 us
    ppermute x4, starting transfers between devices, moved(): return lax.ppermute(value, axis, pairs)  11 us
    pallas_call x1, Pallas kernels, scatter_edges(): pl.pallas_call(functools.partial(edge_kernel, cap, lat_rows, lon_cols), o...  10.6 us
    all_to_all x1, starting transfers between devices, local(): lax.all_to_all(send.reshape(devices, cap + META, LANES), ('lon', 'lat'),...  10.2 us
    pallas_call x1, Pallas kernels, diffuse(): pl.pallas_call(functools.partial(diffuse_kernel, lat_rows, lon_cols, lats...  9.44 us
    pallas_call x1, Pallas kernels, pack(): pl.pallas_call(functools.partial(pack_kernel, cap), out_shape=jax.ShapeDt...  8.85 us
  transfers between devices with their start and end apart: 5, of which 1 were waited for; matrix products, arithmetic and copies ran while one was open for 0% of the time, Pallas kernels for 19%

profile of v4, /device:TPU:32, one launch (start us, length us, event | category | flops | bytes accessed | tf_op | source)
XLA Modules:
  0.0 102.5 jit_solution(2356265198642176132)
XLA Ops:
  0.0 8.8 %pack.1 = bf16[9216,128]{1,0:T(8,128)(2,1)} custom-call(s32[32,128]{1,0:T(8,128)} %bitcast.18, s32[4,4096]{1,0:T(4,128)} %bitcast.16, f32[4,4096]{1,0:T(4,128)} %bitcast.17, bf16[4096,128]{1,0:T(8,128)(2,1)} %rows_hbm.1), custom_call_target="tpu_custom_call" | custom-call | flops 4000000000 | bytes 40000000 | tf_op jit(solution)/shard_map/pack/pallas_call | solution.py:152
  8.9 0.0 copy-start.1
  8.9 10.2 %all-to-all-start = ((bf16[128,72,128]{2,1,0:T(8,128)(2,1)}), bf16[128,72,128]{2,1,0:T(8,128)(2,1)S(1)}, u32[]{:S(2)}, u32[]{:S(2)}) async-start(bf16[128,72,128]{2,1,0:T(8,128)(2,1)} %bitcast.15), calls=%async_computation | async-start | bytes 4718592 | tf_op jit(solution)/shard_map/all_to_all | solution.py:521
  19.1 32.7 %all-to-all-done = bf16[128,72,128]{2,1,0:T(8,128)(2,1)S(1)} async-done(((bf16[128,72,128]{2,1,0:T(8,128)(2,1)}), bf16[128,72,128]{2,1,0:T(8,128)(2,1)S(1)}, u32[]{:S(2)}, u32[]{:S(2)}) %all-to-all-start) | async-done | bytes 2359328 | tf_op jit(solution)/shard_map/all_to_all | solution.py:521
  51.8 0.0 copy-done.1
  51.8 10.6 %scatter_edges.1 = (bf16[8192,128]{1,0:T(8,128)(2,1)S(1)}, f32[64,16,128]{2,1,0:T(8,128)S(1)}, f32[1024,128]{1,0:T(8,128)S(1)}, bf16[528,128]{1,0:T(8,128)(2,1)S...) custom-call(bf16[9216,128]{1,0:T(8,128)(2,1)S(1)} %bitcast.10, f32[64,128]{1,0:T(8,128)S(1)} %bitcast.12), custom_call_target="tpu_custom_call" | custom-call | flops 5000000000 | bytes 20000000 | tf_op jit(solution)/shard_map/scatter_edges/pallas_call | solution.py:276
  62.4 1.9 %collective-permute-start = (bf16[528,128]{1,0:T(8,128)(2,1)S(1)}, bf16[528,128]{1,0:T(8,128)(2,1)S(1)}, u32[]{:S(2)}, u32[]{:S(2)}) collective-permute-start(bf16[528,128]{1,0:T(8,128)(2,1)S(1)} %get-tuple-element.20), channel_id=1, source_target_pairs={{0,1},{1,2},{2,3},{4,5},{5,6},{6,7},{8,9},{9,10},{10,11},{12,13},{... | collective-permute-start | bytes 405512 | tf_op jit(solution)/shard_map/ppermute | solution.py:512
  64.4 3.9 %collective-permute-start.1 = (bf16[528,128]{1,0:T(8,128)(2,1)S(1)}, bf16[528,128]{1,0:T(8,128)(2,1)S(1)}, u32[]{:S(2)}, u32[]{:S(2)}) collective-permute-start(bf16[528,128]{1,0:T(8,128)(2,1)S(1)} %get-tuple-element.21), channel_id=1, source_target_pairs={{1,0},{2,1},{3,2},{5,4},{6,5},{7,6},{9,8},{10,9},{11,10},{13,12},{... | collective-permute-start | bytes 405512 | tf_op jit(solution)/shard_map/ppermute | solution.py:512
  68.3 9.7 %scatter_middle.2.mid1_ref = f32[1536,128]{1,0:T(8,128)S(1)} custom-call(bf16[8192,128]{1,0:T(8,128)(2,1)S(1)} %get-tuple-element.18.rows_ref, f32[64,16,128]{2,1,0:T(8,128)S(1)} %get-tuple-element.22.meta_ref), custom_call_target="tpu_custom_call" | custom-call | flops 7000000000 | bytes 20000000 | tf_op jit(solution)/shard_map/scatter_middle/pallas_call | solution.py:307
  78.0 0.0 collective-permute-done.below_ref
  78.0 0.0 collective-permute-done.1.above_ref
  78.0 0.1 turn.1
  78.1 0.1 collective-permute-start.2
  78.2 0.0 copy-start
  78.2 0.0 copy-start.2
  78.2 5.0 %collective-permute-start.3 = (bf16[240,128]{1,0:T(8,128)(2,1)S(1)}, bf16[240,128]{1,0:T(8,128)(2,1)S(1)}, u32[]{:S(2)}, u32[]{:S(2)}) collective-permute-start(bf16[240,128]{1,0:T(8,128)(2,1)S(1)} %get-tuple-element.27), channel_id=1, source_target_pairs={{4,0},{8,4},{12,8},{16,12},{20,16},{24,20},{28,24},{32,28},{36,32}... | collective-permute-start | bytes 184328 | tf_op jit(solution)/shard_map/ppermute | solution.py:512
  83.2 9.8 %scatter_middle.3.mid2_ref = f32[1536,128]{1,0:T(8,128)S(1)} custom-call(bf16[8192,128]{1,0:T(8,128)(2,1)S(1)} %get-tuple-element.18.rows_ref, f32[64,16,128]{2,1,0:T(8,128)S(1)} %get-tuple-element.22.meta_ref), custom_call_target="tpu_custom_call" | custom-call | flops 7000000000 | bytes 20000000 | tf_op jit(solution)/shard_map/scatter_middle/pallas_call | solution.py:307
  93.0 0.0 collective-permute-done.2.west_ref
  93.0 0.0 collective-permute-done.3.east_ref
  93.0 0.0 copy-done
  93.1 0.0 copy-done.2
  93.1 9.4 %diffuse.1 = f32[5120,128]{1,0:T(8,128)} custom-call(s32[1]{0:T(128)} %bitcast.place_ref, f32[1024,128]{1,0:T(8,128)S(1)} %get-tuple-element.17.outer_ref, f32[1536,128]{1,0:T(8,128)S(1)} %scatter_middle.2.mid1_ref, f32[1536,128]{1,0:T(8,128)S(1)} %scatter_middle.3.mid2_ref, bf16[528,128]{1,0:T(8,128)(2,1)S(1)} %collective-permute-done.below_ref, ...), custom_call_target="tpu_custom_call" | custom-call | flops 1000000000 | bytes 20000000 | tf_op jit(solution)/shard_map/diffuse/pallas_call | solution.py:496
Async XLA Ops:
  8.9 43.0 %copy-start.1 = (f32[2,32,128]{2,1,0:T(8,128)S(1)}, f32[2,32,128]{2,1,0:T(8,128)}, u32[]{:S(2)}) copy-start(f32[2,32,128]{2,1,0:T(8,128)} %param.13) | copy-start | bytes 98308
  8.9 43.0 %all-to-all-start = ((bf16[128,72,128]{2,1,0:T(8,128)(2,1)}), bf16[128,72,128]{2,1,0:T(8,128)(2,1)S(1)}, u32[]{:S(2)}, u32[]{:S(2)}) async-start(bf16[128,72,128]{2,1,0:T(8,128)(2,1)} %bitcast.15), calls=%async_computation | async-start | bytes 4718592 | tf_op jit(solution)/shard_map/all_to_all | solution.py:521
  62.4 15.6 %collective-permute-start = (bf16[528,128]{1,0:T(8,128)(2,1)S(1)}, bf16[528,128]{1,0:T(8,128)(2,1)S(1)}, u32[]{:S(2)}, u32[]{:S(2)}) collective-permute-start(bf16[528,128]{1,0:T(8,128)(2,1)S(1)} %get-tuple-element.20), channel_id=1, source_target_pairs={{0,1},{1,2},{2,3},{4,5},{5,6},{6,7},{8,9},{9,10},{10,11},{12,13},{... | collective-permute-start | bytes 405512 | tf_op jit(solution)/shard_map/ppermute | solution.py:512
  64.4 13.7 %collective-permute-start.1 = (bf16[528,128]{1,0:T(8,128)(2,1)S(1)}, bf16[528,128]{1,0:T(8,128)(2,1)S(1)}, u32[]{:S(2)}, u32[]{:S(2)}) collective-permute-start(bf16[528,128]{1,0:T(8,128)(2,1)S(1)} %get-tuple-element.21), channel_id=1, source_target_pairs={{1,0},{2,1},{3,2},{5,4},{6,5},{7,6},{9,8},{10,9},{11,10},{13,12},{... | collective-permute-start | bytes 405512 | tf_op jit(solution)/shard_map/ppermute | solution.py:512
  78.1 14.9 %collective-permute-start.2 = (bf16[240,128]{1,0:T(8,128)(2,1)S(1)}, bf16[240,128]{1,0:T(8,128)(2,1)S(1)}, u32[]{:S(2)}, u32[]{:S(2)}) collective-permute-start(bf16[240,128]{1,0:T(8,128)(2,1)S(1)} %get-tuple-element.26), channel_id=1, source_target_pairs={{124,0},{0,4},{4,8},{8,12},{12,16},{16,20},{20,24},{24,28},{28,32}... | collective-permute-start | bytes 184328 | tf_op jit(solution)/shard_map/ppermute | solution.py:512
  78.2 14.9 %copy-start = (bf16[128,160]{0,1:T(8,128)(2,1)S(1)}, bf16[128,160]{0,1:T(8,128)(2,1)}, u32[]{:S(2)}) copy-start(bf16[128,160]{0,1:T(8,128)(2,1)} %param.12) | copy-start | bytes 122884
  78.2 14.9 %copy-start.2 = (f32[128]{0:T(128)S(1)}, f32[128]{0:T(128)}, u32[]{:S(2)}) copy-start(f32[128]{0:T(128)} %param.11) | copy-start | bytes 1540
  78.2 14.8 %collective-permute-start.3 = (bf16[240,128]{1,0:T(8,128)(2,1)S(1)}, bf16[240,128]{1,0:T(8,128)(2,1)S(1)}, u32[]{:S(2)}, u32[]{:S(2)}) collective-permute-start(bf16[240,128]{1,0:T(8,128)(2,1)S(1)} %get-tuple-element.27), channel_id=1, source_target_pairs={{4,0},{8,4},{12,8},{16,12},{20,16},{24,20},{28,24},{32,28},{36,32}... | collective-permute-start | bytes 184328 | tf_op jit(solution)/shard_map/ppermute | solution.py:512

commit v5 on v4

--- a/solution.py
+++ b/solution.py
@@ -13,11 +13,12 @@
 PAD = 8
 GROUPS = 8
 TILES = 16
+MIDDLE_TILES = 32
 CHUNKS = 8
 UNROLL_RANK = 8
 UNROLL_SWEEP = 6
 SWEEP_PARTS = 2
-UNROLL_PROJECT = 16
+OUT_PARTS = 4
 F32 = jnp.float32
 BF16 = jnp.bfloat16
 MIB = 1024 * 1024
@@ -181,18 +182,20 @@
     return (p % GROUPS) * (lon_cols // GROUPS) + p // GROUPS
 
 
-def one_hots(metas, lat_rows, lon_cols):
-    both = jnp.concatenate(metas, axis=1)
+def column_hots(both, lon_cols):
     depth = both.shape[1]
     col_id = column_of(lon_cols, (lon_cols, depth)).astype(F32).astype(BF16)
-    row_id = iota((lat_rows, depth), 0).astype(F32)
-    col, row = [], []
+    col = []
     for k in range(4):
         apart = jnp.broadcast_to(both[4 + k : 5 + k], (16, depth)).astype(BF16)
         apart = jnp.concatenate([apart] * (lon_cols // 16), axis=0) - col_id
         col.append(jnp.maximum(1.0 - apart * apart, 0.0).astype(BF16))
-        row.append(jnp.where(both[k : k + 1] == row_id, both[8 + k : 9 + k], 0.0))
-    return both, col, row
+    return col
+
+
+def row_weights(both, first, count):
+    row_id = (iota((count, both.shape[1]), 0) + first).astype(F32)
+    return [jnp.where(both[k : k + 1] == row_id, both[8 + k : 9 + k], 0.0) for k in range(4)]
 
 
 def spread_rows(col, row, which, lon_cols):
@@ -207,7 +210,7 @@
 
 
 def edge_kernel(
-    cap, lat_rows, lon_cols, recv_ref, rates_ref, rows, meta, field_ref, south_ref, north_ref, strip_ref, acc, tmp
+    cap, lat_rows, lon_cols, recv_ref, rates_ref, rows, meta, hots_ref, field_ref, south_ref, north_ref, strip_ref, acc, tmp
 ):
     slots = rows.shape[0]
     left = iota((META, LANES), 1) < cap
@@ -236,7 +239,12 @@
 
     def accumulate(t, _):
         data = rows[pl.ds(pl.multiple_of(t * depth, depth), depth), :]
-        both, col, row = one_hots([meta[TILES * t + h] for h in range(TILES)], lat_rows, lon_cols)
+        both = jnp.concatenate([meta[TILES * t + h] for h in range(TILES)], axis=1)
+        col = column_hots(both, lon_cols)
+        row = row_weights(both, 0, lat_rows)
+        here = pl.ds(pl.multiple_of(t * depth, depth), depth)
+        for k in range(4):
+            hots_ref[k * lon_cols : (k + 1) * lon_cols, here] = col[k]
         rowb = [r.astype(BF16) for r in row]
         field_ref[...] += jnp.dot(spread_rows(col, row, outer, lon_cols), data, preferred_element_type=F32)
         parts = []
@@ -268,6 +276,7 @@
     shapes = [
         jax.ShapeDtypeStruct((slots, LANES), BF16),
         jax.ShapeDtypeStruct((slots // LANES, 16, LANES), F32),
+        jax.ShapeDtypeStruct((4 * lon_cols, slots), BF16),
         jax.ShapeDtypeStruct((2 * wide, LANES), F32),
         jax.ShapeDtypeStruct((wide + 16, LANES), BF16),
         jax.ShapeDtypeStruct((wide + 16, LANES), BF16),
@@ -279,22 +288,25 @@
         in_specs=[full] * 2,
         out_specs=[full] * len(shapes),
         scratch_shapes=[pltpu.VMEM((2 * STEPS * lat_rows, LANES), F32), pltpu.VMEM((16, LANES), F32)],
-        compiler_params=pltpu.CompilerParams(vmem_limit_bytes=14 * MIB),
+        compiler_params=pltpu.CompilerParams(vmem_limit_bytes=24 * MIB),
         cost_estimate=pl.CostEstimate(flops=5_000_000_000, bytes_accessed=20_000_000, transcendentals=0),
         name="scatter_edges",
     )(recv, rates)
 
 
-def middle_kernel(first, last, lat_rows, lon_cols, rows_ref, meta_ref, field_ref):
+def middle_kernel(first, last, lon_cols, rows_ref, meta_ref, hots_ref, field_ref):
     field_ref[...] = jnp.zeros_like(field_ref)
-    depth = TILES * LANES
+    depth = MIDDLE_TILES * LANES
     per = 4
 
     def accumulate(t, _):
         data = rows_ref[pl.ds(pl.multiple_of(t * depth, depth), depth), :]
-        _, col, row = one_hots([meta_ref[TILES * t + h] for h in range(TILES)], lat_rows, lon_cols)
+        both = jnp.concatenate([meta_ref[MIDDLE_TILES * t + h] for h in range(MIDDLE_TILES)], axis=1)
+        here = pl.ds(pl.multiple_of(t * depth, depth), depth)
+        col = [hots_ref[k * lon_cols : (k + 1) * lon_cols, here] for k in range(4)]
+        row = row_weights(both, first, 16)
         for i in range(first, last, per):
-            spread = spread_rows(col, row, range(i, i + per), lon_cols)
+            spread = spread_rows(col, row, range(i - first, i - first + per), lon_cols)
             at = pl.ds((i - first) * lon_cols, per * lon_cols)
             field_ref[at, :] += jnp.dot(spread, data, preferred_element_type=F32)
         return 0
@@ -302,17 +314,17 @@
     lax.fori_loop(0, rows_ref.shape[0] // depth, accumulate, 0)
 
 
-def scatter_middle(rows, meta, first, last, lat_rows, lon_cols):
+def scatter_middle(rows, meta, hots, first, last, lon_cols):
     full = pl.BlockSpec(memory_space=pltpu.VMEM)
     return pl.pallas_call(
-        functools.partial(middle_kernel, first, last, lat_rows, lon_cols),
+        functools.partial(middle_kernel, first, last, lon_cols),
         out_shape=jax.ShapeDtypeStruct(((last - first) * lon_cols, LANES), F32),
-        in_specs=[full] * 2,
+        in_specs=[full] * 3,
         out_specs=full,
-        compiler_params=pltpu.CompilerParams(vmem_limit_bytes=10 * MIB),
+        compiler_params=pltpu.CompilerParams(vmem_limit_bytes=20 * MIB),
         cost_estimate=pl.CostEstimate(flops=7_000_000_000, bytes_accessed=20_000_000, transcendentals=0),
         name="scatter_middle",
-    )(rows, meta)
+    )(rows, meta, hots)
 
 
 def turn_kernel(lat_rows, lon_cols, below_ref, above_ref, strip_ref, rates_ref, west_ref, east_ref, tall_ref, cols, wide_rows):
@@ -372,12 +384,14 @@
     rates_ref,
     gain_ref,
     jac_ref,
+    out_hbm,
     out_ref,
     ping,
     pong,
     face_x,
     face_y,
     kappa,
+    out_sems,
 ):
     width = lon_cols + 2 * PAD
     tall = lat_rows + 2 * STEPS
@@ -470,7 +484,10 @@
     jac = jnp.concatenate([jac_ref[...], jac_ref[...]], axis=1)
     levels = jac_ref.shape[0]
 
-    def project(h, _):
+    shape = out_hbm.shape
+    stores = []
+    band = lat_rows // OUT_PARTS
+    for h in range(lat_rows // 2):
         pair = []
         for u in range(2):
             at = (2 * h + u + STEPS) * span + inner
@@ -483,9 +500,15 @@
         result = lax.dot_general(jac, both, (((1,), (1,)), ((), ())), preferred_element_type=F32)
         out_ref[pl.ds(2 * h, levels, stride=lat_rows), :] = result[:, :lon_cols]
         out_ref[pl.ds(2 * h + 1, levels, stride=lat_rows), :] = result[:, lon_cols:]
-        return 0
-
-    lax.fori_loop(0, lat_rows // 2, project, 0, unroll=UNROLL_PROJECT)
+        if (2 * h + 2) % band == 0:
+            rows = pl.ds(2 * h + 2 - band, band)
+            n = len(stores)
+            stores.append(
+                pltpu.make_async_copy(out_ref.reshape(shape).at[:, rows, :], out_hbm.at[:, rows, :], out_sems.at[n])
+            )
+            stores[n].start()
+    for store in stores:
+        store.wait()
 
 
 def diffuse(place, outer, mid1, mid2, below, above, west, east, rates, inv_var, jacobian, lat_rows, lon_cols, lats):
@@ -493,17 +516,18 @@
     levels = jacobian.shape[1]
     tall, width = lat_rows + 2 * STEPS, lon_cols + 2 * PAD
     span = lon_cols + 2 * STEPS * GROUPS
-    out = pl.pallas_call(
+    return pl.pallas_call(
         functools.partial(diffuse_kernel, lat_rows, lon_cols, lats),
-        out_shape=jax.ShapeDtypeStruct((levels * lat_rows, lon_cols), F32),
+        out_shape=jax.ShapeDtypeStruct((levels, lat_rows, lon_cols), F32),
         in_specs=[pl.BlockSpec(memory_space=pltpu.SMEM)] + [full] * 10,
-        out_specs=full,
-        scratch_shapes=[pltpu.VMEM((tall * span, LANES), F32)] * 4 + [pltpu.VMEM((2, width, LANES), F32)],
+        out_specs=pl.BlockSpec(memory_space=pltpu.HBM),
+        scratch_shapes=[pltpu.VMEM((levels * lat_rows, lon_cols), F32)]
+        + [pltpu.VMEM((tall * span, LANES), F32)] * 4
+        + [pltpu.VMEM((2, width, LANES), F32), pltpu.SemaphoreType.DMA((OUT_PARTS,))],
         compiler_params=pltpu.CompilerParams(vmem_limit_bytes=28 * MIB),
         cost_estimate=pl.CostEstimate(flops=1_000_000_000, bytes_accessed=20_000_000, transcendentals=0),
         name="diffuse",
     )(place, outer, mid1, mid2, below, above, west, east, rates, inv_var.reshape(1, -1), jacobian.T)
-    return out.reshape(levels, lat_rows, lon_cols)
 
 
 def moved(value, axis, step, wrap):
@@ -521,16 +545,16 @@
     recv = lax.all_to_all(
         send.reshape(devices, cap + META, LANES), ("lon", "lat"), split_axis=0, concat_axis=0, tiled=True
     ).reshape(devices * (cap + META), LANES)
-    rows, meta, outer, south, north, strip = scatter_edges(recv, rates, devices, cap, lat_rows, lon_cols)
+    rows, meta, hots, outer, south, north, strip = scatter_edges(recv, rates, devices, cap, lat_rows, lon_cols)
     below = moved(north, "lat", -1, False)
     above = moved(south, "lat", 1, False)
     middle = lat_rows // 2
-    mid1 = scatter_middle(rows, meta, STEPS, middle, lat_rows, lon_cols)
+    mid1 = scatter_middle(rows, meta, hots, STEPS, middle, lon_cols)
     meta, below, above = lax.optimization_barrier((meta, below, above))
     to_west, to_east, tall_rates = turn(below, above, strip, rates, lat_rows, lon_cols)
     west = moved(to_east, "lon", -1, True)
     east = moved(to_west, "lon", 1, True)
-    mid2 = scatter_middle(rows, meta, middle, lat_rows - STEPS, lat_rows, lon_cols)
+    mid2 = scatter_middle(rows, meta, hots, middle, lat_rows - STEPS, lon_cols)
     place = lax.axis_index("lat").astype(jnp.int32).reshape(1)
     return diffuse(
         place,

time: 103 us -> 101 us (0.981)
  Pallas kernels: 48.4 us -> 46.5 us
    pallas_call x2, Pallas kernels: 19.5 us -> 17.5 us  [scatter_middle(): pl.pallas_call(functools.partial(middle_kernel, first, last, lon_cols), o...]
  transfers between devices with their start and end apart: 5 -> 5, of which waited for: 1 -> 1; matrix products, arithmetic and copies ran while one was open for 0% -> 0% of each run, Pallas kernels for 19% -> 17%
where the time goes in v5:
time: 101 us
  Pallas kernels  46.5 us (46%)
  waiting for transfers between devices  32.7 us (32%)
  starting transfers between devices  21.2 us (21%)
    all_to_all x1, waiting for transfers between devices, local(): lax.all_to_all(send.reshape(devices, cap + META, LANES), ('lon', 'lat'),...  32.7 us
    pallas_call x2, Pallas kernels, scatter_middle(): pl.pallas_call(functools.partial(middle_kernel, first, last, lon_cols), o...  17.5 us
    pallas_call x1, Pallas kernels, scatter_edges(): pl.pallas_call(functools.partial(edge_kernel, cap, lat_rows, lon_cols), o...  11.3 us
    ppermute x4, starting transfers between devices, moved(): return lax.ppermute(value, axis, pairs)  11 us
    all_to_all x1, starting transfers between devices, local(): lax.all_to_all(send.reshape(devices, cap + META, LANES), ('lon', 'lat'),...  10.2 us
    pallas_call x1, Pallas kernels, pack(): pl.pallas_call(functools.partial(pack_kernel, cap), out_shape=jax.ShapeDt...  8.85 us
    pallas_call x1, Pallas kernels, diffuse(): pl.pallas_call(functools.partial(diffuse_kernel, lat_rows, lon_cols, lats...  8.79 us
  transfers between devices with their start and end apart: 5, of which 1 were waited for; matrix products, arithmetic and copies ran while one was open for 0% of the time, Pallas kernels for 17%

profile of v5, /device:TPU:32, one launch (start us, length us, event | category | flops | bytes accessed | tf_op | source)
XLA Modules:
  0.0 100.8 jit_solution(13324019345640363037)
XLA Ops:
  0.0 8.8 %pack.1 = bf16[9216,128]{1,0:T(8,128)(2,1)} custom-call(s32[32,128]{1,0:T(8,128)} %bitcast.17, s32[4,4096]{1,0:T(4,128)} %bitcast.15, f32[4,4096]{1,0:T(4,128)} %bitcast.16, bf16[4096,128]{1,0:T(8,128)(2,1)} %rows_hbm.1), custom_call_target="tpu_custom_call" | custom-call | flops 4000000000 | bytes 40000000 | tf_op jit(solution)/shard_map/pack/pallas_call | solution.py:153
  8.9 0.0 copy-start.1
  8.9 10.2 %all-to-all-start = ((bf16[128,72,128]{2,1,0:T(8,128)(2,1)}), bf16[128,72,128]{2,1,0:T(8,128)(2,1)S(1)}, u32[]{:S(2)}, u32[]{:S(2)}) async-start(bf16[128,72,128]{2,1,0:T(8,128)(2,1)} %bitcast.14), calls=%async_computation | async-start | bytes 4718592 | tf_op jit(solution)/shard_map/all_to_all | solution.py:545
  19.1 32.7 %all-to-all-done = bf16[128,72,128]{2,1,0:T(8,128)(2,1)S(1)} async-done(((bf16[128,72,128]{2,1,0:T(8,128)(2,1)}), bf16[128,72,128]{2,1,0:T(8,128)(2,1)S(1)}, u32[]{:S(2)}, u32[]{:S(2)}) %all-to-all-start) | async-done | bytes 2359328 | tf_op jit(solution)/shard_map/all_to_all | solution.py:545
  51.8 0.0 copy-done.1
  51.8 11.3 %scatter_edges.1 = (bf16[8192,128]{1,0:T(8,128)(2,1)S(1)}, f32[64,16,128]{2,1,0:T(8,128)S(1)}, bf16[512,8192]{1,0:T(8,128)(2,1)S(1)}, f32[1024,128]{1,0:T(8,128)...) custom-call(bf16[9216,128]{1,0:T(8,128)(2,1)S(1)} %bitcast.9, ...), custom_call_target="tpu_custom_call" | custom-call | flops 5000000000 | bytes 20000000 | tf_op jit(solution)/shard_map/scatter_edges/pallas_call | solution.py:285
  63.1 1.9 %collective-permute-start = (bf16[528,128]{1,0:T(8,128)(2,1)S(1)}, bf16[528,128]{1,0:T(8,128)(2,1)S(1)}, u32[]{:S(2)}, u32[]{:S(2)}) collective-permute-start(bf16[528,128]{1,0:T(8,128)(2,1)S(1)} %get-tuple-element.22), channel_id=1, source_target_pairs={{0,1},{1,2},{2,3},{4,5},{5,6},{6,7},{8,9},{9,10},{10,11},{12,13},{... | collective-permute-start | bytes 405512 | tf_op jit(solution)/shard_map/ppermute | solution.py:536
  65.1 3.9 %collective-permute-start.1 = (bf16[528,128]{1,0:T(8,128)(2,1)S(1)}, bf16[528,128]{1,0:T(8,128)(2,1)S(1)}, u32[]{:S(2)}, u32[]{:S(2)}) collective-permute-start(bf16[528,128]{1,0:T(8,128)(2,1)S(1)} %get-tuple-element.23), channel_id=1, source_target_pairs={{1,0},{2,1},{3,2},{5,4},{6,5},{7,6},{9,8},{10,9},{11,10},{13,12},{... | collective-permute-start | bytes 405512 | tf_op jit(solution)/shard_map/ppermute | solution.py:536
  69.0 8.8 %scatter_middle.2.mid1_ref = f32[1536,128]{1,0:T(8,128)S(1)} custom-call(bf16[8192,128]{1,0:T(8,128)(2,1)S(1)} %get-tuple-element.19.rows_ref, f32[64,16,128]{2,1,0:T(8,128)S(1)} %get-tuple-element.24.meta_ref, bf16[512,8192]{1,0:T(8,128)(2,1)S(1)} %get-tuple-element.21.hots_ref), custom_call_target="tpu_custom_call" | custom-call | flops 7000000000 | bytes 20000000 | tf_op jit(solution)/shard_map/scatter_middle/pallas_call | solution.py:319
  77.8 0.0 collective-permute-done.below_ref
  77.8 0.0 collective-permute-done.1.above_ref
  77.8 0.1 turn.1
  77.9 0.1 collective-permute-start.2
  78.0 0.0 copy-start
  78.0 0.0 copy-start.2
  78.0 5.0 %collective-permute-start.3 = (bf16[240,128]{1,0:T(8,128)(2,1)S(1)}, bf16[240,128]{1,0:T(8,128)(2,1)S(1)}, u32[]{:S(2)}, u32[]{:S(2)}) collective-permute-start(bf16[240,128]{1,0:T(8,128)(2,1)S(1)} %get-tuple-element.29), channel_id=1, source_target_pairs={{4,0},{8,4},{12,8},{16,12},{20,16},{24,20},{28,24},{32,28},{36,32}... | collective-permute-start | bytes 184328 | tf_op jit(solution)/shard_map/ppermute | solution.py:536
  83.0 8.8 %scatter_middle.3.mid2_ref = f32[1536,128]{1,0:T(8,128)S(1)} custom-call(bf16[8192,128]{1,0:T(8,128)(2,1)S(1)} %get-tuple-element.19.rows_ref, f32[64,16,128]{2,1,0:T(8,128)S(1)} %get-tuple-element.24.meta_ref, bf16[512,8192]{1,0:T(8,128)(2,1)S(1)} %get-tuple-element.21.hots_ref), custom_call_target="tpu_custom_call" | custom-call | flops 7000000000 | bytes 20000000 | tf_op jit(solution)/shard_map/scatter_middle/pallas_call | solution.py:319
  91.8 0.0 collective-permute-done.2.west_ref
  91.8 0.0 collective-permute-done.3.east_ref
  91.8 0.0 copy-done
  91.8 0.0 copy-done.2
  91.8 8.8 %diffuse.1 = f32[160,32,128]{2,1,0:T(8,128)} custom-call(s32[1]{0:T(128)} %bitcast.place_ref, f32[1024,128]{1,0:T(8,128)S(1)} %get-tuple-element.18.outer_ref, f32[1536,128]{1,0:T(8,128)S(1)} %scatter_middle.2.mid1_ref, f32[1536,128]{1,0:T(8,128)S(1)} %scatter_middle.3.mid2_ref, bf16[528,128]{1,0:T(8,128)(2,1)S(1)} %collective-permute-done.below_ref, ...), custom_call_target="tpu_custom_call" | custom-call | flops 1000000000 | bytes 20000000 | tf_op jit(solution)/shard_map/diffuse/pallas_call | solution.py:519
Async XLA Ops:
  8.9 43.0 %copy-start.1 = (f32[2,32,128]{2,1,0:T(8,128)S(1)}, f32[2,32,128]{2,1,0:T(8,128)}, u32[]{:S(2)}) copy-start(f32[2,32,128]{2,1,0:T(8,128)} %param.13) | copy-start | bytes 98308
  8.9 43.0 %all-to-all-start = ((bf16[128,72,128]{2,1,0:T(8,128)(2,1)}), bf16[128,72,128]{2,1,0:T(8,128)(2,1)S(1)}, u32[]{:S(2)}, u32[]{:S(2)}) async-start(bf16[128,72,128]{2,1,0:T(8,128)(2,1)} %bitcast.14), calls=%async_computation | async-start | bytes 4718592 | tf_op jit(solution)/shard_map/all_to_all | solution.py:545
  63.1 14.7 %collective-permute-start = (bf16[528,128]{1,0:T(8,128)(2,1)S(1)}, bf16[528,128]{1,0:T(8,128)(2,1)S(1)}, u32[]{:S(2)}, u32[]{:S(2)}) collective-permute-start(bf16[528,128]{1,0:T(8,128)(2,1)S(1)} %get-tuple-element.22), channel_id=1, source_target_pairs={{0,1},{1,2},{2,3},{4,5},{5,6},{6,7},{8,9},{9,10},{10,11},{12,13},{... | collective-permute-start | bytes 405512 | tf_op jit(solution)/shard_map/ppermute | solution.py:536
  65.1 12.7 %collective-permute-start.1 = (bf16[528,128]{1,0:T(8,128)(2,1)S(1)}, bf16[528,128]{1,0:T(8,128)(2,1)S(1)}, u32[]{:S(2)}, u32[]{:S(2)}) collective-permute-start(bf16[528,128]{1,0:T(8,128)(2,1)S(1)} %get-tuple-element.23), channel_id=1, source_target_pairs={{1,0},{2,1},{3,2},{5,4},{6,5},{7,6},{9,8},{10,9},{11,10},{13,12},{... | collective-permute-start | bytes 405512 | tf_op jit(solution)/shard_map/ppermute | solution.py:536
  77.9 13.9 %collective-permute-start.2 = (bf16[240,128]{1,0:T(8,128)(2,1)S(1)}, bf16[240,128]{1,0:T(8,128)(2,1)S(1)}, u32[]{:S(2)}, u32[]{:S(2)}) collective-permute-start(bf16[240,128]{1,0:T(8,128)(2,1)S(1)} %get-tuple-element.28), channel_id=1, source_target_pairs={{124,0},{0,4},{4,8},{8,12},{12,16},{16,20},{20,24},{24,28},{28,32}... | collective-permute-start | bytes 184328 | tf_op jit(solution)/shard_map/ppermute | solution.py:536
  78.0 13.8 %copy-start = (bf16[128,160]{0,1:T(8,128)(2,1)S(1)}, bf16[128,160]{0,1:T(8,128)(2,1)}, u32[]{:S(2)}) copy-start(bf16[128,160]{0,1:T(8,128)(2,1)} %param.12) | copy-start | bytes 122884
  78.0 13.8 %copy-start.2 = (f32[128]{0:T(128)S(1)}, f32[128]{0:T(128)}, u32[]{:S(2)}) copy-start(f32[128]{0:T(128)} %param.11) | copy-start | bytes 1540
  78.0 13.8 %collective-permute-start.3 = (bf16[240,128]{1,0:T(8,128)(2,1)S(1)}, bf16[240,128]{1,0:T(8,128)(2,1)S(1)}, u32[]{:S(2)}, u32[]{:S(2)}) collective-permute-start(bf16[240,128]{1,0:T(8,128)(2,1)S(1)} %get-tuple-element.29), channel_id=1, source_target_pairs={{4,0},{8,4},{12,8},{16,12},{20,16},{24,20},{28,24},{32,28},{36,32}... | collective-permute-start | bytes 184328 | tf_op jit(solution)/shard_map/ppermute | solution.py:536

commit v6 on v5

--- a/solution.py
+++ b/solution.py
@@ -230,7 +230,7 @@
         )
         return 0
 
-    lax.fori_loop(0, slots // LANES, unpack, 0, unroll=4)
+    lax.fori_loop(0, slots // LANES, unpack, 0, unroll=16)
     field_ref[...] = jnp.zeros_like(field_ref)
     acc[...] = jnp.zeros_like(acc)
     depth = TILES * LANES
@@ -422,10 +422,21 @@
     row = place_ref[0] * lat_rows - STEPS + iota((span, LANES), 1)
     inside = (row >= 0) & (row < lat_rows * lat_devices - 1)
     ny = jnp.where(inside, 0.5 * (ky + pltpu.roll(ky, LANES - 1, 1)), 0.0)
-    for i in range(tall):
-        at = pl.ds(i * span, span)
-        face_x[at, :] = jnp.broadcast_to(ex[:, i : i + 1], (span, LANES))
-        face_y[at, :] = jnp.broadcast_to(ny[:, i : i + 1], (span, LANES))
+    left = jnp.where(iota((2 * span, LANES), 1) < tall, jnp.concatenate([ex, ny], axis=0), 0.0)
+    pieces = None
+    for n in range(3):
+        piece = left.astype(BF16).astype(F32)
+        left = left - piece
+        pieces = piece if n == 0 else pieces + pltpu.roll(piece, n * tall, 1)
+    pieces = pieces.astype(BF16)
+    lane = iota((LANES, LANES), 0) % tall
+    for i in range(0, tall, 2):
+        choice = jnp.concatenate([(lane == i).astype(F32), (lane == i + 1).astype(F32)], axis=1).astype(BF16)
+        spread = jnp.dot(pieces, choice, preferred_element_type=F32)
+        for u in range(2):
+            at = pl.ds((i + u) * span, span)
+            face_x[at, :] = spread[:span, u * LANES : (u + 1) * LANES]
+            face_y[at, :] = spread[span:, u * LANES : (u + 1) * LANES]
 
     strip_id = iota((GROUPS, LANES), 0)
     inner = STEPS * GROUPS

time: 101 us -> 99.7 us (0.987)
  Pallas kernels: 46.5 us -> 45.1 us
  transfers between devices with their start and end apart: 5 -> 5, of which waited for: 1 -> 1; matrix products, arithmetic and copies ran while one was open for 0% -> 0% of each run, Pallas kernels for 17% -> 18%
where the time goes in v6:
time: 99.7 us; the launch traced here: 99.4 us
  Pallas kernels  45.1 us (45%)
  waiting for transfers between devices  32.7 us (33%)
  starting transfers between devices  21.2 us (21%)
    all_to_all x1, waiting for transfers between devices, local(): lax.all_to_all(send.reshape(devices, cap + META, LANES), ('lon', 'lat'),...  32.7 us
    pallas_call x2, Pallas kernels, scatter_middle(): pl.pallas_call(functools.partial(middle_kernel, first, last, lon_cols), o...  17.5 us
    ppermute x4, starting transfers between devices, moved(): return lax.ppermute(value, axis, pairs)  11 us
    pallas_call x1, Pallas kernels, scatter_edges(): pl.pallas_call(functools.partial(edge_kernel, cap, lat_rows, lon_cols), o...  10.7 us
    all_to_all x1, starting transfers between devices, local(): lax.all_to_all(send.reshape(devices, cap + META, LANES), ('lon', 'lat'),...  10.2 us
    pallas_call x1, Pallas kernels, pack(): pl.pallas_call(functools.partial(pack_kernel, cap), out_shape=jax.ShapeDt...  8.85 us
    pallas_call x1, Pallas kernels, diffuse(): pl.pallas_call(functools.partial(diffuse_kernel, lat_rows, lon_cols, lats...  7.96 us
  transfers between devices with their start and end apart: 5, of which 1 were waited for; matrix products, arithmetic and copies ran while one was open for 0% of the time, Pallas kernels for 18%

profile of v6, /device:TPU:32, one launch (start us, length us, event | category | flops | bytes accessed | tf_op | source)
XLA Modules:
  0.0 99.4 jit_solution(15106791810277992583)
XLA Ops:
  0.0 8.8 %pack.1 = bf16[9216,128]{1,0:T(8,128)(2,1)} custom-call(s32[32,128]{1,0:T(8,128)} %bitcast.17, s32[4,4096]{1,0:T(4,128)} %bitcast.15, f32[4,4096]{1,0:T(4,128)} %bitcast.16, bf16[4096,128]{1,0:T(8,128)(2,1)} %rows_hbm.1), custom_call_target="tpu_custom_call" | custom-call | flops 4000000000 | bytes 40000000 | tf_op jit(solution)/shard_map/pack/pallas_call | solution.py:153
  8.9 0.0 copy-start.1
  8.9 10.2 %all-to-all-start = ((bf16[128,72,128]{2,1,0:T(8,128)(2,1)}), bf16[128,72,128]{2,1,0:T(8,128)(2,1)S(1)}, u32[]{:S(2)}, u32[]{:S(2)}) async-start(bf16[128,72,128]{2,1,0:T(8,128)(2,1)} %bitcast.14), calls=%async_computation | async-start | bytes 4718592 | tf_op jit(solution)/shard_map/all_to_all | solution.py:556
  19.1 32.7 %all-to-all-done = bf16[128,72,128]{2,1,0:T(8,128)(2,1)S(1)} async-done(((bf16[128,72,128]{2,1,0:T(8,128)(2,1)}), bf16[128,72,128]{2,1,0:T(8,128)(2,1)S(1)}, u32[]{:S(2)}, u32[]{:S(2)}) %all-to-all-start) | async-done | bytes 2359328 | tf_op jit(solution)/shard_map/all_to_all | solution.py:556
  51.8 0.0 copy-done.1
  51.8 10.7 %scatter_edges.1 = (bf16[8192,128]{1,0:T(8,128)(2,1)S(1)}, f32[64,16,128]{2,1,0:T(8,128)S(1)}, bf16[512,8192]{1,0:T(8,128)(2,1)S(1)}, f32[1024,128]{1,0:T(8,128)...) custom-call(bf16[9216,128]{1,0:T(8,128)(2,1)S(1)} %bitcast.9, ...), custom_call_target="tpu_custom_call" | custom-call | flops 5000000000 | bytes 20000000 | tf_op jit(solution)/shard_map/scatter_edges/pallas_call | solution.py:285
  62.6 1.9 %collective-permute-start = (bf16[528,128]{1,0:T(8,128)(2,1)S(1)}, bf16[528,128]{1,0:T(8,128)(2,1)S(1)}, u32[]{:S(2)}, u32[]{:S(2)}) collective-permute-start(bf16[528,128]{1,0:T(8,128)(2,1)S(1)} %get-tuple-element.22), channel_id=1, source_target_pairs={{0,1},{1,2},{2,3},{4,5},{5,6},{6,7},{8,9},{9,10},{10,11},{12,13},{... | collective-permute-start | bytes 405512 | tf_op jit(solution)/shard_map/ppermute | solution.py:547
  64.5 3.9 %collective-permute-start.1 = (bf16[528,128]{1,0:T(8,128)(2,1)S(1)}, bf16[528,128]{1,0:T(8,128)(2,1)S(1)}, u32[]{:S(2)}, u32[]{:S(2)}) collective-permute-start(bf16[528,128]{1,0:T(8,128)(2,1)S(1)} %get-tuple-element.23), channel_id=1, source_target_pairs={{1,0},{2,1},{3,2},{5,4},{6,5},{7,6},{9,8},{10,9},{11,10},{13,12},{... | collective-permute-start | bytes 405512 | tf_op jit(solution)/shard_map/ppermute | solution.py:547
  68.4 8.8 %scatter_middle.2.mid1_ref = f32[1536,128]{1,0:T(8,128)S(1)} custom-call(bf16[8192,128]{1,0:T(8,128)(2,1)S(1)} %get-tuple-element.19.rows_ref, f32[64,16,128]{2,1,0:T(8,128)S(1)} %get-tuple-element.24.meta_ref, bf16[512,8192]{1,0:T(8,128)(2,1)S(1)} %get-tuple-element.21.hots_ref), custom_call_target="tpu_custom_call" | custom-call | flops 7000000000 | bytes 20000000 | tf_op jit(solution)/shard_map/scatter_middle/pallas_call | solution.py:319
  77.2 0.0 collective-permute-done.below_ref
  77.2 0.0 collective-permute-done.1.above_ref
  77.2 0.1 turn.1
  77.3 0.1 collective-permute-start.2
  77.4 0.0 copy-start
  77.4 0.0 copy-start.2
  77.4 5.0 %collective-permute-start.3 = (bf16[240,128]{1,0:T(8,128)(2,1)S(1)}, bf16[240,128]{1,0:T(8,128)(2,1)S(1)}, u32[]{:S(2)}, u32[]{:S(2)}) collective-permute-start(bf16[240,128]{1,0:T(8,128)(2,1)S(1)} %get-tuple-element.29), channel_id=1, source_target_pairs={{4,0},{8,4},{12,8},{16,12},{20,16},{24,20},{28,24},{32,28},{36,32}... | collective-permute-start | bytes 184328 | tf_op jit(solution)/shard_map/ppermute | solution.py:547
  82.4 8.8 %scatter_middle.3.mid2_ref = f32[1536,128]{1,0:T(8,128)S(1)} custom-call(bf16[8192,128]{1,0:T(8,128)(2,1)S(1)} %get-tuple-element.19.rows_ref, f32[64,16,128]{2,1,0:T(8,128)S(1)} %get-tuple-element.24.meta_ref, bf16[512,8192]{1,0:T(8,128)(2,1)S(1)} %get-tuple-element.21.hots_ref), custom_call_target="tpu_custom_call" | custom-call | flops 7000000000 | bytes 20000000 | tf_op jit(solution)/shard_map/scatter_middle/pallas_call | solution.py:319
  91.2 0.0 collective-permute-done.2.west_ref
  91.2 0.0 collective-permute-done.3.east_ref
  91.2 0.0 copy-done
  91.2 0.0 copy-done.2
  91.2 8.0 %diffuse.1 = f32[160,32,128]{2,1,0:T(8,128)} custom-call(s32[1]{0:T(128)} %bitcast.place_ref, f32[1024,128]{1,0:T(8,128)S(1)} %get-tuple-element.18.outer_ref, f32[1536,128]{1,0:T(8,128)S(1)} %scatter_middle.2.mid1_ref, f32[1536,128]{1,0:T(8,128)S(1)} %scatter_middle.3.mid2_ref, bf16[528,128]{1,0:T(8,128)(2,1)S(1)} %collective-permute-done.below_ref, ...), custom_call_target="tpu_custom_call" | custom-call | flops 1000000000 | bytes 20000000 | tf_op jit(solution)/shard_map/diffuse/pallas_call | solution.py:530
Async XLA Ops:
  8.9 43.0 %copy-start.1 = (f32[2,32,128]{2,1,0:T(8,128)S(1)}, f32[2,32,128]{2,1,0:T(8,128)}, u32[]{:S(2)}) copy-start(f32[2,32,128]{2,1,0:T(8,128)} %param.13) | copy-start | bytes 98308
  8.9 43.0 %all-to-all-start = ((bf16[128,72,128]{2,1,0:T(8,128)(2,1)}), bf16[128,72,128]{2,1,0:T(8,128)(2,1)S(1)}, u32[]{:S(2)}, u32[]{:S(2)}) async-start(bf16[128,72,128]{2,1,0:T(8,128)(2,1)} %bitcast.14), calls=%async_computation | async-start | bytes 4718592 | tf_op jit(solution)/shard_map/all_to_all | solution.py:556
  62.6 14.7 %collective-permute-start = (bf16[528,128]{1,0:T(8,128)(2,1)S(1)}, bf16[528,128]{1,0:T(8,128)(2,1)S(1)}, u32[]{:S(2)}, u32[]{:S(2)}) collective-permute-start(bf16[528,128]{1,0:T(8,128)(2,1)S(1)} %get-tuple-element.22), channel_id=1, source_target_pairs={{0,1},{1,2},{2,3},{4,5},{5,6},{6,7},{8,9},{9,10},{10,11},{12,13},{... | collective-permute-start | bytes 405512 | tf_op jit(solution)/shard_map/ppermute | solution.py:547
  64.5 12.7 %collective-permute-start.1 = (bf16[528,128]{1,0:T(8,128)(2,1)S(1)}, bf16[528,128]{1,0:T(8,128)(2,1)S(1)}, u32[]{:S(2)}, u32[]{:S(2)}) collective-permute-start(bf16[528,128]{1,0:T(8,128)(2,1)S(1)} %get-tuple-element.23), channel_id=1, source_target_pairs={{1,0},{2,1},{3,2},{5,4},{6,5},{7,6},{9,8},{10,9},{11,10},{13,12},{... | collective-permute-start | bytes 405512 | tf_op jit(solution)/shard_map/ppermute | solution.py:547
  77.3 13.9 %collective-permute-start.2 = (bf16[240,128]{1,0:T(8,128)(2,1)S(1)}, bf16[240,128]{1,0:T(8,128)(2,1)S(1)}, u32[]{:S(2)}, u32[]{:S(2)}) collective-permute-start(bf16[240,128]{1,0:T(8,128)(2,1)S(1)} %get-tuple-element.28), channel_id=1, source_target_pairs={{124,0},{0,4},{4,8},{8,12},{12,16},{16,20},{20,24},{24,28},{28,32}... | collective-permute-start | bytes 184328 | tf_op jit(solution)/shard_map/ppermute | solution.py:547
  77.4 13.8 %copy-start = (bf16[128,160]{0,1:T(8,128)(2,1)S(1)}, bf16[128,160]{0,1:T(8,128)(2,1)}, u32[]{:S(2)}) copy-start(bf16[128,160]{0,1:T(8,128)(2,1)} %param.12) | copy-start | bytes 122884
  77.4 13.8 %copy-start.2 = (f32[128]{0:T(128)S(1)}, f32[128]{0:T(128)}, u32[]{:S(2)}) copy-start(f32[128]{0:T(128)} %param.11) | copy-start | bytes 1540
  77.4 13.8 %collective-permute-start.3 = (bf16[240,128]{1,0:T(8,128)(2,1)S(1)}, bf16[240,128]{1,0:T(8,128)(2,1)S(1)}, u32[]{:S(2)}, u32[]{:S(2)}) collective-permute-start(bf16[240,128]{1,0:T(8,128)(2,1)S(1)} %get-tuple-element.29), channel_id=1, source_target_pairs={{4,0},{8,4},{12,8},{16,12},{20,16},{24,20},{28,24},{32,28},{36,32}... | collective-permute-start | bytes 184328 | tf_op jit(solution)/shard_map/ppermute | solution.py:547

commit v7 on v6

--- a/solution.py
+++ b/solution.py
@@ -16,9 +16,9 @@
 MIDDLE_TILES = 32
 CHUNKS = 8
 UNROLL_RANK = 8
-UNROLL_SWEEP = 6
+UNROLL_SWEEP = 12
 SWEEP_PARTS = 2
-OUT_PARTS = 4
+OUT_PARTS = 8
 F32 = jnp.float32
 BF16 = jnp.bfloat16
 MIB = 1024 * 1024
@@ -102,10 +102,15 @@
 
     def move(g, _):
         first = pl.multiple_of(g * LANES, LANES)
-        for u in range(LANES):
-            s = slots_s[g, u]
-            yd[pl.ds(s, 1), :] = xd[pl.ds(first + u, 1), :]
-            ym[pl.ds(s, 1), :] = xm[pl.ds(first + u, 1), :]
+        for start in range(0, LANES, 4):
+            batch = range(start, start + 4)
+            where = [slots_s[g, u] for u in batch]
+            data = [xd[pl.ds(first + u, 1), :] for u in batch]
+            meta = [xm[pl.ds(first + u, 1), :] for u in batch]
+            for s, value in zip(where, data):
+                yd[pl.ds(s, 1), :] = value
+            for s, value in zip(where, meta):
+                ym[pl.ds(s, 1), :] = value
         return 0
 
     half = groups // 2

time: 99.7 us -> 99.6 us (level)
  no operation moved by 1% of the time
where the time goes in v7:
time: 99.6 us; the launch traced here: 99.3 us
  Pallas kernels  45.1 us (45%)
  waiting for transfers between devices  32.7 us (33%)
  starting transfers between devices  21.2 us (21%)
    all_to_all x1, waiting for transfers between devices, local(): lax.all_to_all(send.reshape(devices, cap + META, LANES), ('lon', 'lat'),...  32.7 us
    pallas_call x2, Pallas kernels, scatter_middle(): pl.pallas_call(functools.partial(middle_kernel, first, last, lon_cols), o...  17.5 us
    ppermute x4, starting transfers between devices, moved(): return lax.ppermute(value, axis, pairs)  11 us
    pallas_call x1, Pallas kernels, scatter_edges(): pl.pallas_call(functools.partial(edge_kernel, cap, lat_rows, lon_cols), o...  10.8 us
    all_to_all x1, starting transfers between devices, local(): lax.all_to_all(send.reshape(devices, cap + META, LANES), ('lon', 'lat'),...  10.2 us
    pallas_call x1, Pallas kernels, pack(): pl.pallas_call(functools.partial(pack_kernel, cap), out_shape=jax.ShapeDt...  8.85 us
    pallas_call x1, Pallas kernels, diffuse(): pl.pallas_call(functools.partial(diffuse_kernel, lat_rows, lon_cols, lats...  7.89 us
  transfers between devices with their start and end apart: 5, of which 1 were waited for; matrix products, arithmetic and copies ran while one was open for 0% of the time, Pallas kernels for 18%

profile of v7, /device:TPU:32, one launch (start us, length us, event | category | flops | bytes accessed | tf_op | source)
XLA Modules:
  0.0 99.3 jit_solution(3903764569913455172)
XLA Ops:
  0.0 8.9 %pack.1 = bf16[9216,128]{1,0:T(8,128)(2,1)} custom-call(s32[32,128]{1,0:T(8,128)} %bitcast.17, s32[4,4096]{1,0:T(4,128)} %bitcast.15, f32[4,4096]{1,0:T(4,128)} %bitcast.16, bf16[4096,128]{1,0:T(8,128)(2,1)} %rows_hbm.1), custom_call_target="tpu_custom_call" | custom-call | flops 4000000000 | bytes 40000000 | tf_op jit(solution)/shard_map/pack/pallas_call | solution.py:158
  8.9 0.0 copy-start.1
  8.9 10.2 %all-to-all-start = ((bf16[128,72,128]{2,1,0:T(8,128)(2,1)}), bf16[128,72,128]{2,1,0:T(8,128)(2,1)S(1)}, u32[]{:S(2)}, u32[]{:S(2)}) async-start(bf16[128,72,128]{2,1,0:T(8,128)(2,1)} %bitcast.14), calls=%async_computation | async-start | bytes 4718592 | tf_op jit(solution)/shard_map/all_to_all | solution.py:561
  19.1 32.7 %all-to-all-done = bf16[128,72,128]{2,1,0:T(8,128)(2,1)S(1)} async-done(((bf16[128,72,128]{2,1,0:T(8,128)(2,1)}), bf16[128,72,128]{2,1,0:T(8,128)(2,1)S(1)}, u32[]{:S(2)}, u32[]{:S(2)}) %all-to-all-start) | async-done | bytes 2359328 | tf_op jit(solution)/shard_map/all_to_all | solution.py:561
  51.8 0.0 copy-done.1
  51.8 10.8 %scatter_edges.1 = (bf16[8192,128]{1,0:T(8,128)(2,1)S(1)}, f32[64,16,128]{2,1,0:T(8,128)S(1)}, bf16[512,8192]{1,0:T(8,128)(2,1)S(1)}, f32[1024,128]{1,0:T(8,128)...) custom-call(bf16[9216,128]{1,0:T(8,128)(2,1)S(1)} %bitcast.9, ...), custom_call_target="tpu_custom_call" | custom-call | flops 5000000000 | bytes 20000000 | tf_op jit(solution)/shard_map/scatter_edges/pallas_call | solution.py:290
  62.6 1.9 %collective-permute-start = (bf16[528,128]{1,0:T(8,128)(2,1)S(1)}, bf16[528,128]{1,0:T(8,128)(2,1)S(1)}, u32[]{:S(2)}, u32[]{:S(2)}) collective-permute-start(bf16[528,128]{1,0:T(8,128)(2,1)S(1)} %get-tuple-element.22), channel_id=1, source_target_pairs={{0,1},{1,2},{2,3},{4,5},{5,6},{6,7},{8,9},{9,10},{10,11},{12,13},{... | collective-permute-start | bytes 405512 | tf_op jit(solution)/shard_map/ppermute | solution.py:552
  64.5 3.9 %collective-permute-start.1 = (bf16[528,128]{1,0:T(8,128)(2,1)S(1)}, bf16[528,128]{1,0:T(8,128)(2,1)S(1)}, u32[]{:S(2)}, u32[]{:S(2)}) collective-permute-start(bf16[528,128]{1,0:T(8,128)(2,1)S(1)} %get-tuple-element.23), channel_id=1, source_target_pairs={{1,0},{2,1},{3,2},{5,4},{6,5},{7,6},{9,8},{10,9},{11,10},{13,12},{... | collective-permute-start | bytes 405512 | tf_op jit(solution)/shard_map/ppermute | solution.py:552
  68.5 8.8 %scatter_middle.2.mid1_ref = f32[1536,128]{1,0:T(8,128)S(1)} custom-call(bf16[8192,128]{1,0:T(8,128)(2,1)S(1)} %get-tuple-element.19.rows_ref, f32[64,16,128]{2,1,0:T(8,128)S(1)} %get-tuple-element.24.meta_ref, bf16[512,8192]{1,0:T(8,128)(2,1)S(1)} %get-tuple-element.21.hots_ref), custom_call_target="tpu_custom_call" | custom-call | flops 7000000000 | bytes 20000000 | tf_op jit(solution)/shard_map/scatter_middle/pallas_call | solution.py:324
  77.2 0.0 collective-permute-done.below_ref
  77.3 0.0 collective-permute-done.1.above_ref
  77.3 0.1 turn.1
  77.3 0.1 collective-permute-start.2
  77.4 0.0 copy-start
  77.4 0.0 copy-start.2
  77.4 5.0 %collective-permute-start.3 = (bf16[240,128]{1,0:T(8,128)(2,1)S(1)}, bf16[240,128]{1,0:T(8,128)(2,1)S(1)}, u32[]{:S(2)}, u32[]{:S(2)}) collective-permute-start(bf16[240,128]{1,0:T(8,128)(2,1)S(1)} %get-tuple-element.29), channel_id=1, source_target_pairs={{4,0},{8,4},{12,8},{16,12},{20,16},{24,20},{28,24},{32,28},{36,32}... | collective-permute-start | bytes 184328 | tf_op jit(solution)/shard_map/ppermute | solution.py:552
  82.5 8.8 %scatter_middle.3.mid2_ref = f32[1536,128]{1,0:T(8,128)S(1)} custom-call(bf16[8192,128]{1,0:T(8,128)(2,1)S(1)} %get-tuple-element.19.rows_ref, f32[64,16,128]{2,1,0:T(8,128)S(1)} %get-tuple-element.24.meta_ref, bf16[512,8192]{1,0:T(8,128)(2,1)S(1)} %get-tuple-element.21.hots_ref), custom_call_target="tpu_custom_call" | custom-call | flops 7000000000 | bytes 20000000 | tf_op jit(solution)/shard_map/scatter_middle/pallas_call | solution.py:324
  91.2 0.0 collective-permute-done.2.west_ref
  91.2 0.0 collective-permute-done.3.east_ref
  91.2 0.0 copy-done
  91.3 0.0 copy-done.2
  91.3 7.9 %diffuse.1 = f32[160,32,128]{2,1,0:T(8,128)} custom-call(s32[1]{0:T(128)} %bitcast.place_ref, f32[1024,128]{1,0:T(8,128)S(1)} %get-tuple-element.18.outer_ref, f32[1536,128]{1,0:T(8,128)S(1)} %scatter_middle.2.mid1_ref, f32[1536,128]{1,0:T(8,128)S(1)} %scatter_middle.3.mid2_ref, bf16[528,128]{1,0:T(8,128)(2,1)S(1)} %collective-permute-done.below_ref, ...), custom_call_target="tpu_custom_call" | custom-call | flops 1000000000 | bytes 20000000 | tf_op jit(solution)/shard_map/diffuse/pallas_call | solution.py:535
Async XLA Ops:
  8.9 43.0 %copy-start.1 = (f32[2,32,128]{2,1,0:T(8,128)S(1)}, f32[2,32,128]{2,1,0:T(8,128)}, u32[]{:S(2)}) copy-start(f32[2,32,128]{2,1,0:T(8,128)} %param.13) | copy-start | bytes 98308
  8.9 43.0 %all-to-all-start = ((bf16[128,72,128]{2,1,0:T(8,128)(2,1)}), bf16[128,72,128]{2,1,0:T(8,128)(2,1)S(1)}, u32[]{:S(2)}, u32[]{:S(2)}) async-start(bf16[128,72,128]{2,1,0:T(8,128)(2,1)} %bitcast.14), calls=%async_computation | async-start | bytes 4718592 | tf_op jit(solution)/shard_map/all_to_all | solution.py:561
  62.6 14.6 %collective-permute-start = (bf16[528,128]{1,0:T(8,128)(2,1)S(1)}, bf16[528,128]{1,0:T(8,128)(2,1)S(1)}, u32[]{:S(2)}, u32[]{:S(2)}) collective-permute-start(bf16[528,128]{1,0:T(8,128)(2,1)S(1)} %get-tuple-element.22), channel_id=1, source_target_pairs={{0,1},{1,2},{2,3},{4,5},{5,6},{6,7},{8,9},{9,10},{10,11},{12,13},{... | collective-permute-start | bytes 405512 | tf_op jit(solution)/shard_map/ppermute | solution.py:552
  64.5 12.7 %collective-permute-start.1 = (bf16[528,128]{1,0:T(8,128)(2,1)S(1)}, bf16[528,128]{1,0:T(8,128)(2,1)S(1)}, u32[]{:S(2)}, u32[]{:S(2)}) collective-permute-start(bf16[528,128]{1,0:T(8,128)(2,1)S(1)} %get-tuple-element.23), channel_id=1, source_target_pairs={{1,0},{2,1},{3,2},{5,4},{6,5},{7,6},{9,8},{10,9},{11,10},{13,12},{... | collective-permute-start | bytes 405512 | tf_op jit(solution)/shard_map/ppermute | solution.py:552
  77.3 13.9 %collective-permute-start.2 = (bf16[240,128]{1,0:T(8,128)(2,1)S(1)}, bf16[240,128]{1,0:T(8,128)(2,1)S(1)}, u32[]{:S(2)}, u32[]{:S(2)}) collective-permute-start(bf16[240,128]{1,0:T(8,128)(2,1)S(1)} %get-tuple-element.28), channel_id=1, source_target_pairs={{124,0},{0,4},{4,8},{8,12},{12,16},{16,20},{20,24},{24,28},{28,32}... | collective-permute-start | bytes 184328 | tf_op jit(solution)/shard_map/ppermute | solution.py:552
  77.4 13.8 %copy-start = (bf16[128,160]{0,1:T(8,128)(2,1)S(1)}, bf16[128,160]{0,1:T(8,128)(2,1)}, u32[]{:S(2)}) copy-start(bf16[128,160]{0,1:T(8,128)(2,1)} %param.12) | copy-start | bytes 122884
  77.4 13.8 %copy-start.2 = (f32[128]{0:T(128)S(1)}, f32[128]{0:T(128)}, u32[]{:S(2)}) copy-start(f32[128]{0:T(128)} %param.11) | copy-start | bytes 1540
  77.4 13.8 %collective-permute-start.3 = (bf16[240,128]{1,0:T(8,128)(2,1)S(1)}, bf16[240,128]{1,0:T(8,128)(2,1)S(1)}, u32[]{:S(2)}, u32[]{:S(2)}) collective-permute-start(bf16[240,128]{1,0:T(8,128)(2,1)S(1)} %get-tuple-element.29), channel_id=1, source_target_pairs={{4,0},{8,4},{12,8},{16,12},{20,16},{24,20},{28,24},{32,28},{36,32}... | collective-permute-start | bytes 184328 | tf_op jit(solution)/shard_map/ppermute | solution.py:552
